TPU v7x, 32 devices: a whole 2x2x4 slice. The times are simulated.
32 devices in a mesh: parts: 2 (over x), node: 2 (over core), dev: 8 (over z, y).
Axes of the slice: x: 2, y: 2, z: 4, core: 2. Of those that a mesh axis runs over, the one named last changes fastest.
Arguments:
- tokens: bfloat16 [512, 7168], P(('parts', 'node', 'dev')), parts along dimension 0, may hold values from -6 to 6
- routes: int32 [512, 2], P(('parts', 'node', 'dev')), parts along dimension 0, may hold values from 0 to 3, all different within a row; in each aligned block of 16 rows (0 to 15, 16 to 31, ...) at most 16 rows name the same one
- route_weight: float32 [512, 2], P(('parts', 'node', 'dev')), parts along dimension 0, may hold values from 0.1 to 1
- w_gate: bfloat16 [16, 7168, 256], P(('node', 'dev')), may hold values from -0.0625 to 0.0625
- w_up: bfloat16 [16, 7168, 256], P(('node', 'dev')), may hold values from -0.0625 to 0.0625
- w_down: bfloat16 [16, 256, 7168], P(('node', 'dev')), may hold values from -0.1875 to 0.1875
- queries: bfloat16 [32, 128, 576], P(('parts', 'node', 'dev')), parts along dimension 0, may hold values from -2000 to 2000
- latent_cache: bfloat16 [32, 1024, 576], P(('parts', 'node', 'dev')), parts along dimension 0, may hold values from -8 to 8
- lengths: int32 [32], P(('parts', 'node', 'dev')), parts along dimension 0, may hold values from 128 to 1024, as said below
Outputs:
- moe_out: bfloat16 [512, 7168], P(('parts', 'node', 'dev')), parts along dimension 0
- context: bfloat16 [32, 128, 512], P(('parts', 'node', 'dev')), parts along dimension 0
There are 2 independent parts, one for each index of `parts`. A program takes and returns all parts, laid end to end along the dimension named above; an argument that names none is the same for every part. Nothing has to cross between parts.
Inputs may be any that keep to these rules, and one draw needn't show every extreme that they name: `routes`: each token names 2 different experts; the tokens of one device name no expert more than 16 times, a bound that some block reaches. `lengths`: some row of every part has length 1024.
All inputs are finite; a program needn't handle non-finite values.
Results may differ from a plain program's by a relative error of at most 0.0058.
Values may be sent and summed in bfloat16 or wider, within the bound.
No kernel may reach another device: no remote copies, remote signals or barrier semaphores. Data moves between devices by JAX's collectives and lax.ppermute only.
A program may use at most 128 MiB of HBM per device.

v0:
```python
import jax
import jax.numpy as jnp
from jax import lax
from jax.sharding import PartitionSpec as P

LAT = 512
HEAD_QK = 192
SLICES = 4


def slot_tables(routes, route_weight, experts_all, capacity):
    choices_hit = routes[:, :, None] == jnp.arange(experts_all, dtype=jnp.int32)[None, None, :]
    member = jnp.sum(choices_hit.astype(jnp.int32), axis=1)
    combine = jnp.sum(
        jnp.where(choices_hit, route_weight[:, :, None], jnp.zeros((), route_weight.dtype)), axis=1
    )
    slot_index = jnp.cumsum(member, axis=0) - member
    slot_ids = jnp.arange(capacity, dtype=jnp.int32)
    picked = (slot_index.T[:, None, :] == slot_ids[None, :, None]) & (member.T[:, None, :] == 1)
    return (picked.astype(jnp.float32), combine)


def attend(queries, latent_cache, lengths):
    score_scale = HEAD_QK ** (-0.5)
    scores = (
        jnp.einsum("rhk,rlk->rhl", queries, latent_cache, preferred_element_type=jnp.float32)
        * score_scale
    )
    positions = jnp.arange(latent_cache.shape[1], dtype=jnp.int32)
    visible = positions[None, None, :] < lengths[:, None, None]
    scores = jnp.where(visible, scores, -1e30)
    row_max = jnp.max(scores, axis=-1, keepdims=True)
    expo = jnp.exp(scores - row_max)
    row_sum = jnp.sum(expo, axis=-1, keepdims=True)
    weights_bf = (expo / row_sum).astype(jnp.bfloat16)
    context = jnp.einsum(
        "rhl,rlk->rhk", weights_bf, latent_cache[:, :, :LAT], preferred_element_type=jnp.float32
    )
    return context.astype(jnp.bfloat16)


def body(tokens, routes, route_weight, w_gate, w_up, w_down, queries, latent_cache, lengths):
    owners = lax.axis_size("node") * lax.axis_size("dev")
    experts_all = owners // SLICES
    rows_here, top_routes = routes.shape
    capacity = min(rows_here, 2 * rows_here * top_routes // experts_all)
    width = tokens.shape[1]
    selector, combine = slot_tables(routes, route_weight, experts_all, capacity)
    outgoing = jnp.einsum(
        "ect,td->ecd", selector.astype(jnp.bfloat16), tokens, preferred_element_type=jnp.float32
    ).astype(jnp.bfloat16)
    gate_rows = w_gate[0]
    up_rows = w_up[0]
    down_rows = w_down[0]
    replicas = jnp.repeat(outgoing, SLICES, axis=0)
    received = lax.all_to_all(replicas, ("node", "dev"), split_axis=0, concat_axis=0, tiled=True)
    flat_rows = received.reshape(-1, received.shape[-1])
    gate_val = jnp.dot(flat_rows, gate_rows, preferred_element_type=jnp.float32)
    up_val = jnp.dot(flat_rows, up_rows, preferred_element_type=jnp.float32)
    act = (jax.nn.silu(gate_val) * up_val).astype(jnp.bfloat16)
    partial_value = jnp.dot(act, down_rows, preferred_element_type=jnp.float32).astype(jnp.bfloat16)
    returned_rows = lax.all_to_all(
        partial_value.reshape(received.shape),
        ("node", "dev"),
        split_axis=0,
        concat_axis=0,
        tiled=True,
    )
    expert_out = jnp.sum(
        returned_rows.reshape(experts_all, SLICES, capacity, width).astype(jnp.float32), axis=1
    )
    weighted = selector * combine.T[:, None, :]
    moe_out = jnp.einsum(
        "ect,ecd->td", weighted, expert_out, precision=lax.Precision.HIGHEST
    ).astype(jnp.bfloat16)
    context = attend(queries, latent_cache, lengths)
    return (moe_out, context)


def solution(mesh):
    return jax.shard_map(
        body,
        mesh=mesh,
        in_specs=(
            P(("parts", "node", "dev"), None),
            P(("parts", "node", "dev"), None),
            P(("parts", "node", "dev"), None),
            P(("node", "dev"), None, None),
            P(("node", "dev"), None, None),
            P(("node", "dev"), None, None),
            P(("parts", "node", "dev"), None, None),
            P(("parts", "node", "dev"), None, None),
            P(("parts", "node", "dev")),
        ),
        out_specs=(P(("parts", "node", "dev"), None), P(("parts", "node", "dev"), None, None)),
        check_vma=False,
    )
```

profile of v0, /device:TPU:0, one launch (start us, length us, event | category | flops | bytes accessed | tf_op | source)
XLA Modules:
  0.0 195.6 jit_solution(16703655253786136977)
XLA Ops:
  0.6 0.0 copy-start
  0.6 0.7 convert_reduce_fusion.1
  1.4 0.1 copy.16
  1.5 0.1 copy.18
  1.6 0.0 copy-done
  1.6 0.5 convolution_convert_fusion.1
  2.1 0.4 broadcast_in_dim.40
  2.5 0.0 copy-start.6
  2.5 90.7 %all_to_all.10 = bf16[16,16,7168]{2,1,0:T(8,128)(2,1)S(1)} all-to-all(bf16[16,16,7168]{2,1,0:T(8,128)(2,1)S(1)} %bitcast.56), channel_id=1, replica_groups=mesh['parts'=2,'node'=2,'dev'=8] {'node','dev'}, dimensions={0} | all-to-all | bytes 7340032 | tf_op jit(solution)/shard_map/all_to_all | solution.py:56
  93.2 1.8 copy-done.1
  95.1 0.0 copy-done.6
  95.1 1.1 fusion.4
  96.2 10.0 %convolution_convert_fusion = bf16[256,7168]{1,0:T(8,128)(2,1)} fusion(bf16[1,256,7168]{2,1,0:T(8,128)(2,1)} %param.14, bf16[256,7168]{1,0:T(8,128)(2,1)} %bitcast.55, bf16[1,7168,256]{2,1,0:T(8,128)(2,1)} %param.13, f32[256,256]{1,0:T(8,128)S(1)} %fusion.4), kind=kOutput, calls=%fused_computation | convolution fusion | flops 1881276416 | bytes 14942208 | tf_op jit(solution)/shard_map/dot_general | solution.py:61
  106.2 4.7 %all-to-all-start.1 = ((bf16[16,16,7168]{2,1,0:T(8,128)(2,1)}), bf16[16,16,7168]{2,1,0:T(8,128)(2,1)}, u32[]{:S(2)}, u32[]{:S(2)}) async-start(bf16[16,16,7168]{2,1,0:T(8,128)(2,1)} %bitcast.53), calls=%async_computation.1 | async-start | bytes 7340032 | tf_op jit(solution)/shard_map/all_to_all | solution.py:62
  111.5 0.0 copy-done.4
  111.5 0.0 copy-done.5
  111.5 0.0 copy-done.2
  111.6 0.0 copy-done.3
  111.6 0.5 fusion.41
  112.1 0.2 fusion.19
  112.3 1.2 fusion.16
  113.5 76.6 %all-to-all-done.1 = bf16[16,16,7168]{2,1,0:T(8,128)(2,1)} async-done(((bf16[16,16,7168]{2,1,0:T(8,128)(2,1)}), bf16[16,16,7168]{2,1,0:T(8,128)(2,1)}, u32[]{:S(2)}, u32[]{:S(2)}) %all-to-all-start.1) | async-done | bytes 3670048 | tf_op jit(solution)/shard_map/all_to_all | solution.py:62
  190.0 2.8 %convert_reduce_fusion = f32[4,16,7168]{2,1,0:T(8,128)S(1)} fusion(bf16[16,16,7168]{2,1,0:T(8,128)(2,1)} %all-to-all-done.1), kind=kLoop, calls=%fused_computation.4 | loop fusion | flops 3211264 | bytes 5505024 | tf_op jit(solution)/shard_map/reduce_sum | solution.py:69
  192.9 2.8 %fusion = bf16[16,7168]{1,0:T(8,128)(2,1)} fusion(f32[4,16,7168]{2,1,0:T(8,128)S(1)} %convert_reduce_fusion, f32[4,16]{1,0:T(4,128)S(1)} %bitcast.57, s32[4,16]{1,0:T(4,128)S(1)} %copy.18, pred[4,16]{1,0:T(4,128)(4,1)S(1)} %compare_bitcast_fusion), kind=kOutput, calls=%fused_computation.3 | convolution fusion | flops 88198144 | bytes 2064960 | tf_op jit(solution)/shard_map/ect,ecd->td/dot_general | solution.py:73
  (10 shorter events, 0.1 us)
Async XLA Ops:
  0.6 1.0 copy-start
  2.5 92.5 %copy-start.6 = (bf16[1,7168,256]{2,1,0:T(8,128)(2,1)S(1)}, bf16[1,7168,256]{2,1,0:T(8,128)(2,1)}, u32[]{:S(2)}) copy-start(bf16[1,7168,256]{2,1,0:T(8,128)(2,1)} %param.12) | copy-start | bytes 11010052
  93.2 1.8 copy-start.1
  106.2 5.3 %copy-start.4 = (s32[16,2]{0,1:T(2,128)S(1)}, s32[16,2]{0,1:T(2,128)}, u32[]{:S(2)}) copy-start(s32[16,2]{0,1:T(2,128)} %param.10) | copy-start | bytes 388
  106.2 5.3 %copy-start.5 = (f32[16,2]{0,1:T(2,128)S(1)}, f32[16,2]{0,1:T(2,128)}, u32[]{:S(2)}) copy-start(f32[16,2]{0,1:T(2,128)} %param.11) | copy-start | bytes 388
  106.2 5.4 %copy-start.2 = (bf16[1,1024,576]{1,2,0:T(8,128)(2,1)S(1)}, bf16[1,1024,576]{1,2,0:T(8,128)(2,1)}, u32[]{:S(2)}) copy-start(bf16[1,1024,576]{1,2,0:T(8,128)(2,1)} %param.16) | copy-start | bytes 3538948
  106.2 5.4 %copy-start.3 = (bf16[1,128,576]{1,2,0:T(8,128)(2,1)S(1)}, bf16[1,128,576]{1,2,0:T(8,128)(2,1)}, u32[]{:S(2)}) copy-start(bf16[1,128,576]{1,2,0:T(8,128)(2,1)} %param.15) | copy-start | bytes 442372
  106.2 83.8 %all-to-all-start.1 = ((bf16[16,16,7168]{2,1,0:T(8,128)(2,1)}), bf16[16,16,7168]{2,1,0:T(8,128)(2,1)}, u32[]{:S(2)}, u32[]{:S(2)}) async-start(bf16[16,16,7168]{2,1,0:T(8,128)(2,1)} %bitcast.53), calls=%async_computation.1 | async-start | bytes 7340032 | tf_op jit(solution)/shard_map/all_to_all | solution.py:62
where the time goes:
time: 198 us; the launch traced here: 196 us
  blocking collectives  90.7 us (46%)
  waiting for transfers between devices  76.6 us (39%)
  matrix products  16 us (8%)
  starting transfers between devices  4.65 us (2%)
  other arithmetic  3.86 us (2%)
  local copies, waits for them, and re-layouts  2.46 us (1%)
    all_to_all x1, blocking collectives, body(): lax.all_to_all(replicas, ('node', 'dev'), split_axis=0, concat_axis=0, ti...  90.7 us
    all_to_all x1, waiting for transfers between devices, body(): lax.all_to_all(partial_value.reshape(received.shape), ('node', 'dev'), sp...  76.6 us
    dot_general x1, matrix products, body(): jnp.dot(act, down_rows, preferred_element_type=jnp.float32)  10 us
    all_to_all x1, starting transfers between devices, body(): lax.all_to_all(partial_value.reshape(received.shape), ('node', 'dev'), sp...  4.65 us
  transfers between devices with their start and end apart: 1, of which 1 were waited for; matrix products, arithmetic and copies ran while one was open for 1% of the time, Pallas kernels for 0%

commit v1 on v0

v1 whole, which is shorter than its diff:
```python
import functools

import jax
import jax.numpy as jnp
from jax import lax
from jax.experimental import pallas as pl
from jax.experimental.pallas import tpu as pltpu
from jax.sharding import PartitionSpec as P

LAT = 512
HEAD_QK = 192
SLICES = 4
LANES = 128
PAIR = 2


def chunk_of(size, most):
    best = LANES
    for c in range(LANES, most + 1, LANES):
        if size % c == 0:
            best = c
    return best


def pack_kernel(experts_all, routes_ref, weight_ref, tokens_ref, out_ref):
    rows, width = tokens_ref.shape
    out_ref[:, :width] = tokens_ref[...]
    extra = out_ref.shape[1] - width
    column = lax.broadcasted_iota(jnp.int32, (rows, extra), 1)
    part = column // experts_all
    expert = (column - part * experts_all).astype(jnp.float32)
    square = (rows, rows)
    same = lax.broadcasted_iota(jnp.int32, square, 0) == lax.broadcasted_iota(jnp.int32, square, 1)

    def upright(row):
        return jnp.sum(jnp.where(same, row, 0.0), axis=1, keepdims=True)

    value = jnp.zeros((rows, extra), jnp.float32)
    for choice in range(routes_ref.shape[0]):
        named = upright(routes_ref[choice : choice + 1, :].astype(jnp.float32))
        value = value + jnp.where(named == expert, upright(weight_ref[choice : choice + 1, :]), 0.0)
    high = value.astype(jnp.bfloat16)
    rest = value - high.astype(jnp.float32)
    middle = rest.astype(jnp.bfloat16)
    low = (rest - middle.astype(jnp.float32)).astype(jnp.bfloat16)
    picked = jnp.where(
        part == 0,
        high.astype(jnp.float32),
        jnp.where(
            part == 1,
            middle.astype(jnp.float32),
            jnp.where(part == 2, low.astype(jnp.float32), 0.0),
        ),
    )
    out_ref[:, width:] = picked.astype(jnp.bfloat16)


def pack(tokens, routes, route_weight, experts_all):
    rows, width = tokens.shape
    extra = -(-3 * experts_all // LANES) * LANES
    return pl.pallas_call(
        functools.partial(pack_kernel, experts_all),
        out_shape=pltpu.VMEM((rows, width + extra), tokens.dtype),
        in_specs=[pl.BlockSpec(memory_space=pltpu.VMEM)] * 3,
        out_specs=pl.BlockSpec(memory_space=pltpu.VMEM),
        name="pack",
    )(routes.T, route_weight.T, tokens)


def expert_kernel(count, steps, *refs):
    blocks, masks = refs[:count], refs[count]
    weights = refs[count + 1 : count + 7]
    outs = refs[count + 7 : 2 * count + 7]
    rows, width = outs[0].shape
    depth = width // steps

    def columns(part):
        return jnp.concatenate([b[:, part] for b in blocks], axis=0)

    table = columns(pl.ds(width, blocks[0].shape[1] - width)).astype(jnp.float32)
    acts, scales = [], []
    for p in range(2):
        gate = up = None
        for k in range(steps):
            part = pl.ds(k * depth, depth)
            x = columns(part)
            g = jnp.dot(x, weights[3 * p][0, part, :], preferred_element_type=jnp.float32)
            u = jnp.dot(x, weights[3 * p + 1][0, part, :], preferred_element_type=jnp.float32)
            gate, up = (g, u) if gate is None else (gate + g, up + u)
        acts.append((jax.nn.silu(gate) * up).astype(jnp.bfloat16))
        scales.append(jnp.sum(table * masks[p : p + 1, :], axis=1, keepdims=True))
    for n in range(steps):
        part = pl.ds(n * depth, depth)
        total = None
        for p in range(2):
            value = scales[p] * jnp.dot(
                acts[p], weights[3 * p + 2][0, :, part], preferred_element_type=jnp.float32
            )
            total = value if total is None else total + value
        total = total.astype(jnp.bfloat16)
        for i, o in enumerate(outs):
            o[:, part] = total[i * rows : (i + 1) * rows]


def run_experts(blocks, masks, weights):
    count = len(blocks)
    rows, packed = blocks[0].shape
    width, hidden = weights[0].shape[1:]
    steps = width // chunk_of(width, 1024)
    return pl.pallas_call(
        functools.partial(expert_kernel, count, steps),
        out_shape=[pltpu.VMEM((rows, width), jnp.bfloat16)] * count,
        in_specs=[pl.BlockSpec(memory_space=pltpu.VMEM)] * (count + 7),
        out_specs=[pl.BlockSpec(memory_space=pltpu.VMEM)] * count,
        compiler_params=pltpu.CompilerParams(vmem_limit_bytes=2 * count * rows * packed + (16 << 20)),
        cost_estimate=pl.CostEstimate(
            flops=2 * count * rows * width * hidden * 6,
            bytes_accessed=2 * 6 * width * hidden,
            transcendentals=0,
        ),
        name="experts",
    )(
        *(pltpu.with_memory_space_constraint(b, pltpu.VMEM) for b in blocks),
        masks,
        *(pltpu.with_memory_space_constraint(w, pltpu.VMEM) for w in weights),
    )


def attend(queries, latent_cache, lengths):
    score_scale = HEAD_QK ** (-0.5)
    scores = (
        jnp.einsum("rhk,rlk->rhl", queries, latent_cache, preferred_element_type=jnp.float32)
        * score_scale
    )
    positions = jnp.arange(latent_cache.shape[1], dtype=jnp.int32)
    visible = positions[None, None, :] < lengths[:, None, None]
    scores = jnp.where(visible, scores, -1e30)
    row_max = jnp.max(scores, axis=-1, keepdims=True)
    expo = jnp.exp(scores - row_max)
    row_sum = jnp.sum(expo, axis=-1, keepdims=True)
    weights_bf = (expo / row_sum).astype(jnp.bfloat16)
    context = jnp.einsum(
        "rhl,rlk->rhk", weights_bf, latent_cache[:, :, :LAT], preferred_element_type=jnp.float32
    )
    return context.astype(jnp.bfloat16)


def add_all(*terms):
    total = terms[0].astype(jnp.float32)
    for t in terms[1:]:
        total = total + t.astype(jnp.float32)
    return total.astype(jnp.bfloat16)


def body(tokens, routes, route_weight, w_gate, w_up, w_down, queries, latent_cache, lengths):
    nodes, devs = lax.axis_size("node"), lax.axis_size("dev")
    experts_all = nodes * devs // SLICES
    lines = devs // PAIR

    def hop(value, offset):
        return lax.ppermute(value, "dev", [(d, d ^ offset) for d in range(devs)])

    def swap(value):
        return lax.ppermute(value, "node", [(i, i ^ 1) for i in range(nodes)])

    own = (w_gate, w_up, w_down)
    weights = own + tuple(swap(w) for w in own)
    dev, node = lax.axis_index("dev"), lax.axis_index("node")
    here = (node * devs + dev) // SLICES
    there = ((node ^ 1) * devs + dev) // SLICES

    packed = pack(tokens, routes, route_weight, experts_all)
    extra = packed.shape[1] - tokens.shape[1]
    column = jnp.arange(extra, dtype=jnp.int32)
    named = jnp.where(column < 3 * experts_all, column % experts_all, -1)
    masks = (named[None, :] == jnp.stack([here, there])[:, None]).astype(jnp.float32)

    gathered = {0: packed}
    bit = lines // 2
    while bit:
        for m in list(gathered):
            gathered[m ^ bit] = hop(gathered[m], bit * PAIR)
        bit //= 2
    keys = [(m, s) for m in range(lines) for s in range(PAIR)]
    blocks = [gathered[m] if s == 0 else hop(gathered[m], 1) for m, s in keys]

    partial = dict(zip(keys, run_experts(blocks, masks, weights), strict=True))
    context = attend(queries, latent_cache, lengths)

    terms = {m: [partial[m, 0]] for m in range(lines)}
    for m in reversed(range(lines)):
        terms[m].append(hop(partial[m, 1], 1))
    bit = 1
    while bit < lines:
        for m in sorted(terms, reverse=True):
            if m & bit:
                terms[m ^ bit].append(hop(add_all(*terms.pop(m)), bit * PAIR))
        bit *= 2
    return add_all(*terms[0]), context


def solution(mesh):
    return jax.shard_map(
        body,
        mesh=mesh,
        in_specs=(
            P(("parts", "node", "dev"), None),
            P(("parts", "node", "dev"), None),
            P(("parts", "node", "dev"), None),
            P(("node", "dev"), None, None),
            P(("node", "dev"), None, None),
            P(("node", "dev"), None, None),
            P(("parts", "node", "dev"), None, None),
            P(("parts", "node", "dev"), None, None),
            P(("parts", "node", "dev")),
        ),
        out_specs=(P(("parts", "node", "dev"), None), P(("parts", "node", "dev"), None, None)),
        check_vma=False,
    )
```

time: 198 us -> 84.1 us (0.42); the launches traced: 196 us -> 83.8 us
  blocking collectives: 90.7 us -> 0 us
  waiting for transfers between devices: 76.6 us -> 45 us
  starting transfers between devices: 4.65 us -> 19.5 us
  matrix products: 16 us -> 1.65 us
  Pallas kernels: 0 us -> 8.78 us
  local copies, waits for them, and re-layouts: 2.46 us -> 6.12 us
  other arithmetic: 3.86 us -> 1.4 us
    all_to_all x1 -> x0, blocking collectives: 90.7 us -> none  [body(): lax.all_to_all(replicas, ('node', 'dev'), split_axis=0, concat_axis=0, ti...]
    all_to_all x1 -> x0, waiting for transfers between devices: 76.6 us -> none  [body(): lax.all_to_all(partial_value.reshape(received.shape), ('node', 'dev'), sp...]
    ppermute x0 -> x17, waiting for transfers between devices: none -> 45 us  [the longest x14 45 us: hop(): return lax.ppermute(value, 'dev', [(d, d ^ offset) for d in range(devs)])]
    ppermute x0 -> x17, starting transfers between devices: none -> 19.5 us  [the longest x14 18.5 us: hop(): return lax.ppermute(value, 'dev', [(d, d ^ offset) for d in range(devs)])]
    dot_general x4 -> x0, matrix products: 14.4 us -> none  [the longest x1 10 us: body(): jnp.dot(act, down_rows, preferred_element_type=jnp.float32)]
    pallas_call x0 -> x2, Pallas kernels: none -> 8.78 us  [the longest x1 7.7 us: run_experts(): pl.pallas_call(functools.partial(expert_kernel, count, steps), out_shape=...]
    all_to_all x1 -> x0, starting transfers between devices: 4.65 us -> none  [body(): lax.all_to_all(partial_value.reshape(received.shape), ('node', 'dev'), sp...]
    unnamed x14 -> x10, local copies, waits for them, and re-layouts: 1.86 us -> 6.12 us
  transfers between devices with their start and end apart: 1 -> 17, of which waited for: 1 -> 11; matrix products, arithmetic and copies ran while one was open for 1% -> 3% of each run, Pallas kernels for 0% -> 1%
where the time goes in v1:
time: 84.1 us; the launch traced here: 83.8 us
  waiting for transfers between devices  45 us (54%)
  starting transfers between devices  19.5 us (23%)
  Pallas kernels  8.78 us (10%)
  local copies, waits for them, and re-layouts  6.12 us (7%)
  matrix products  1.65 us (2%)
  other arithmetic  1.4 us (2%)
  between operations  1.38 us (2%)
    ppermute x14, waiting for transfers between devices, hop(): return lax.ppermute(value, 'dev', [(d, d ^ offset) for d in range(devs)])  45 us
    ppermute x14, starting transfers between devices, hop(): return lax.ppermute(value, 'dev', [(d, d ^ offset) for d in range(devs)])  18.5 us
    pallas_call x1, Pallas kernels, run_experts(): pl.pallas_call(functools.partial(expert_kernel, count, steps), out_shape=...  7.7 us
    unnamed x10, local copies, waits for them, and re-layouts  6.12 us
  transfers between devices with their start and end apart: 17, of which 11 were waited for; matrix products, arithmetic and copies ran while one was open for 3% of the time, Pallas kernels for 1%

profile of v1, /device:TPU:0, one launch (start us, length us, event | category | flops | bytes accessed | tf_op | source)
XLA Modules:
  0.0 83.8 jit_solution(13224295324494394425)
XLA Ops:
  1.7 1.1 %pack.1.refs_0_ = bf16[16,7296]{1,0:T(8,128)(2,1)S(1)} custom-call(s32[2,16]{1,0:T(2,128)} %bitcast.21, f32[2,16]{1,0:T(2,128)} %bitcast.22, bf16[16,7168]{1,0:T(8,128)(2,1)} %tokens_ref.1), custom_call_target="tpu_custom_call" | custom-call | tf_op jit(solution)/shard_map/pack/pallas_call | solution.py:61
  2.8 3.7 %collective-permute-start.3 = (bf16[16,7296]{1,0:T(8,128)(2,1)S(1)}, bf16[16,7296]{1,0:T(8,128)(2,1)S(1)}, u32[]{:S(2)}, u32[]{:S(2)}) collective-permute-start(bf16[16,7296]{1,0:T(8,128)(2,1)S(1)} %pack.1.refs_0_), channel_id=1, source_target_pairs={{0,4},{1,5},{2,6},{3,7},{4,0},{5,1},{6,2},{7,3},{8,12},{9,13},{10,... | collective-permute-start | bytes 700424 | tf_op jit(solution)/shard_map/ppermute | solution.py:161
  6.5 1.6 %collective-permute-start.1 = (bf16[16,7296]{1,0:T(8,128)(2,1)S(1)}, bf16[16,7296]{1,0:T(8,128)(2,1)S(1)}, u32[]{:S(2)}, u32[]{:S(2)}) collective-permute-start(bf16[16,7296]{1,0:T(8,128)(2,1)S(1)} %pack.1.refs_0_), channel_id=1, source_target_pairs={{0,2},{1,3},{2,0},{3,1},{4,6},{5,7},{6,4},{7,5},{8,10},{9,11},{10,... | collective-permute-start | bytes 700424 | tf_op jit(solution)/shard_map/ppermute | solution.py:161
  8.1 9.8 %collective-permute-done.3.refs_4_ = bf16[16,7296]{1,0:T(8,128)(2,1)S(1)} collective-permute-done((bf16[16,7296]{1,0:T(8,128)(2,1)S(1)}, bf16[16,7296]{1,0:T(8,128)(2,1)S(1)}, u32[]{:S(2)}, u32[]{:S(2)}) %collective-permute-start.3) | collective-permute-done | bytes 233504 | tf_op jit(solution)/shard_map/ppermute | solution.py:161
  17.9 1.6 %collective-permute-start = (bf16[16,7296]{1,0:T(8,128)(2,1)S(1)}, bf16[16,7296]{1,0:T(8,128)(2,1)S(1)}, u32[]{:S(2)}, u32[]{:S(2)}) collective-permute-start(bf16[16,7296]{1,0:T(8,128)(2,1)S(1)} %pack.1.refs_0_), channel_id=1, source_target_pairs={{0,1},{1,0},{2,3},{3,2},{4,5},{5,4},{6,7},{7,6},{8,9},{9,8},{10,11... | collective-permute-start | bytes 700424 | tf_op jit(solution)/shard_map/ppermute | solution.py:161
  20.0 5.2 %collective-permute-done.refs_1_ = bf16[16,7296]{1,0:T(8,128)(2,1)S(1)} collective-permute-done((bf16[16,7296]{1,0:T(8,128)(2,1)S(1)}, bf16[16,7296]{1,0:T(8,128)(2,1)S(1)}, u32[]{:S(2)}, u32[]{:S(2)}) %collective-permute-start) | collective-permute-done | bytes 233504 | tf_op jit(solution)/shard_map/ppermute | solution.py:161
  25.3 1.4 %collective-permute-start.4 = (bf16[16,7296]{1,0:T(8,128)(2,1)S(1)}, bf16[16,7296]{1,0:T(8,128)(2,1)S(1)}, u32[]{:S(2)}, u32[]{:S(2)}) collective-permute-start(bf16[16,7296]{1,0:T(8,128)(2,1)S(1)} %collective-permute-done.3.refs_4_), channel_id=1, source_target_pairs={{0,1},{1,0},{2,3},{3,2},{4,5},{5,4},{6,7},{7,6},{8,9},{9,8},{10,11... | collective-permute-start | bytes 700424 | tf_op jit(solution)/shard_map/ppermute | solution.py:161
  28.1 5.8 %collective-permute-done.4.refs_5_ = bf16[16,7296]{1,0:T(8,128)(2,1)S(1)} collective-permute-done((bf16[16,7296]{1,0:T(8,128)(2,1)S(1)}, bf16[16,7296]{1,0:T(8,128)(2,1)S(1)}, u32[]{:S(2)}, u32[]{:S(2)}) %collective-permute-start.4) | collective-permute-done | bytes 233504 | tf_op jit(solution)/shard_map/ppermute | solution.py:161
  33.9 1.4 %collective-permute-start.6 = (bf16[16,7296]{1,0:T(8,128)(2,1)S(1)}, bf16[16,7296]{1,0:T(8,128)(2,1)S(1)}, u32[]{:S(2)}, u32[]{:S(2)}) collective-permute-start(bf16[16,7296]{1,0:T(8,128)(2,1)S(1)} %collective-permute-done.5.refs_6_), channel_id=1, source_target_pairs={{0,1},{1,0},{2,3},{3,2},{4,5},{5,4},{6,7},{7,6},{8,9},{9,8},{10,11... | collective-permute-start | bytes 700424 | tf_op jit(solution)/shard_map/ppermute | solution.py:161
  35.4 3.5 %collective-permute-done.2.refs_3_ = bf16[16,7296]{1,0:T(8,128)(2,1)S(1)} collective-permute-done((bf16[16,7296]{1,0:T(8,128)(2,1)S(1)}, bf16[16,7296]{1,0:T(8,128)(2,1)S(1)}, u32[]{:S(2)}, u32[]{:S(2)}) %collective-permute-start.2) | collective-permute-done | bytes 233504 | tf_op jit(solution)/shard_map/ppermute | solution.py:161
  38.9 2.9 %collective-permute-done.6.refs_7_ = bf16[16,7296]{1,0:T(8,128)(2,1)S(1)} collective-permute-done((bf16[16,7296]{1,0:T(8,128)(2,1)S(1)}, bf16[16,7296]{1,0:T(8,128)(2,1)S(1)}, u32[]{:S(2)}, u32[]{:S(2)}) %collective-permute-start.6) | collective-permute-done | bytes 233504 | tf_op jit(solution)/shard_map/ppermute | solution.py:161
  41.8 2.0 %copy-done.1 = bf16[1,7168,256]{2,1,0:T(8,128)(2,1)S(1)} copy-done((bf16[1,7168,256]{2,1,0:T(8,128)(2,1)S(1)}, bf16[1,7168,256]{2,1,0:T(8,128)(2,1)}, u32[]{:S(2)}) %copy-start.1) | copy-done | bytes 3670040
  43.8 2.0 %copy-done.2 = bf16[1,7168,256]{2,1,0:T(8,128)(2,1)S(1)} copy-done((bf16[1,7168,256]{2,1,0:T(8,128)(2,1)S(1)}, bf16[1,7168,256]{2,1,0:T(8,128)(2,1)}, u32[]{:S(2)}) %copy-start.2) | copy-done | bytes 3670040
  45.9 2.0 %copy-done.3 = bf16[1,256,7168]{2,1,0:T(8,128)(2,1)S(1)} copy-done((bf16[1,256,7168]{2,1,0:T(8,128)(2,1)S(1)}, bf16[1,256,7168]{2,1,0:T(8,128)(2,1)}, u32[]{:S(2)}) %copy-start.3) | copy-done | bytes 3670040
  47.9 7.7 %experts.1 = (bf16[16,7168]{1,0:T(8,128)(2,1)S(1)}, bf16[16,7168]{1,0:T(8,128)(2,1)S(1)}, bf16[16,7168]{1,0:T(8,128)(2,1)S(1)}, bf16[16,7168]{1,0:T(8,128)(2,1)S...) custom-call(bf16[16,7296]{1,0:T(8,128)(2,1)S(1)} %pack.1.refs_0_, ...), custom_call_target="tpu_custom_call" | custom-call | flops 2818572288 | bytes 22020096 | tf_op jit(solution)/shard_map/experts/pallas_call | solution.py:110
  55.6 1.2 %collective-permute-start.14 = (bf16[16,7168]{1,0:T(8,128)(2,1)S(1)}, bf16[16,7168]{1,0:T(8,128)(2,1)S(1)}, u32[]{:S(2)}, u32[]{:S(2)}) collective-permute-start(bf16[16,7168]{1,0:T(8,128)(2,1)S(1)} %get-tuple-element.17), channel_id=1, source_target_pairs={{0,1},{1,0},{2,3},{3,2},{4,5},{5,4},{6,7},{7,6},{8,9},{9,8},{10,11... | collective-permute-start | bytes 688136 | tf_op jit(solution)/shard_map/ppermute | solution.py:161
  58.5 1.1 %collective-permute-start.13 = (bf16[16,7168]{1,0:T(8,128)(2,1)S(1)}, bf16[16,7168]{1,0:T(8,128)(2,1)S(1)}, u32[]{:S(2)}, u32[]{:S(2)}) collective-permute-start(bf16[16,7168]{1,0:T(8,128)(2,1)S(1)} %get-tuple-element.15), channel_id=1, source_target_pairs={{0,1},{1,0},{2,3},{3,2},{4,5},{5,4},{6,7},{7,6},{8,9},{9,8},{10,11... | collective-permute-start | bytes 688136 | tf_op jit(solution)/shard_map/ppermute | solution.py:161
  60.5 3.7 %collective-permute-done.14 = bf16[16,7168]{1,0:T(8,128)(2,1)S(1)} collective-permute-done((bf16[16,7168]{1,0:T(8,128)(2,1)S(1)}, bf16[16,7168]{1,0:T(8,128)(2,1)S(1)}, u32[]{:S(2)}, u32[]{:S(2)}) %collective-permute-start.14) | collective-permute-done | bytes 229408 | tf_op jit(solution)/shard_map/ppermute | solution.py:161
  64.3 1.3 %collective-permute-start.15 = (bf16[16,7168]{1,0:T(8,128)(2,1)S(1)}, bf16[16,7168]{1,0:T(8,128)(2,1)S(1)}, u32[]{:S(2)}, u32[]{:S(2)}) collective-permute-start(bf16[16,7168]{1,0:T(8,128)(2,1)S(1)} %add_convert_fusion.2), channel_id=1, source_target_pairs={{0,2},{1,3},{2,0},{3,1},{4,6},{5,7},{6,4},{7,5},{8,10},{9,11},{10,... | collective-permute-start | bytes 688136 | tf_op jit(solution)/shard_map/ppermute | solution.py:161
  65.6 3.6 %collective-permute-done.11 = bf16[16,7168]{1,0:T(8,128)(2,1)S(1)} collective-permute-done((bf16[16,7168]{1,0:T(8,128)(2,1)S(1)}, bf16[16,7168]{1,0:T(8,128)(2,1)S(1)}, u32[]{:S(2)}, u32[]{:S(2)}) %collective-permute-start.11) | collective-permute-done | bytes 229408 | tf_op jit(solution)/shard_map/ppermute | solution.py:161
  69.2 1.3 %collective-permute-start.12 = (bf16[16,7168]{1,0:T(8,128)(2,1)S(1)}, bf16[16,7168]{1,0:T(8,128)(2,1)S(1)}, u32[]{:S(2)}, u32[]{:S(2)}) collective-permute-start(bf16[16,7168]{1,0:T(8,128)(2,1)S(1)} %add_convert_fusion.3), channel_id=1, source_target_pairs={{0,2},{1,3},{2,0},{3,1},{4,6},{5,7},{6,4},{7,5},{8,10},{9,11},{10,... | collective-permute-start | bytes 688136 | tf_op jit(solution)/shard_map/ppermute | solution.py:161
  70.5 3.0 %collective-permute-done.13 = bf16[16,7168]{1,0:T(8,128)(2,1)S(1)} collective-permute-done((bf16[16,7168]{1,0:T(8,128)(2,1)S(1)}, bf16[16,7168]{1,0:T(8,128)(2,1)S(1)}, u32[]{:S(2)}, u32[]{:S(2)}) %collective-permute-start.13) | collective-permute-done | bytes 229408 | tf_op jit(solution)/shard_map/ppermute | solution.py:161
  74.5 1.2 %fusion.2 = bf16[1,128,512]{2,1,0:T(8,128)(2,1)} fusion(bf16[1,1024,576]{1,2,0:T(8,128)(2,1)S(1)} %copy-done.4, f32[128,1024]{1,0:T(8,128)S(1)} %get-tuple-element.19, f32[128]{0:T(128)S(1)} %fusion.5, f32[128]{0:T(128)S(1)} %get-tuple-element.18), kind=kOutput, calls=%fused_computation.4 | convolution fusion | flops 134676480 | bytes 1704960 | tf_op jit(solution)/shard_map/rhl,rlk->rhk/dot_general | solution.py:142
  76.7 6.4 %collective-permute-done.16 = bf16[16,7168]{1,0:T(8,128)(2,1)S(1)} collective-permute-done((bf16[16,7168]{1,0:T(8,128)(2,1)S(1)}, bf16[16,7168]{1,0:T(8,128)(2,1)S(1)}, u32[]{:S(2)}, u32[]{:S(2)}) %collective-permute-start.16) | collective-permute-done | bytes 229408 | tf_op jit(solution)/shard_map/ppermute | solution.py:161
  (33 shorter events, 8.0 us)
Async XLA Ops:
  0.6 56.2 %copy-start = (bf16[1,128,576]{1,2,0:T(8,128)(2,1)S(1)}, bf16[1,128,576]{1,2,0:T(8,128)(2,1)}, u32[]{:S(2)}) copy-start(bf16[1,128,576]{1,2,0:T(8,128)(2,1)} %param.15) | copy-start | bytes 442372
  0.6 41.1 %collective-permute-start.7 = (bf16[1,7168,256]{2,1,0:T(8,128)(2,1)}, bf16[1,7168,256]{2,1,0:T(8,128)(2,1)}, u32[]{:S(2)}, u32[]{:S(2)}) collective-permute-start(bf16[1,7168,256]{2,1,0:T(8,128)(2,1)} %refs_9_.1), channel_id=1, source_target_pairs={{0,8},{8,0},{1,9},{9,1},{2,10},{10,2},{3,11},{11,3},{4,12},{12,4},... | collective-permute-start | bytes 11010056 | tf_op jit(solution)/shard_map/ppermute | solution.py:164
  1.2 40.6 %collective-permute-start.8 = (bf16[1,7168,256]{2,1,0:T(8,128)(2,1)}, bf16[1,7168,256]{2,1,0:T(8,128)(2,1)}, u32[]{:S(2)}, u32[]{:S(2)}) collective-permute-start(bf16[1,7168,256]{2,1,0:T(8,128)(2,1)} %refs_10_.1), channel_id=1, source_target_pairs={{0,8},{8,0},{1,9},{9,1},{2,10},{10,2},{3,11},{11,3},{4,12},{12,4},... | collective-permute-start | bytes 11010056 | tf_op jit(solution)/shard_map/ppermute | solution.py:164
  1.2 40.5 %collective-permute-start.9 = (bf16[1,256,7168]{2,1,0:T(8,128)(2,1)}, bf16[1,256,7168]{2,1,0:T(8,128)(2,1)}, u32[]{:S(2)}, u32[]{:S(2)}) collective-permute-start(bf16[1,256,7168]{2,1,0:T(8,128)(2,1)} %refs_11_.1), channel_id=1, source_target_pairs={{0,8},{8,0},{1,9},{9,1},{2,10},{10,2},{3,11},{11,3},{4,12},{12,4},... | collective-permute-start | bytes 11010056 | tf_op jit(solution)/shard_map/ppermute | solution.py:164
  2.8 15.1 %collective-permute-start.3 = (bf16[16,7296]{1,0:T(8,128)(2,1)S(1)}, bf16[16,7296]{1,0:T(8,128)(2,1)S(1)}, u32[]{:S(2)}, u32[]{:S(2)}) collective-permute-start(bf16[16,7296]{1,0:T(8,128)(2,1)S(1)} %pack.1.refs_0_), channel_id=1, source_target_pairs={{0,4},{1,5},{2,6},{3,7},{4,0},{5,1},{6,2},{7,3},{8,12},{9,13},{10,... | collective-permute-start | bytes 700424 | tf_op jit(solution)/shard_map/ppermute | solution.py:161
  6.5 13.0 %collective-permute-start.1 = (bf16[16,7296]{1,0:T(8,128)(2,1)S(1)}, bf16[16,7296]{1,0:T(8,128)(2,1)S(1)}, u32[]{:S(2)}, u32[]{:S(2)}) collective-permute-start(bf16[16,7296]{1,0:T(8,128)(2,1)S(1)} %pack.1.refs_0_), channel_id=1, source_target_pairs={{0,2},{1,3},{2,0},{3,1},{4,6},{5,7},{6,4},{7,5},{8,10},{9,11},{10,... | collective-permute-start | bytes 700424 | tf_op jit(solution)/shard_map/ppermute | solution.py:161
  17.9 7.4 %collective-permute-start = (bf16[16,7296]{1,0:T(8,128)(2,1)S(1)}, bf16[16,7296]{1,0:T(8,128)(2,1)S(1)}, u32[]{:S(2)}, u32[]{:S(2)}) collective-permute-start(bf16[16,7296]{1,0:T(8,128)(2,1)S(1)} %pack.1.refs_0_), channel_id=1, source_target_pairs={{0,1},{1,0},{2,3},{3,2},{4,5},{5,4},{6,7},{7,6},{8,9},{9,8},{10,11... | collective-permute-start | bytes 700424 | tf_op jit(solution)/shard_map/ppermute | solution.py:161
  19.5 7.9 %collective-permute-start.5 = (bf16[16,7296]{1,0:T(8,128)(2,1)S(1)}, bf16[16,7296]{1,0:T(8,128)(2,1)S(1)}, u32[]{:S(2)}, u32[]{:S(2)}) collective-permute-start(bf16[16,7296]{1,0:T(8,128)(2,1)S(1)} %collective-permute-done.3.refs_4_), channel_id=1, source_target_pairs={{0,2},{1,3},{2,0},{3,1},{4,6},{5,7},{6,4},{7,5},{8,10},{9,11},{10,... | collective-permute-start | bytes 700424 | tf_op jit(solution)/shard_map/ppermute | solution.py:161
  25.3 8.6 %collective-permute-start.4 = (bf16[16,7296]{1,0:T(8,128)(2,1)S(1)}, bf16[16,7296]{1,0:T(8,128)(2,1)S(1)}, u32[]{:S(2)}, u32[]{:S(2)}) collective-permute-start(bf16[16,7296]{1,0:T(8,128)(2,1)S(1)} %collective-permute-done.3.refs_4_), channel_id=1, source_target_pairs={{0,1},{1,0},{2,3},{3,2},{4,5},{5,4},{6,7},{7,6},{8,9},{9,8},{10,11... | collective-permute-start | bytes 700424 | tf_op jit(solution)/shard_map/ppermute | solution.py:161
  27.3 11.6 %collective-permute-start.2 = (bf16[16,7296]{1,0:T(8,128)(2,1)S(1)}, bf16[16,7296]{1,0:T(8,128)(2,1)S(1)}, u32[]{:S(2)}, u32[]{:S(2)}) collective-permute-start(bf16[16,7296]{1,0:T(8,128)(2,1)S(1)} %collective-permute-done.1.refs_2_), channel_id=1, source_target_pairs={{0,1},{1,0},{2,3},{3,2},{4,5},{5,4},{6,7},{7,6},{8,9},{9,8},{10,11... | collective-permute-start | bytes 700424 | tf_op jit(solution)/shard_map/ppermute | solution.py:161
  33.9 7.9 %collective-permute-start.6 = (bf16[16,7296]{1,0:T(8,128)(2,1)S(1)}, bf16[16,7296]{1,0:T(8,128)(2,1)S(1)}, u32[]{:S(2)}, u32[]{:S(2)}) collective-permute-start(bf16[16,7296]{1,0:T(8,128)(2,1)S(1)} %collective-permute-done.5.refs_6_), channel_id=1, source_target_pairs={{0,1},{1,0},{2,3},{3,2},{4,5},{5,4},{6,7},{7,6},{8,9},{9,8},{10,11... | collective-permute-start | bytes 700424 | tf_op jit(solution)/shard_map/ppermute | solution.py:161
  41.8 2.0 %copy-start.1 = (bf16[1,7168,256]{2,1,0:T(8,128)(2,1)S(1)}, bf16[1,7168,256]{2,1,0:T(8,128)(2,1)}, u32[]{:S(2)}) copy-start(bf16[1,7168,256]{2,1,0:T(8,128)(2,1)} %refs_9_.1) | copy-start | bytes 11010052
  43.8 2.0 %copy-start.2 = (bf16[1,7168,256]{2,1,0:T(8,128)(2,1)S(1)}, bf16[1,7168,256]{2,1,0:T(8,128)(2,1)}, u32[]{:S(2)}) copy-start(bf16[1,7168,256]{2,1,0:T(8,128)(2,1)} %refs_10_.1) | copy-start | bytes 11010052
  45.9 2.0 %copy-start.3 = (bf16[1,256,7168]{2,1,0:T(8,128)(2,1)S(1)}, bf16[1,256,7168]{2,1,0:T(8,128)(2,1)}, u32[]{:S(2)}) copy-start(bf16[1,256,7168]{2,1,0:T(8,128)(2,1)} %refs_11_.1) | copy-start | bytes 11010052
  47.9 8.9 %copy-start.4 = (bf16[1,1024,576]{1,2,0:T(8,128)(2,1)S(1)}, bf16[1,1024,576]{1,2,0:T(8,128)(2,1)}, u32[]{:S(2)}) copy-start(bf16[1,1024,576]{1,2,0:T(8,128)(2,1)} %param.16) | copy-start | bytes 3538948
  55.6 8.6 %collective-permute-start.14 = (bf16[16,7168]{1,0:T(8,128)(2,1)S(1)}, bf16[16,7168]{1,0:T(8,128)(2,1)S(1)}, u32[]{:S(2)}, u32[]{:S(2)}) collective-permute-start(bf16[16,7168]{1,0:T(8,128)(2,1)S(1)} %get-tuple-element.17), channel_id=1, source_target_pairs={{0,1},{1,0},{2,3},{3,2},{4,5},{5,4},{6,7},{7,6},{8,9},{9,8},{10,11... | collective-permute-start | bytes 688136 | tf_op jit(solution)/shard_map/ppermute | solution.py:161
  57.6 11.6 %collective-permute-start.11 = (bf16[16,7168]{1,0:T(8,128)(2,1)S(1)}, bf16[16,7168]{1,0:T(8,128)(2,1)S(1)}, u32[]{:S(2)}, u32[]{:S(2)}) collective-permute-start(bf16[16,7168]{1,0:T(8,128)(2,1)S(1)} %get-tuple-element.13), channel_id=1, source_target_pairs={{0,1},{1,0},{2,3},{3,2},{4,5},{5,4},{6,7},{7,6},{8,9},{9,8},{10,11... | collective-permute-start | bytes 688136 | tf_op jit(solution)/shard_map/ppermute | solution.py:161
  58.5 15.0 %collective-permute-start.13 = (bf16[16,7168]{1,0:T(8,128)(2,1)S(1)}, bf16[16,7168]{1,0:T(8,128)(2,1)S(1)}, u32[]{:S(2)}, u32[]{:S(2)}) collective-permute-start(bf16[16,7168]{1,0:T(8,128)(2,1)S(1)} %get-tuple-element.15), channel_id=1, source_target_pairs={{0,1},{1,0},{2,3},{3,2},{4,5},{5,4},{6,7},{7,6},{8,9},{9,8},{10,11... | collective-permute-start | bytes 688136 | tf_op jit(solution)/shard_map/ppermute | solution.py:161
  59.7 16.3 %collective-permute-start.10 = (bf16[16,7168]{1,0:T(8,128)(2,1)S(1)}, bf16[16,7168]{1,0:T(8,128)(2,1)S(1)}, u32[]{:S(2)}, u32[]{:S(2)}) collective-permute-start(bf16[16,7168]{1,0:T(8,128)(2,1)S(1)} %get-tuple-element.11), channel_id=1, source_target_pairs={{0,1},{1,0},{2,3},{3,2},{4,5},{5,4},{6,7},{7,6},{8,9},{9,8},{10,11... | collective-permute-start | bytes 688136 | tf_op jit(solution)/shard_map/ppermute | solution.py:161
  64.3 9.2 %collective-permute-start.15 = (bf16[16,7168]{1,0:T(8,128)(2,1)S(1)}, bf16[16,7168]{1,0:T(8,128)(2,1)S(1)}, u32[]{:S(2)}, u32[]{:S(2)}) collective-permute-start(bf16[16,7168]{1,0:T(8,128)(2,1)S(1)} %add_convert_fusion.2), channel_id=1, source_target_pairs={{0,2},{1,3},{2,0},{3,1},{4,6},{5,7},{6,4},{7,5},{8,10},{9,11},{10,... | collective-permute-start | bytes 688136 | tf_op jit(solution)/shard_map/ppermute | solution.py:161
  69.2 7.5 %collective-permute-start.12 = (bf16[16,7168]{1,0:T(8,128)(2,1)S(1)}, bf16[16,7168]{1,0:T(8,128)(2,1)S(1)}, u32[]{:S(2)}, u32[]{:S(2)}) collective-permute-start(bf16[16,7168]{1,0:T(8,128)(2,1)S(1)} %add_convert_fusion.3), channel_id=1, source_target_pairs={{0,2},{1,3},{2,0},{3,1},{4,6},{5,7},{6,4},{7,5},{8,10},{9,11},{10,... | collective-permute-start | bytes 688136 | tf_op jit(solution)/shard_map/ppermute | solution.py:161
  73.6 9.4 %collective-permute-start.16 = (bf16[16,7168]{1,0:T(8,128)(2,1)S(1)}, bf16[16,7168]{1,0:T(8,128)(2,1)S(1)}, u32[]{:S(2)}, u32[]{:S(2)}) collective-permute-start(bf16[16,7168]{1,0:T(8,128)(2,1)S(1)} %add_convert_fusion.1), channel_id=1, source_target_pairs={{0,4},{1,5},{2,6},{3,7},{4,0},{5,1},{6,2},{7,3},{8,12},{9,13},{10,... | collective-permute-start | bytes 688136 | tf_op jit(solution)/shard_map/ppermute | solution.py:161

commit v2 on v1

--- a/solution.py
+++ b/solution.py
@@ -11,6 +11,7 @@
 HEAD_QK = 192
 SLICES = 4
 LANES = 128
+CALL_ROWS = 256
 PAIR = 2
 
 
@@ -22,9 +23,17 @@
     return best
 
 
-def pack_kernel(experts_all, routes_ref, weight_ref, tokens_ref, out_ref):
-    rows, width = tokens_ref.shape
-    out_ref[:, :width] = tokens_ref[...]
+def pack_kernel(experts_all, routes_hbm, weight_hbm, tokens_hbm, out_ref, routes_ref, weight_ref, sems):
+    rows, width = tokens_hbm.shape
+    copies = [
+        pltpu.make_async_copy(tokens_hbm, out_ref.at[:, pl.ds(0, width)], sems.at[0]),
+        pltpu.make_async_copy(routes_hbm, routes_ref, sems.at[1]),
+        pltpu.make_async_copy(weight_hbm, weight_ref, sems.at[2]),
+    ]
+    for c in copies:
+        c.start()
+    copies[1].wait()
+    copies[2].wait()
     extra = out_ref.shape[1] - width
     column = lax.broadcasted_iota(jnp.int32, (rows, extra), 1)
     part = column // experts_all
@@ -53,77 +62,104 @@
         ),
     )
     out_ref[:, width:] = picked.astype(jnp.bfloat16)
+    copies[0].wait()
 
 
 def pack(tokens, routes, route_weight, experts_all):
     rows, width = tokens.shape
     extra = -(-3 * experts_all // LANES) * LANES
+    operands = (routes.T, route_weight.T, tokens)
     return pl.pallas_call(
         functools.partial(pack_kernel, experts_all),
         out_shape=pltpu.VMEM((rows, width + extra), tokens.dtype),
-        in_specs=[pl.BlockSpec(memory_space=pltpu.VMEM)] * 3,
+        in_specs=[pl.BlockSpec(memory_space=pltpu.HBM)] * 3,
         out_specs=pl.BlockSpec(memory_space=pltpu.VMEM),
+        scratch_shapes=[
+            pltpu.VMEM(routes.T.shape, routes.dtype),
+            pltpu.VMEM(route_weight.T.shape, route_weight.dtype),
+            pltpu.SemaphoreType.DMA((3,)),
+        ],
+        compiler_params=pltpu.CompilerParams(vmem_limit_bytes=2 << 20),
         name="pack",
-    )(routes.T, route_weight.T, tokens)
+    )(*(pltpu.with_memory_space_constraint(a, pltpu.HBM) for a in operands))
 
 
 def expert_kernel(count, steps, *refs):
-    blocks, masks = refs[:count], refs[count]
-    weights = refs[count + 1 : count + 7]
-    outs = refs[count + 7 : 2 * count + 7]
-    rows, width = outs[0].shape
+    blocks, mask = refs[:count], refs[count]
+    gate_w, up_w, down_w = refs[count + 1 : count + 4]
+    outs = refs[count + 4 :]
+    width = outs[0].shape[1]
+    rows = outs[0].shape[0]
     depth = width // steps
 
     def columns(part):
         return jnp.concatenate([b[:, part] for b in blocks], axis=0)
 
     table = columns(pl.ds(width, blocks[0].shape[1] - width)).astype(jnp.float32)
-    acts, scales = [], []
-    for p in range(2):
-        gate = up = None
-        for k in range(steps):
-            part = pl.ds(k * depth, depth)
-            x = columns(part)
-            g = jnp.dot(x, weights[3 * p][0, part, :], preferred_element_type=jnp.float32)
-            u = jnp.dot(x, weights[3 * p + 1][0, part, :], preferred_element_type=jnp.float32)
-            gate, up = (g, u) if gate is None else (gate + g, up + u)
-        acts.append((jax.nn.silu(gate) * up).astype(jnp.bfloat16))
-        scales.append(jnp.sum(table * masks[p : p + 1, :], axis=1, keepdims=True))
+    scale = jnp.sum(table * mask[...], axis=1, keepdims=True)
+    gate = up = None
+    for k in range(steps):
+        part = pl.ds(k * depth, depth)
+        x = columns(part)
+        g = jnp.dot(x, gate_w[0, part, :], preferred_element_type=jnp.float32)
+        u = jnp.dot(x, up_w[0, part, :], preferred_element_type=jnp.float32)
+        gate, up = (g, u) if gate is None else (gate + g, up + u)
+    act = (jax.nn.silu(gate) * up).astype(jnp.bfloat16)
     for n in range(steps):
         part = pl.ds(n * depth, depth)
-        total = None
-        for p in range(2):
-            value = scales[p] * jnp.dot(
-                acts[p], weights[3 * p + 2][0, :, part], preferred_element_type=jnp.float32
-            )
-            total = value if total is None else total + value
-        total = total.astype(jnp.bfloat16)
+        value = scale * jnp.dot(act, down_w[0, :, part], preferred_element_type=jnp.float32)
+        value = value.astype(jnp.bfloat16)
         for i, o in enumerate(outs):
-            o[:, part] = total[i * rows : (i + 1) * rows]
-
-
-def run_experts(blocks, masks, weights):
+            o[:, part] = value[i * rows : (i + 1) * rows]
+
+
+def stage_kernel(count, *refs):
+    sources, targets, sems = refs[:count], refs[count : 2 * count], refs[2 * count]
+    copies = [
+        pltpu.make_async_copy(a, b, sems.at[i])
+        for i, (a, b) in enumerate(zip(sources, targets, strict=True))
+    ]
+    for c in copies:
+        c.start()
+    for c in copies:
+        c.wait()
+
+
+def stage(*arrays):
+    count = len(arrays)
+    return pl.pallas_call(
+        functools.partial(stage_kernel, count),
+        out_shape=[pltpu.VMEM(a.shape, a.dtype) for a in arrays],
+        in_specs=[pl.BlockSpec(memory_space=pltpu.HBM)] * count,
+        out_specs=[pl.BlockSpec(memory_space=pltpu.VMEM)] * count,
+        scratch_shapes=[pltpu.SemaphoreType.DMA((count,))],
+        compiler_params=pltpu.CompilerParams(vmem_limit_bytes=1 << 20),
+        cost_estimate=pl.CostEstimate(
+            flops=0, bytes_accessed=sum(2 * a.size for a in arrays), transcendentals=0
+        ),
+        name="stage",
+    )(*(pltpu.with_memory_space_constraint(a, pltpu.HBM) for a in arrays))
+
+
+def run_experts(blocks, group, mask, weights):
     count = len(blocks)
     rows, packed = blocks[0].shape
     width, hidden = weights[0].shape[1:]
     steps = width // chunk_of(width, 1024)
+    pinned = [pltpu.with_memory_space_constraint(a, pltpu.VMEM) for a in (*blocks, mask, *weights)]
     return pl.pallas_call(
         functools.partial(expert_kernel, count, steps),
-        out_shape=[pltpu.VMEM((rows, width), jnp.bfloat16)] * count,
-        in_specs=[pl.BlockSpec(memory_space=pltpu.VMEM)] * (count + 7),
-        out_specs=[pl.BlockSpec(memory_space=pltpu.VMEM)] * count,
+        out_shape=[pltpu.VMEM((group * rows, width), jnp.bfloat16)] * (count // group),
+        in_specs=[pl.BlockSpec(memory_space=pltpu.VMEM)] * len(pinned),
+        out_specs=[pl.BlockSpec(memory_space=pltpu.VMEM)] * (count // group),
         compiler_params=pltpu.CompilerParams(vmem_limit_bytes=2 * count * rows * packed + (16 << 20)),
         cost_estimate=pl.CostEstimate(
-            flops=2 * count * rows * width * hidden * 6,
-            bytes_accessed=2 * 6 * width * hidden,
+            flops=2 * count * rows * width * hidden * 3,
+            bytes_accessed=2 * 3 * width * hidden,
             transcendentals=0,
         ),
         name="experts",
-    )(
-        *(pltpu.with_memory_space_constraint(b, pltpu.VMEM) for b in blocks),
-        masks,
-        *(pltpu.with_memory_space_constraint(w, pltpu.VMEM) for w in weights),
-    )
+    )(*pinned)
 
 
 def attend(queries, latent_cache, lengths):
@@ -163,33 +199,54 @@
     def swap(value):
         return lax.ppermute(value, "node", [(i, i ^ 1) for i in range(nodes)])
 
-    own = (w_gate, w_up, w_down)
-    weights = own + tuple(swap(w) for w in own)
-    dev, node = lax.axis_index("dev"), lax.axis_index("node")
-    here = (node * devs + dev) // SLICES
-    there = ((node ^ 1) * devs + dev) // SLICES
-
-    packed = pack(tokens, routes, route_weight, experts_all)
-    extra = packed.shape[1] - tokens.shape[1]
+    here = (lax.axis_index("node") * devs + lax.axis_index("dev")) // SLICES
+
+    extra = -(-3 * experts_all // LANES) * LANES
     column = jnp.arange(extra, dtype=jnp.int32)
     named = jnp.where(column < 3 * experts_all, column % experts_all, -1)
-    masks = (named[None, :] == jnp.stack([here, there])[:, None]).astype(jnp.float32)
-
-    gathered = {0: packed}
+    mask = (named == here).astype(jnp.float32)[None, :]
+    barrier = lax.optimization_barrier
+    tokens, mask = barrier((tokens, mask))
+    packed = pack(tokens, routes, route_weight, experts_all)
+    weights = stage(w_gate, w_up, w_down)
+
+    barrier = lax.optimization_barrier
+    gathered, across = {0: packed}, {}
     bit = lines // 2
     while bit:
         for m in list(gathered):
             gathered[m ^ bit] = hop(gathered[m], bit * PAIR)
+        if bit == lines // 2:
+            gathered[bit], weights = barrier((gathered[bit], weights))
         bit //= 2
+    for m in range(lines):
+        if m == 2:
+            gathered[m], across[m - 1] = barrier((gathered[m], across[m - 1]))
+        across[m] = hop(gathered[m], 1)
     keys = [(m, s) for m in range(lines) for s in range(PAIR)]
-    blocks = [gathered[m] if s == 0 else hop(gathered[m], 1) for m, s in keys]
-
-    partial = dict(zip(keys, run_experts(blocks, masks, weights), strict=True))
+    mine = [(gathered, across)[s][m] for m, s in keys]
+    theirs = [swap(x) for x in mine]
+
+    rows = tokens.shape[0]
+    batch = max(1, CALL_ROWS // (2 * PAIR * rows))
+    kept, sent = [], []
+    for first in range(0, lines, batch):
+        cut = slice(PAIR * first, PAIR * (first + batch))
+        sums = run_experts(mine[cut] + theirs[cut], PAIR, mask, weights)
+        kept += sums[: len(sums) // 2]
+        sent += sums[len(sums) // 2 :]
     context = attend(queries, latent_cache, lengths)
 
-    terms = {m: [partial[m, 0]] for m in range(lines)}
+    terms, crossed = {}, {}
     for m in reversed(range(lines)):
-        terms[m].append(hop(partial[m, 1], 1))
+        met = swap(sent[m])
+        out = add_all(kept[m][rows:], met[rows:])
+        if m + 2 in crossed:
+            out, crossed[m + 2] = barrier((out, crossed[m + 2]))
+        crossed[m] = hop(out, 1)
+        terms[m] = [kept[m][:rows], met[:rows]]
+    for m in range(lines):
+        terms[m].append(crossed[m])
     bit = 1
     while bit < lines:
         for m in sorted(terms, reverse=True):

time: 84.1 us -> 71.6 us (0.85)
  waiting for transfers between devices: 45 us -> 36.6 us
  local copies, waits for them, and re-layouts: 6.12 us -> 0.02 us
  starting transfers between devices: 19.5 us -> 21.7 us
    ppermute x14, waiting for transfers between devices: 45 us -> 35.4 us  [hop(): return lax.ppermute(value, 'dev', [(d, d ^ offset) for d in range(devs)])]
    unnamed x10 -> x4, local copies, waits for them, and re-layouts: 6.12 us -> 0.02 us
    pallas_call x1, Pallas kernels: 7.7 us -> 3.17 us  [run_experts(): pl.pallas_call(functools.partial(expert_kernel, count, steps), out_shape=...]
    pallas_call x0 -> x1, Pallas kernels: none -> 4.23 us  [stage(): pl.pallas_call(functools.partial(stage_kernel, count), out_shape=[pltpu.V...]
    ppermute x3 -> x12, starting transfers between devices: 1.03 us -> 2.25 us  [swap(): return lax.ppermute(value, 'node', [(i, i ^ 1) for i in range(nodes)])]
    ppermute x3 -> x12, waiting for transfers between devices: 0.01 us -> 1.22 us  [swap(): return lax.ppermute(value, 'node', [(i, i ^ 1) for i in range(nodes)])]
    ppermute x14, starting transfers between devices: 18.5 us -> 19.5 us  [hop(): return lax.ppermute(value, 'dev', [(d, d ^ offset) for d in range(devs)])]
  transfers between devices with their start and end apart: 17 -> 26, of which waited for: 11 -> 14; matrix products, arithmetic and copies ran while one was open for 3% -> 3% of each run, Pallas kernels for 1% -> 6%
where the time goes in v2:
time: 71.6 us; the launch traced here: 71.4 us
  waiting for transfers between devices  36.6 us (51%)
  starting transfers between devices  21.7 us (30%)
  Pallas kernels  8.39 us (12%)
  matrix products  1.64 us (2%)
  other arithmetic  1.59 us (2%)
  between operations  1.45 us (2%)
    ppermute x14, waiting for transfers between devices, hop(): return lax.ppermute(value, 'dev', [(d, d ^ offset) for d in range(devs)])  35.4 us
    ppermute x14, starting transfers between devices, hop(): return lax.ppermute(value, 'dev', [(d, d ^ offset) for d in range(devs)])  19.5 us
    pallas_call x1, Pallas kernels, stage(): pl.pallas_call(functools.partial(stage_kernel, count), out_shape=[pltpu.V...  4.23 us
    pallas_call x1, Pallas kernels, run_experts(): pl.pallas_call(functools.partial(expert_kernel, count, steps), out_shape=...  3.17 us
    ppermute x12, starting transfers between devices, swap(): return lax.ppermute(value, 'node', [(i, i ^ 1) for i in range(nodes)])  2.25 us
  transfers between devices with their start and end apart: 26, of which 14 were waited for; matrix products, arithmetic and copies ran while one was open for 3% of the time, Pallas kernels for 6%

profile of v2, /device:TPU:0, one launch (start us, length us, event | category | flops | bytes accessed | tf_op | source)
XLA Modules:
  0.0 71.4 jit_solution(6039574722321316999)
XLA Ops:
  0.7 1.0 %pack.1.refs_0_ = bf16[16,7296]{1,0:T(8,128)(2,1)S(1)} custom-call(s32[2,16]{1,0:T(2,128)} %bitcast.19, f32[2,16]{1,0:T(2,128)} %bitcast.20, bf16[16,7168]{1,0:T(8,128)(2,1)} %tokens_hbm), custom_call_target="tpu_custom_call" | custom-call | tf_op jit(solution)/shard_map/pack/pallas_call | solution.py:72
  1.7 3.1 %collective-permute-start.1 = (bf16[16,7296]{1,0:T(8,128)(2,1)S(1)}, bf16[16,7296]{1,0:T(8,128)(2,1)S(1)}, u32[]{:S(2)}, u32[]{:S(2)}) collective-permute-start(bf16[16,7296]{1,0:T(8,128)(2,1)S(1)} %pack.1.refs_0_), channel_id=1, source_target_pairs={{0,2},{1,3},{2,0},{3,1},{4,6},{5,7},{6,4},{7,5},{8,10},{9,11},{10,... | collective-permute-start | bytes 700424 | tf_op jit(solution)/shard_map/ppermute | solution.py:197
  4.8 2.6 %collective-permute-start.2 = (bf16[16,7296]{1,0:T(8,128)(2,1)S(1)}, bf16[16,7296]{1,0:T(8,128)(2,1)S(1)}, u32[]{:S(2)}, u32[]{:S(2)}) collective-permute-start(bf16[16,7296]{1,0:T(8,128)(2,1)S(1)} %pack.1.refs_0_), channel_id=1, source_target_pairs={{0,4},{1,5},{2,6},{3,7},{4,0},{5,1},{6,2},{7,3},{8,12},{9,13},{10,... | collective-permute-start | bytes 700424 | tf_op jit(solution)/shard_map/ppermute | solution.py:197
  7.4 1.5 %collective-permute-start = (bf16[16,7296]{1,0:T(8,128)(2,1)S(1)}, bf16[16,7296]{1,0:T(8,128)(2,1)S(1)}, u32[]{:S(2)}, u32[]{:S(2)}) collective-permute-start(bf16[16,7296]{1,0:T(8,128)(2,1)S(1)} %pack.1.refs_0_), channel_id=1, source_target_pairs={{0,1},{1,0},{2,3},{3,2},{4,5},{5,4},{6,7},{7,6},{8,9},{9,8},{10,11... | collective-permute-start | bytes 700424 | tf_op jit(solution)/shard_map/ppermute | solution.py:197
  8.9 4.2 %stage.1 = (bf16[1,7168,256]{2,1,0:T(8,128)(2,1)S(1)}, bf16[1,7168,256]{2,1,0:T(8,128)(2,1)S(1)}, bf16[1,256,7168]{2,1,0:T(8,128)(2,1)S(1)}) custom-call(bf16[1,7168,256]{2,1,0:T(8,128)(2,1)} %refs_0_.1, bf16[1,7168,256]{2,1,0:T(8,128)(2,1)} %refs_1_.1, bf16[1,256,7168]{2,1,0:T(8,128)(2,1)} %refs_2_.1), custom_call_target="tpu_custom_call" | custom-call | bytes 11010048 | tf_op jit(solution)/shard_map/stage/pallas_call | solution.py:130
  13.1 2.2 %collective-permute-done.1.refs_2_ = bf16[16,7296]{1,0:T(8,128)(2,1)S(1)} collective-permute-done((bf16[16,7296]{1,0:T(8,128)(2,1)S(1)}, bf16[16,7296]{1,0:T(8,128)(2,1)S(1)}, u32[]{:S(2)}, u32[]{:S(2)}) %collective-permute-start.1) | collective-permute-done | bytes 233504 | tf_op jit(solution)/shard_map/ppermute | solution.py:197
  15.3 1.7 %collective-permute-start.3 = (bf16[16,7296]{1,0:T(8,128)(2,1)S(1)}, bf16[16,7296]{1,0:T(8,128)(2,1)S(1)}, u32[]{:S(2)}, u32[]{:S(2)}) collective-permute-start(bf16[16,7296]{1,0:T(8,128)(2,1)S(1)} %collective-permute-done.1.refs_2_), channel_id=1, source_target_pairs={{0,1},{1,0},{2,3},{3,2},{4,5},{5,4},{6,7},{7,6},{8,9},{9,8},{10,11... | collective-permute-start | bytes 700424 | tf_op jit(solution)/shard_map/ppermute | solution.py:197
  18.8 3.4 %collective-permute-done.3.refs_3_ = bf16[16,7296]{1,0:T(8,128)(2,1)S(1)} collective-permute-done((bf16[16,7296]{1,0:T(8,128)(2,1)S(1)}, bf16[16,7296]{1,0:T(8,128)(2,1)S(1)}, u32[]{:S(2)}, u32[]{:S(2)}) %collective-permute-start.3) | collective-permute-done | bytes 233504 | tf_op jit(solution)/shard_map/ppermute | solution.py:197
  22.2 1.4 %collective-permute-start.4 = (bf16[16,7296]{1,0:T(8,128)(2,1)S(1)}, bf16[16,7296]{1,0:T(8,128)(2,1)S(1)}, u32[]{:S(2)}, u32[]{:S(2)}) collective-permute-start(bf16[16,7296]{1,0:T(8,128)(2,1)S(1)} %collective-permute-done.2.refs_4_), channel_id=1, source_target_pairs={{0,1},{1,0},{2,3},{3,2},{4,5},{5,4},{6,7},{7,6},{8,9},{9,8},{10,11... | collective-permute-start | bytes 700424 | tf_op jit(solution)/shard_map/ppermute | solution.py:197
  23.9 1.5 %collective-permute-start.6 = (bf16[16,7296]{1,0:T(8,128)(2,1)S(1)}, bf16[16,7296]{1,0:T(8,128)(2,1)S(1)}, u32[]{:S(2)}, u32[]{:S(2)}) collective-permute-start(bf16[16,7296]{1,0:T(8,128)(2,1)S(1)} %collective-permute-done.5.refs_6_), channel_id=1, source_target_pairs={{0,1},{1,0},{2,3},{3,2},{4,5},{5,4},{6,7},{7,6},{8,9},{9,8},{10,11... | collective-permute-start | bytes 700424 | tf_op jit(solution)/shard_map/ppermute | solution.py:197
  26.1 4.6 %collective-permute-done.4.refs_5_ = bf16[16,7296]{1,0:T(8,128)(2,1)S(1)} collective-permute-done((bf16[16,7296]{1,0:T(8,128)(2,1)S(1)}, bf16[16,7296]{1,0:T(8,128)(2,1)S(1)}, u32[]{:S(2)}, u32[]{:S(2)}) %collective-permute-start.4) | collective-permute-done | bytes 233504 | tf_op jit(solution)/shard_map/ppermute | solution.py:197
  30.7 2.5 %collective-permute-done.6.refs_7_ = bf16[16,7296]{1,0:T(8,128)(2,1)S(1)} collective-permute-done((bf16[16,7296]{1,0:T(8,128)(2,1)S(1)}, bf16[16,7296]{1,0:T(8,128)(2,1)S(1)}, u32[]{:S(2)}, u32[]{:S(2)}) %collective-permute-start.6) | collective-permute-done | bytes 233504 | tf_op jit(solution)/shard_map/ppermute | solution.py:197
  34.7 3.2 %experts.1 = (bf16[32,7168]{1,0:T(8,128)(2,1)S(1)}, bf16[32,7168]{1,0:T(8,128)(2,1)S(1)}, bf16[32,7168]{1,0:T(8,128)(2,1)S(1)}, bf16[32,7168]{1,0:T(8,128)(2,1)S...) custom-call(bf16[16,7296]{1,0:T(8,128)(2,1)S(1)} %pack.1.refs_0_, ...), custom_call_target="tpu_custom_call" | custom-call | flops 2818572288 | bytes 11010048 | tf_op jit(solution)/shard_map/experts/pallas_call | solution.py:150
  39.8 1.1 %collective-permute-start.21 = (bf16[16,7168]{1,0:T(8,128)(2,1)S(1)}, bf16[16,7168]{1,0:T(8,128)(2,1)S(1)}, u32[]{:S(2)}, u32[]{:S(2)}) collective-permute-start(bf16[16,7168]{1,0:T(8,128)(2,1)S(1)} %add_convert_fusion.4), channel_id=1, source_target_pairs={{0,1},{1,0},{2,3},{3,2},{4,5},{5,4},{6,7},{7,6},{8,9},{9,8},{10,11... | collective-permute-start | bytes 688136 | tf_op jit(solution)/shard_map/ppermute | solution.py:197
  41.4 1.1 %collective-permute-start.17 = (bf16[16,7168]{1,0:T(8,128)(2,1)S(1)}, bf16[16,7168]{1,0:T(8,128)(2,1)S(1)}, u32[]{:S(2)}, u32[]{:S(2)}) collective-permute-start(bf16[16,7168]{1,0:T(8,128)(2,1)S(1)} %add_convert_fusion.6), channel_id=1, source_target_pairs={{0,1},{1,0},{2,3},{3,2},{4,5},{5,4},{6,7},{7,6},{8,9},{9,8},{10,11... | collective-permute-start | bytes 688136 | tf_op jit(solution)/shard_map/ppermute | solution.py:197
  42.7 5.7 %collective-permute-done.21 = bf16[16,7168]{1,0:T(8,128)(2,1)S(1)} collective-permute-done((bf16[16,7168]{1,0:T(8,128)(2,1)S(1)}, bf16[16,7168]{1,0:T(8,128)(2,1)S(1)}, u32[]{:S(2)}, u32[]{:S(2)}) %collective-permute-start.21) | collective-permute-done | bytes 229408 | tf_op jit(solution)/shard_map/ppermute | solution.py:197
  48.3 1.0 %collective-permute-start.22 = (bf16[16,7168]{1,0:T(8,128)(2,1)S(1)}, bf16[16,7168]{1,0:T(8,128)(2,1)S(1)}, u32[]{:S(2)}, u32[]{:S(2)}) collective-permute-start(bf16[16,7168]{1,0:T(8,128)(2,1)S(1)} %add_convert_fusion.5), channel_id=1, source_target_pairs={{0,1},{1,0},{2,3},{3,2},{4,5},{5,4},{6,7},{7,6},{8,9},{9,8},{10,11... | collective-permute-start | bytes 688136 | tf_op jit(solution)/shard_map/ppermute | solution.py:197
  49.5 3.8 %collective-permute-done.17 = bf16[16,7168]{1,0:T(8,128)(2,1)S(1)} collective-permute-done((bf16[16,7168]{1,0:T(8,128)(2,1)S(1)}, bf16[16,7168]{1,0:T(8,128)(2,1)S(1)}, u32[]{:S(2)}, u32[]{:S(2)}) %collective-permute-start.17) | collective-permute-done | bytes 229408 | tf_op jit(solution)/shard_map/ppermute | solution.py:197
  53.6 1.5 %collective-permute-start.18 = (bf16[16,7168]{1,0:T(8,128)(2,1)S(1)}, bf16[16,7168]{1,0:T(8,128)(2,1)S(1)}, u32[]{:S(2)}, u32[]{:S(2)}) collective-permute-start(bf16[16,7168]{1,0:T(8,128)(2,1)S(1)} %add_convert_fusion.7), channel_id=1, source_target_pairs={{0,1},{1,0},{2,3},{3,2},{4,5},{5,4},{6,7},{7,6},{8,9},{9,8},{10,11... | collective-permute-start | bytes 688136 | tf_op jit(solution)/shard_map/ppermute | solution.py:197
  55.1 3.1 %collective-permute-done.22 = bf16[16,7168]{1,0:T(8,128)(2,1)S(1)} collective-permute-done((bf16[16,7168]{1,0:T(8,128)(2,1)S(1)}, bf16[16,7168]{1,0:T(8,128)(2,1)S(1)}, u32[]{:S(2)}, u32[]{:S(2)}) %collective-permute-start.22) | collective-permute-done | bytes 229408 | tf_op jit(solution)/shard_map/ppermute | solution.py:197
  59.4 1.7 %collective-permute-start.25 = (bf16[16,7168]{1,0:T(8,128)(2,1)S(1)}, bf16[16,7168]{1,0:T(8,128)(2,1)S(1)}, u32[]{:S(2)}, u32[]{:S(2)}) collective-permute-start(bf16[16,7168]{1,0:T(8,128)(2,1)S(1)} %add_convert_fusion.1), channel_id=1, source_target_pairs={{0,4},{1,5},{2,6},{3,7},{4,0},{5,1},{6,2},{7,3},{8,12},{9,13},{10,... | collective-permute-start | bytes 688136 | tf_op jit(solution)/shard_map/ppermute | solution.py:197
  61.1 1.2 %fusion.2 = bf16[1,128,512]{2,1,0:T(8,128)(2,1)} fusion(bf16[1,1024,576]{1,2,0:T(8,128)(2,1)S(1)} %copy-done.1, f32[128,1024]{1,0:T(8,128)S(1)} %get-tuple-element.49, f32[128]{0:T(128)S(1)} %fusion.5, f32[128]{0:T(128)S(1)} %get-tuple-element.48), kind=kOutput, calls=%fused_computation.4 | convolution fusion | flops 134676480 | bytes 1704960 | tf_op jit(solution)/shard_map/rhl,rlk->rhk/dot_general | solution.py:178
  62.3 6.4 %collective-permute-done.23 = bf16[16,7168]{1,0:T(8,128)(2,1)S(1)} collective-permute-done((bf16[16,7168]{1,0:T(8,128)(2,1)S(1)}, bf16[16,7168]{1,0:T(8,128)(2,1)S(1)}, u32[]{:S(2)}, u32[]{:S(2)}) %collective-permute-start.23) | collective-permute-done | bytes 229408 | tf_op jit(solution)/shard_map/ppermute | solution.py:197
  68.6 1.9 %collective-permute-done.25 = bf16[16,7168]{1,0:T(8,128)(2,1)S(1)} collective-permute-done((bf16[16,7168]{1,0:T(8,128)(2,1)S(1)}, bf16[16,7168]{1,0:T(8,128)(2,1)S(1)}, u32[]{:S(2)}, u32[]{:S(2)}) %collective-permute-start.25) | collective-permute-done | bytes 229408 | tf_op jit(solution)/shard_map/ppermute | solution.py:197
  (48 shorter events, 8.6 us)
Async XLA Ops:
  1.7 13.7 %collective-permute-start.1 = (bf16[16,7296]{1,0:T(8,128)(2,1)S(1)}, bf16[16,7296]{1,0:T(8,128)(2,1)S(1)}, u32[]{:S(2)}, u32[]{:S(2)}) collective-permute-start(bf16[16,7296]{1,0:T(8,128)(2,1)S(1)} %pack.1.refs_0_), channel_id=1, source_target_pairs={{0,2},{1,3},{2,0},{3,1},{4,6},{5,7},{6,4},{7,5},{8,10},{9,11},{10,... | collective-permute-start | bytes 700424 | tf_op jit(solution)/shard_map/ppermute | solution.py:197
  4.8 13.1 %collective-permute-start.2 = (bf16[16,7296]{1,0:T(8,128)(2,1)S(1)}, bf16[16,7296]{1,0:T(8,128)(2,1)S(1)}, u32[]{:S(2)}, u32[]{:S(2)}) collective-permute-start(bf16[16,7296]{1,0:T(8,128)(2,1)S(1)} %pack.1.refs_0_), channel_id=1, source_target_pairs={{0,4},{1,5},{2,6},{3,7},{4,0},{5,1},{6,2},{7,3},{8,12},{9,13},{10,... | collective-permute-start | bytes 700424 | tf_op jit(solution)/shard_map/ppermute | solution.py:197
  7.4 11.5 %collective-permute-start = (bf16[16,7296]{1,0:T(8,128)(2,1)S(1)}, bf16[16,7296]{1,0:T(8,128)(2,1)S(1)}, u32[]{:S(2)}, u32[]{:S(2)}) collective-permute-start(bf16[16,7296]{1,0:T(8,128)(2,1)S(1)} %pack.1.refs_0_), channel_id=1, source_target_pairs={{0,1},{1,0},{2,3},{3,2},{4,5},{5,4},{6,7},{7,6},{8,9},{9,8},{10,11... | collective-permute-start | bytes 700424 | tf_op jit(solution)/shard_map/ppermute | solution.py:197
  15.3 6.9 %collective-permute-start.3 = (bf16[16,7296]{1,0:T(8,128)(2,1)S(1)}, bf16[16,7296]{1,0:T(8,128)(2,1)S(1)}, u32[]{:S(2)}, u32[]{:S(2)}) collective-permute-start(bf16[16,7296]{1,0:T(8,128)(2,1)S(1)} %collective-permute-done.1.refs_2_), channel_id=1, source_target_pairs={{0,1},{1,0},{2,3},{3,2},{4,5},{5,4},{6,7},{7,6},{8,9},{9,8},{10,11... | collective-permute-start | bytes 700424 | tf_op jit(solution)/shard_map/ppermute | solution.py:197
  17.9 6.1 %collective-permute-start.5 = (bf16[16,7296]{1,0:T(8,128)(2,1)S(1)}, bf16[16,7296]{1,0:T(8,128)(2,1)S(1)}, u32[]{:S(2)}, u32[]{:S(2)}) collective-permute-start(bf16[16,7296]{1,0:T(8,128)(2,1)S(1)} %collective-permute-done.2.refs_4_), channel_id=1, source_target_pairs={{0,2},{1,3},{2,0},{3,1},{4,6},{5,7},{6,4},{7,5},{8,10},{9,11},{10,... | collective-permute-start | bytes 700424 | tf_op jit(solution)/shard_map/ppermute | solution.py:197
  18.3 7.1 %collective-permute-start.7 = (bf16[16,7296]{1,0:T(8,128)(2,1)S(1)}, bf16[16,7296]{1,0:T(8,128)(2,1)S(1)}, u32[]{:S(2)}, u32[]{:S(2)}) collective-permute-start(bf16[16,7296]{1,0:T(8,128)(2,1)S(1)} %pack.1.refs_0_), channel_id=1, source_target_pairs={{0,8},{8,0},{1,9},{9,1},{2,10},{10,2},{3,11},{11,3},{4,12},{12,4},... | collective-permute-start | bytes 700424 | tf_op jit(solution)/shard_map/ppermute | solution.py:200
  18.3 7.1 %collective-permute-start.9 = (bf16[16,7296]{1,0:T(8,128)(2,1)S(1)}, bf16[16,7296]{1,0:T(8,128)(2,1)S(1)}, u32[]{:S(2)}, u32[]{:S(2)}) collective-permute-start(bf16[16,7296]{1,0:T(8,128)(2,1)S(1)} %collective-permute-done.1.refs_2_), channel_id=1, source_target_pairs={{0,8},{8,0},{1,9},{9,1},{2,10},{10,2},{3,11},{11,3},{4,12},{12,4},... | collective-permute-start | bytes 700424 | tf_op jit(solution)/shard_map/ppermute | solution.py:200
  18.8 7.1 %collective-permute-start.8 = (bf16[16,7296]{1,0:T(8,128)(2,1)S(1)}, bf16[16,7296]{1,0:T(8,128)(2,1)S(1)}, u32[]{:S(2)}, u32[]{:S(2)}) collective-permute-start(bf16[16,7296]{1,0:T(8,128)(2,1)S(1)} %collective-permute-done.refs_1_), channel_id=1, source_target_pairs={{0,8},{8,0},{1,9},{9,1},{2,10},{10,2},{3,11},{11,3},{4,12},{12,4},... | collective-permute-start | bytes 700424 | tf_op jit(solution)/shard_map/ppermute | solution.py:200
  22.2 8.5 %collective-permute-start.4 = (bf16[16,7296]{1,0:T(8,128)(2,1)S(1)}, bf16[16,7296]{1,0:T(8,128)(2,1)S(1)}, u32[]{:S(2)}, u32[]{:S(2)}) collective-permute-start(bf16[16,7296]{1,0:T(8,128)(2,1)S(1)} %collective-permute-done.2.refs_4_), channel_id=1, source_target_pairs={{0,1},{1,0},{2,3},{3,2},{4,5},{5,4},{6,7},{7,6},{8,9},{9,8},{10,11... | collective-permute-start | bytes 700424 | tf_op jit(solution)/shard_map/ppermute | solution.py:197
  23.9 9.2 %collective-permute-start.6 = (bf16[16,7296]{1,0:T(8,128)(2,1)S(1)}, bf16[16,7296]{1,0:T(8,128)(2,1)S(1)}, u32[]{:S(2)}, u32[]{:S(2)}) collective-permute-start(bf16[16,7296]{1,0:T(8,128)(2,1)S(1)} %collective-permute-done.5.refs_6_), channel_id=1, source_target_pairs={{0,1},{1,0},{2,3},{3,2},{4,5},{5,4},{6,7},{7,6},{8,9},{9,8},{10,11... | collective-permute-start | bytes 700424 | tf_op jit(solution)/shard_map/ppermute | solution.py:197
  25.5 8.4 %collective-permute-start.11 = (bf16[16,7296]{1,0:T(8,128)(2,1)S(1)}, bf16[16,7296]{1,0:T(8,128)(2,1)S(1)}, u32[]{:S(2)}, u32[]{:S(2)}) collective-permute-start(bf16[16,7296]{1,0:T(8,128)(2,1)S(1)} %collective-permute-done.2.refs_4_), channel_id=1, source_target_pairs={{0,8},{8,0},{1,9},{9,1},{2,10},{10,2},{3,11},{11,3},{4,12},{12,4},... | collective-permute-start | bytes 700424 | tf_op jit(solution)/shard_map/ppermute | solution.py:200
  25.5 8.4 %collective-permute-start.10 = (bf16[16,7296]{1,0:T(8,128)(2,1)S(1)}, bf16[16,7296]{1,0:T(8,128)(2,1)S(1)}, u32[]{:S(2)}, u32[]{:S(2)}) collective-permute-start(bf16[16,7296]{1,0:T(8,128)(2,1)S(1)} %collective-permute-done.3.refs_3_), channel_id=1, source_target_pairs={{0,8},{8,0},{1,9},{9,1},{2,10},{10,2},{3,11},{11,3},{4,12},{12,4},... | collective-permute-start | bytes 700424 | tf_op jit(solution)/shard_map/ppermute | solution.py:200
  26.0 7.9 %collective-permute-start.13 = (bf16[16,7296]{1,0:T(8,128)(2,1)S(1)}, bf16[16,7296]{1,0:T(8,128)(2,1)S(1)}, u32[]{:S(2)}, u32[]{:S(2)}) collective-permute-start(bf16[16,7296]{1,0:T(8,128)(2,1)S(1)} %collective-permute-done.5.refs_6_), channel_id=1, source_target_pairs={{0,8},{8,0},{1,9},{9,1},{2,10},{10,2},{3,11},{11,3},{4,12},{12,4},... | collective-permute-start | bytes 700424 | tf_op jit(solution)/shard_map/ppermute | solution.py:200
  30.7 3.2 %collective-permute-start.12 = (bf16[16,7296]{1,0:T(8,128)(2,1)S(1)}, bf16[16,7296]{1,0:T(8,128)(2,1)S(1)}, u32[]{:S(2)}, u32[]{:S(2)}) collective-permute-start(bf16[16,7296]{1,0:T(8,128)(2,1)S(1)} %collective-permute-done.4.refs_5_), channel_id=1, source_target_pairs={{0,8},{8,0},{1,9},{9,1},{2,10},{10,2},{3,11},{11,3},{4,12},{12,4},... | collective-permute-start | bytes 700424 | tf_op jit(solution)/shard_map/ppermute | solution.py:200
  38.8 3.7 %collective-permute-start.19 = (bf16[32,7168]{1,0:T(8,128)(2,1)S(1)}, bf16[32,7168]{1,0:T(8,128)(2,1)S(1)}, u32[]{:S(2)}, u32[]{:S(2)}) collective-permute-start(bf16[32,7168]{1,0:T(8,128)(2,1)S(1)} %get-tuple-element.42), channel_id=1, source_target_pairs={{0,8},{8,0},{1,9},{9,1},{2,10},{10,2},{3,11},{11,3},{4,12},{12,4},... | collective-permute-start | bytes 1376264 | tf_op jit(solution)/shard_map/ppermute | solution.py:200
  39.2 2.1 %collective-permute-start.16 = (bf16[32,7168]{1,0:T(8,128)(2,1)S(1)}, bf16[32,7168]{1,0:T(8,128)(2,1)S(1)}, u32[]{:S(2)}, u32[]{:S(2)}) collective-permute-start(bf16[32,7168]{1,0:T(8,128)(2,1)S(1)} %get-tuple-element.39), channel_id=1, source_target_pairs={{0,8},{8,0},{1,9},{9,1},{2,10},{10,2},{3,11},{11,3},{4,12},{12,4},... | collective-permute-start | bytes 1376264 | tf_op jit(solution)/shard_map/ppermute | solution.py:200
  39.4 3.2 %collective-permute-start.15 = (bf16[32,7168]{1,0:T(8,128)(2,1)S(1)}, bf16[32,7168]{1,0:T(8,128)(2,1)S(1)}, u32[]{:S(2)}, u32[]{:S(2)}) collective-permute-start(bf16[32,7168]{1,0:T(8,128)(2,1)S(1)} %get-tuple-element.37), channel_id=1, source_target_pairs={{0,8},{8,0},{1,9},{9,1},{2,10},{10,2},{3,11},{11,3},{4,12},{12,4},... | collective-permute-start | bytes 1376264 | tf_op jit(solution)/shard_map/ppermute | solution.py:200
  39.8 8.5 %collective-permute-start.21 = (bf16[16,7168]{1,0:T(8,128)(2,1)S(1)}, bf16[16,7168]{1,0:T(8,128)(2,1)S(1)}, u32[]{:S(2)}, u32[]{:S(2)}) collective-permute-start(bf16[16,7168]{1,0:T(8,128)(2,1)S(1)} %add_convert_fusion.4), channel_id=1, source_target_pairs={{0,1},{1,0},{2,3},{3,2},{4,5},{5,4},{6,7},{7,6},{8,9},{9,8},{10,11... | collective-permute-start | bytes 688136 | tf_op jit(solution)/shard_map/ppermute | solution.py:197
  41.4 11.8 %collective-permute-start.17 = (bf16[16,7168]{1,0:T(8,128)(2,1)S(1)}, bf16[16,7168]{1,0:T(8,128)(2,1)S(1)}, u32[]{:S(2)}, u32[]{:S(2)}) collective-permute-start(bf16[16,7168]{1,0:T(8,128)(2,1)S(1)} %add_convert_fusion.6), channel_id=1, source_target_pairs={{0,1},{1,0},{2,3},{3,2},{4,5},{5,4},{6,7},{7,6},{8,9},{9,8},{10,11... | collective-permute-start | bytes 688136 | tf_op jit(solution)/shard_map/ppermute | solution.py:197
  48.3 9.8 %collective-permute-start.22 = (bf16[16,7168]{1,0:T(8,128)(2,1)S(1)}, bf16[16,7168]{1,0:T(8,128)(2,1)S(1)}, u32[]{:S(2)}, u32[]{:S(2)}) collective-permute-start(bf16[16,7168]{1,0:T(8,128)(2,1)S(1)} %add_convert_fusion.5), channel_id=1, source_target_pairs={{0,1},{1,0},{2,3},{3,2},{4,5},{5,4},{6,7},{7,6},{8,9},{9,8},{10,11... | collective-permute-start | bytes 688136 | tf_op jit(solution)/shard_map/ppermute | solution.py:197
  53.2 6.0 %collective-permute-start.24 = (bf16[16,7168]{1,0:T(8,128)(2,1)S(1)}, bf16[16,7168]{1,0:T(8,128)(2,1)S(1)}, u32[]{:S(2)}, u32[]{:S(2)}) collective-permute-start(bf16[16,7168]{1,0:T(8,128)(2,1)S(1)} %add_convert_fusion.2), channel_id=1, source_target_pairs={{0,2},{1,3},{2,0},{3,1},{4,6},{5,7},{6,4},{7,5},{8,10},{9,11},{10,... | collective-permute-start | bytes 688136 | tf_op jit(solution)/shard_map/ppermute | solution.py:197
  53.6 8.7 %collective-permute-start.18 = (bf16[16,7168]{1,0:T(8,128)(2,1)S(1)}, bf16[16,7168]{1,0:T(8,128)(2,1)S(1)}, u32[]{:S(2)}, u32[]{:S(2)}) collective-permute-start(bf16[16,7168]{1,0:T(8,128)(2,1)S(1)} %add_convert_fusion.7), channel_id=1, source_target_pairs={{0,1},{1,0},{2,3},{3,2},{4,5},{5,4},{6,7},{7,6},{8,9},{9,8},{10,11... | collective-permute-start | bytes 688136 | tf_op jit(solution)/shard_map/ppermute | solution.py:197
  58.2 10.4 %collective-permute-start.23 = (bf16[16,7168]{1,0:T(8,128)(2,1)S(1)}, bf16[16,7168]{1,0:T(8,128)(2,1)S(1)}, u32[]{:S(2)}, u32[]{:S(2)}) collective-permute-start(bf16[16,7168]{1,0:T(8,128)(2,1)S(1)} %add_convert_fusion.3), channel_id=1, source_target_pairs={{0,2},{1,3},{2,0},{3,1},{4,6},{5,7},{6,4},{7,5},{8,10},{9,11},{10,... | collective-permute-start | bytes 688136 | tf_op jit(solution)/shard_map/ppermute | solution.py:197
  59.4 11.2 %collective-permute-start.25 = (bf16[16,7168]{1,0:T(8,128)(2,1)S(1)}, bf16[16,7168]{1,0:T(8,128)(2,1)S(1)}, u32[]{:S(2)}, u32[]{:S(2)}) collective-permute-start(bf16[16,7168]{1,0:T(8,128)(2,1)S(1)} %add_convert_fusion.1), channel_id=1, source_target_pairs={{0,4},{1,5},{2,6},{3,7},{4,0},{5,1},{6,2},{7,3},{8,12},{9,13},{10,... | collective-permute-start | bytes 688136 | tf_op jit(solution)/shard_map/ppermute | solution.py:197
  (4 other events, 45.1 us)

commit v3 on v2

--- a/solution.py
+++ b/solution.py
@@ -11,7 +11,7 @@
 HEAD_QK = 192
 SLICES = 4
 LANES = 128
-CALL_ROWS = 256
+CALL_ROWS = 128
 PAIR = 2
 
 
@@ -85,32 +85,40 @@
 
 
 def expert_kernel(count, steps, *refs):
-    blocks, mask = refs[:count], refs[count]
-    gate_w, up_w, down_w = refs[count + 1 : count + 4]
-    outs = refs[count + 4 :]
-    width = outs[0].shape[1]
-    rows = outs[0].shape[0]
+    blocks, masks = refs[:count], refs[count]
+    weights = refs[count + 1 : count + 7]
+    outs = refs[count + 7 :]
+    rows, width = outs[0].shape
     depth = width // steps
+    parts = [pl.ds(k * depth, depth) for k in range(steps)]
 
     def columns(part):
         return jnp.concatenate([b[:, part] for b in blocks], axis=0)
 
     table = columns(pl.ds(width, blocks[0].shape[1] - width)).astype(jnp.float32)
-    scale = jnp.sum(table * mask[...], axis=1, keepdims=True)
-    gate = up = None
-    for k in range(steps):
-        part = pl.ds(k * depth, depth)
+    sums = None
+    for part in parts:
         x = columns(part)
-        g = jnp.dot(x, gate_w[0, part, :], preferred_element_type=jnp.float32)
-        u = jnp.dot(x, up_w[0, part, :], preferred_element_type=jnp.float32)
-        gate, up = (g, u) if gate is None else (gate + g, up + u)
-    act = (jax.nn.silu(gate) * up).astype(jnp.bfloat16)
-    for n in range(steps):
-        part = pl.ds(n * depth, depth)
-        value = scale * jnp.dot(act, down_w[0, :, part], preferred_element_type=jnp.float32)
-        value = value.astype(jnp.bfloat16)
+        new = [
+            jnp.dot(x, weights[i][0, part, :], preferred_element_type=jnp.float32)
+            for i in (0, 1, 3, 4)
+        ]
+        sums = new if sums is None else [a + b for a, b in zip(sums, new, strict=True)]
+    acts, scales = [], []
+    for p in range(2):
+        gate, up = sums[2 * p : 2 * p + 2]
+        acts.append((jax.nn.silu(gate) * up).astype(jnp.bfloat16))
+        scales.append(jnp.sum(table * masks[p : p + 1, :], axis=1, keepdims=True))
+    for part in parts:
+        total = None
+        for p in range(2):
+            value = scales[p] * jnp.dot(
+                acts[p], weights[3 * p + 2][0, :, part], preferred_element_type=jnp.float32
+            )
+            total = value if total is None else total + value
+        total = total.astype(jnp.bfloat16)
         for i, o in enumerate(outs):
-            o[:, part] = value[i * rows : (i + 1) * rows]
+            o[:, part] = total[i * rows : (i + 1) * rows]
 
 
 def stage_kernel(count, *refs):
@@ -141,25 +149,25 @@
     )(*(pltpu.with_memory_space_constraint(a, pltpu.HBM) for a in arrays))
 
 
-def run_experts(blocks, group, mask, weights):
+def run_experts(blocks, masks, weights):
     count = len(blocks)
     rows, packed = blocks[0].shape
     width, hidden = weights[0].shape[1:]
     steps = width // chunk_of(width, 1024)
-    pinned = [pltpu.with_memory_space_constraint(a, pltpu.VMEM) for a in (*blocks, mask, *weights)]
+    operands = [pltpu.with_memory_space_constraint(a, pltpu.VMEM) for a in (*blocks, masks, *weights)]
     return pl.pallas_call(
         functools.partial(expert_kernel, count, steps),
-        out_shape=[pltpu.VMEM((group * rows, width), jnp.bfloat16)] * (count // group),
-        in_specs=[pl.BlockSpec(memory_space=pltpu.VMEM)] * len(pinned),
-        out_specs=[pl.BlockSpec(memory_space=pltpu.VMEM)] * (count // group),
+        out_shape=[pltpu.VMEM((rows, width), jnp.bfloat16)] * count,
+        in_specs=[pl.BlockSpec(memory_space=pltpu.VMEM)] * len(operands),
+        out_specs=[pl.BlockSpec(memory_space=pltpu.VMEM)] * count,
         compiler_params=pltpu.CompilerParams(vmem_limit_bytes=2 * count * rows * packed + (16 << 20)),
         cost_estimate=pl.CostEstimate(
-            flops=2 * count * rows * width * hidden * 3,
-            bytes_accessed=2 * 3 * width * hidden,
+            flops=2 * count * rows * width * hidden * 6,
+            bytes_accessed=2 * 6 * width * hidden,
             transcendentals=0,
         ),
         name="experts",
-    )(*pinned)
+    )(*operands)
 
 
 def attend(queries, latent_cache, lengths):
@@ -199,61 +207,74 @@
     def swap(value):
         return lax.ppermute(value, "node", [(i, i ^ 1) for i in range(nodes)])
 
-    here = (lax.axis_index("node") * devs + lax.axis_index("dev")) // SLICES
-
+    barrier = lax.optimization_barrier
+    dev, node = lax.axis_index("dev"), lax.axis_index("node")
+    experts_here = jnp.stack([n * devs + dev for n in (node, node ^ 1)]) // SLICES
     extra = -(-3 * experts_all // LANES) * LANES
     column = jnp.arange(extra, dtype=jnp.int32)
     named = jnp.where(column < 3 * experts_all, column % experts_all, -1)
-    mask = (named == here).astype(jnp.float32)[None, :]
-    barrier = lax.optimization_barrier
-    tokens, mask = barrier((tokens, mask))
+    masks = (named[None, :] == experts_here[:, None]).astype(jnp.float32)
+    tokens, masks = barrier((tokens, masks))
     packed = pack(tokens, routes, route_weight, experts_all)
-    weights = stage(w_gate, w_up, w_down)
-
-    barrier = lax.optimization_barrier
+
+    w_gate, w_up, packed = barrier((w_gate, w_up, packed))
+    gate_there, up_there = swap(w_gate), swap(w_up)
+    bits = [1 << i for i in reversed(range(lines.bit_length() - 1))]
     gathered, across = {0: packed}, {}
-    bit = lines // 2
-    while bit:
-        for m in list(gathered):
-            gathered[m ^ bit] = hop(gathered[m], bit * PAIR)
-        if bit == lines // 2:
-            gathered[bit], weights = barrier((gathered[bit], weights))
-        bit //= 2
-    for m in range(lines):
-        if m == 2:
-            gathered[m], across[m - 1] = barrier((gathered[m], across[m - 1]))
+    for bit in bits:
+        gathered[bit] = hop(packed, bit * PAIR)
+    across[0] = hop(packed, 1)
+    weights_here = stage(w_gate, w_up, w_down)
+    gathered, across, weights_here, gate_there, up_there = barrier(
+        (gathered, across, weights_here, gate_there, up_there)
+    )
+    w_down, gate_there = barrier((w_down, gate_there))
+    down_there = swap(w_down)
+    into_there = stage(gate_there, up_there)
+    for bit in bits[1:]:
+        for m in sorted(gathered):
+            if m & -m > bit:
+                gathered[m ^ bit] = hop(gathered[m], bit * PAIR)
+    other, far, into_there = barrier((across[0], gathered[lines - 1], into_there))
+    gathered[lines - 1] = far
+    across[1] = hop(other, PAIR)
+    for m in range(2, lines):
         across[m] = hop(gathered[m], 1)
-    keys = [(m, s) for m in range(lines) for s in range(PAIR)]
-    mine = [(gathered, across)[s][m] for m, s in keys]
-    theirs = [swap(x) for x in mine]
+    weights = (*weights_here, *into_there, *stage(down_there))
 
     rows = tokens.shape[0]
-    batch = max(1, CALL_ROWS // (2 * PAIR * rows))
-    kept, sent = [], []
+    batch = max(1, CALL_ROWS // (PAIR * rows))
+    terms = {}
     for first in range(0, lines, batch):
-        cut = slice(PAIR * first, PAIR * (first + batch))
-        sums = run_experts(mine[cut] + theirs[cut], PAIR, mask, weights)
-        kept += sums[: len(sums) // 2]
-        sent += sums[len(sums) // 2 :]
+        cut = [(m, s) for m in range(first, min(lines, first + batch)) for s in range(PAIR)]
+        blocks = [(gathered, across)[s][m] for m, s in cut]
+        for key, value in zip(cut, run_experts(blocks, masks, weights), strict=True):
+            terms[key] = [value]
     context = attend(queries, latent_cache, lengths)
 
-    terms, crossed = {}, {}
+    aside = hop(add_all(*terms.pop((1, 1))), PAIR)
+    before = None
     for m in reversed(range(lines)):
-        met = swap(sent[m])
-        out = add_all(kept[m][rows:], met[rows:])
-        if m + 2 in crossed:
-            out, crossed[m + 2] = barrier((out, crossed[m + 2]))
-        crossed[m] = hop(out, 1)
-        terms[m] = [kept[m][:rows], met[:rows]]
-    for m in range(lines):
-        terms[m].append(crossed[m])
-    bit = 1
-    while bit < lines:
-        for m in sorted(terms, reverse=True):
-            if m & bit:
-                terms[m ^ bit].append(hop(add_all(*terms.pop(m)), bit * PAIR))
-        bit *= 2
-    return add_all(*terms[0]), context
+        if m == 1:
+            continue
+        out = add_all(*terms.pop((m, 1)))
+        if before is not None:
+            out, terms[before, 0][-1] = barrier((out, terms[before, 0][-1]))
+        terms[m, 0].append(hop(out, 1))
+        before = m
+        if m == lines - 1:
+            terms[0, 1].append(aside)
+        elif m == lines - 2:
+            terms[m, 0][-1], terms[0, 1][-1] = barrier((terms[m, 0][-1], terms[0, 1][-1]))
+    for bit in reversed(bits):
+        before = None
+        for m in sorted([m for m, _ in terms if m & bit], reverse=True):
+            out = add_all(*terms.pop((m, 0)))
+            if before is not None:
+                out, terms[before, 0][-1] = barrier((out, terms[before, 0][-1]))
+            terms[m ^ bit, 0].append(hop(out, bit * PAIR))
+            before = m ^ bit
+    return add_all(*terms[0, 0]), context
 
 
 def solution(mesh):

time: 71.6 us -> 64 us (0.89)
  waiting for transfers between devices: 36.6 us -> 21 us
  Pallas kernels: 8.39 us -> 14 us
  local copies, waits for them, and re-layouts: 0.02 us -> 2.6 us
    ppermute x14, waiting for transfers between devices: 35.4 us -> 21 us  [hop(): return lax.ppermute(value, 'dev', [(d, d ^ offset) for d in range(devs)])]
    pallas_call x1 -> x3, Pallas kernels: 4.23 us -> 9.45 us  [stage(): pl.pallas_call(functools.partial(stage_kernel, count), out_shape=[pltpu.V...]
    unnamed x4 -> x12, local copies, waits for them, and re-layouts: 0.02 us -> 2.6 us
    ppermute x14, starting transfers between devices: 19.5 us -> 21.1 us  [hop(): return lax.ppermute(value, 'dev', [(d, d ^ offset) for d in range(devs)])]
    ppermute x12 -> x3, starting transfers between devices: 2.25 us -> 0.67 us  [swap(): return lax.ppermute(value, 'node', [(i, i ^ 1) for i in range(nodes)])]
    ppermute x12 -> x3, waiting for transfers between devices: 1.22 us -> 0.01 us  [swap(): return lax.ppermute(value, 'node', [(i, i ^ 1) for i in range(nodes)])]
  transfers between devices with their start and end apart: 26 -> 17, of which waited for: 14 -> 10; matrix products, arithmetic and copies ran while one was open for 3% -> 3% of each run, Pallas kernels for 6% -> 15%
where the time goes in v3:
time: 64 us; the launch traced here: 63.8 us
  starting transfers between devices  21.8 us (34%)
  waiting for transfers between devices  21 us (33%)
  Pallas kernels  14 us (22%)
  local copies, waits for them, and re-layouts  2.6 us (4%)
  matrix products  1.65 us (3%)
  between operations  1.46 us (2%)
  other arithmetic  1.4 us (2%)
    ppermute x14, starting transfers between devices, hop(): return lax.ppermute(value, 'dev', [(d, d ^ offset) for d in range(devs)])  21.1 us
    ppermute x14, waiting for transfers between devices, hop(): return lax.ppermute(value, 'dev', [(d, d ^ offset) for d in range(devs)])  21 us
    pallas_call x3, Pallas kernels, stage(): pl.pallas_call(functools.partial(stage_kernel, count), out_shape=[pltpu.V...  9.45 us
    pallas_call x1, Pallas kernels, run_experts(): pl.pallas_call(functools.partial(expert_kernel, count, steps), out_shape=...  3.54 us
    unnamed x12, local copies, waits for them, and re-layouts  2.6 us
  transfers between devices with their start and end apart: 17, of which 10 were waited for; matrix products, arithmetic and copies ran while one was open for 3% of the time, Pallas kernels for 15%

profile of v3, /device:TPU:0, one launch (start us, length us, event | category | flops | bytes accessed | tf_op | source)
XLA Modules:
  0.0 63.8 jit_solution(4667442218476410422)
XLA Ops:
  0.8 1.0 %pack.1.refs_0_ = bf16[16,7296]{1,0:T(8,128)(2,1)S(1)} custom-call(s32[2,16]{1,0:T(2,128)} %bitcast.21, f32[2,16]{1,0:T(2,128)} %bitcast.22, bf16[16,7168]{1,0:T(8,128)(2,1)} %tokens_hbm), custom_call_target="tpu_custom_call" | custom-call | tf_op jit(solution)/shard_map/pack/pallas_call | solution.py:72
  2.4 3.0 %collective-permute-start = (bf16[16,7296]{1,0:T(8,128)(2,1)S(1)}, bf16[16,7296]{1,0:T(8,128)(2,1)S(1)}, u32[]{:S(2)}, u32[]{:S(2)}) collective-permute-start(bf16[16,7296]{1,0:T(8,128)(2,1)S(1)} %pack.1.refs_0_), channel_id=1, source_target_pairs={{0,2},{1,3},{2,0},{3,1},{4,6},{5,7},{6,4},{7,5},{8,10},{9,11},{10,... | collective-permute-start | bytes 700424 | tf_op jit(solution)/shard_map/ppermute | solution.py:205
  5.4 2.6 %collective-permute-start.1 = (bf16[16,7296]{1,0:T(8,128)(2,1)S(1)}, bf16[16,7296]{1,0:T(8,128)(2,1)S(1)}, u32[]{:S(2)}, u32[]{:S(2)}) collective-permute-start(bf16[16,7296]{1,0:T(8,128)(2,1)S(1)} %pack.1.refs_0_), channel_id=1, source_target_pairs={{0,4},{1,5},{2,6},{3,7},{4,0},{5,1},{6,2},{7,3},{8,12},{9,13},{10,... | collective-permute-start | bytes 700424 | tf_op jit(solution)/shard_map/ppermute | solution.py:205
  8.0 1.5 %collective-permute-start.2 = (bf16[16,7296]{1,0:T(8,128)(2,1)S(1)}, bf16[16,7296]{1,0:T(8,128)(2,1)S(1)}, u32[]{:S(2)}, u32[]{:S(2)}) collective-permute-start(bf16[16,7296]{1,0:T(8,128)(2,1)S(1)} %pack.1.refs_0_), channel_id=1, source_target_pairs={{0,1},{1,0},{2,3},{3,2},{4,5},{5,4},{6,7},{7,6},{8,9},{9,8},{10,11... | collective-permute-start | bytes 700424 | tf_op jit(solution)/shard_map/ppermute | solution.py:205
  9.5 4.2 %stage.3 = (bf16[1,7168,256]{2,1,0:T(8,128)(2,1)S(1)}, bf16[1,7168,256]{2,1,0:T(8,128)(2,1)S(1)}, bf16[1,256,7168]{2,1,0:T(8,128)(2,1)S(1)}) custom-call(bf16[1,7168,256]{2,1,0:T(8,128)(2,1)} %refs_0_, bf16[1,7168,256]{2,1,0:T(8,128)(2,1)} %refs_1_, bf16[1,256,7168]{2,1,0:T(8,128)(2,1)} %refs_2_.1), custom_call_target="tpu_custom_call" | custom-call | bytes 11010048 | tf_op jit(solution)/shard_map/stage/pallas_call | solution.py:138
  13.8 2.5 %collective-permute-done.refs_2_ = bf16[16,7296]{1,0:T(8,128)(2,1)S(1)} collective-permute-done((bf16[16,7296]{1,0:T(8,128)(2,1)S(1)}, bf16[16,7296]{1,0:T(8,128)(2,1)S(1)}, u32[]{:S(2)}, u32[]{:S(2)}) %collective-permute-start) | collective-permute-done | bytes 233504 | tf_op jit(solution)/shard_map/ppermute | solution.py:205
  16.2 2.5 %collective-permute-done.1.refs_4_ = bf16[16,7296]{1,0:T(8,128)(2,1)S(1)} collective-permute-done((bf16[16,7296]{1,0:T(8,128)(2,1)S(1)}, bf16[16,7296]{1,0:T(8,128)(2,1)S(1)}, u32[]{:S(2)}, u32[]{:S(2)}) %collective-permute-start.1) | collective-permute-done | bytes 233504 | tf_op jit(solution)/shard_map/ppermute | solution.py:205
  19.4 1.5 %collective-permute-start.7 = (bf16[16,7296]{1,0:T(8,128)(2,1)S(1)}, bf16[16,7296]{1,0:T(8,128)(2,1)S(1)}, u32[]{:S(2)}, u32[]{:S(2)}) collective-permute-start(bf16[16,7296]{1,0:T(8,128)(2,1)S(1)} %collective-permute-done.1.refs_4_), channel_id=1, source_target_pairs={{0,1},{1,0},{2,3},{3,2},{4,5},{5,4},{6,7},{7,6},{8,9},{9,8},{10,11... | collective-permute-start | bytes 700424 | tf_op jit(solution)/shard_map/ppermute | solution.py:205
  21.7 3.2 %stage.4 = (bf16[1,7168,256]{2,1,0:T(8,128)(2,1)S(1)}, bf16[1,7168,256]{2,1,0:T(8,128)(2,1)S(1)}) custom-call(bf16[1,7168,256]{2,1,0:T(8,128)(2,1)} %copy-done.1, bf16[1,7168,256]{2,1,0:T(8,128)(2,1)} %copy-done.2), custom_call_target="tpu_custom_call" | custom-call | bytes 7340032 | tf_op jit(solution)/shard_map/stage/pallas_call | solution.py:138
  24.9 2.1 %collective-permute-done.5.refs_6_ = bf16[16,7296]{1,0:T(8,128)(2,1)S(1)} collective-permute-done((bf16[16,7296]{1,0:T(8,128)(2,1)S(1)}, bf16[16,7296]{1,0:T(8,128)(2,1)S(1)}, u32[]{:S(2)}, u32[]{:S(2)}) %collective-permute-start.5) | collective-permute-done | bytes 233504 | tf_op jit(solution)/shard_map/ppermute | solution.py:205
  27.4 1.5 %collective-permute-start.8 = (bf16[16,7296]{1,0:T(8,128)(2,1)S(1)}, bf16[16,7296]{1,0:T(8,128)(2,1)S(1)}, u32[]{:S(2)}, u32[]{:S(2)}) collective-permute-start(bf16[16,7296]{1,0:T(8,128)(2,1)S(1)} %collective-permute-done.5.refs_6_), channel_id=1, source_target_pairs={{0,1},{1,0},{2,3},{3,2},{4,5},{5,4},{6,7},{7,6},{8,9},{9,8},{10,11... | collective-permute-start | bytes 700424 | tf_op jit(solution)/shard_map/ppermute | solution.py:205
  29.6 1.8 %copy-done.3 = bf16[1,256,7168]{2,1,0:T(8,128)(2,1)} copy-done((bf16[1,256,7168]{2,1,0:T(8,128)(2,1)}, bf16[1,256,7168]{2,1,0:T(8,128)(2,1)S(1)}, u32[]{:S(2)}) %copy-start.3) | copy-done | bytes 3670040
  31.4 2.0 %stage.5.refs_14_ = bf16[1,256,7168]{2,1,0:T(8,128)(2,1)S(1)} custom-call(bf16[1,256,7168]{2,1,0:T(8,128)(2,1)} %copy-done.3), custom_call_target="tpu_custom_call" | custom-call | bytes 3670016 | tf_op jit(solution)/shard_map/stage/pallas_call | solution.py:138
  34.4 3.5 %experts.1 = (bf16[16,7168]{1,0:T(8,128)(2,1)S(1)}, bf16[16,7168]{1,0:T(8,128)(2,1)S(1)}, bf16[16,7168]{1,0:T(8,128)(2,1)S(1)}, bf16[16,7168]{1,0:T(8,128)(2,1)S...) custom-call(bf16[16,7296]{1,0:T(8,128)(2,1)S(1)} %pack.1.refs_0_, ...), custom_call_target="tpu_custom_call" | custom-call | flops 2818572288 | bytes 22020096 | tf_op jit(solution)/shard_map/experts/pallas_call | solution.py:158
  38.0 1.6 %collective-permute-start.10 = (bf16[16,7168]{1,0:T(8,128)(2,1)S(1)}, bf16[16,7168]{1,0:T(8,128)(2,1)S(1)}, u32[]{:S(2)}, u32[]{:S(2)}) collective-permute-start(bf16[16,7168]{1,0:T(8,128)(2,1)S(1)} %get-tuple-element.71), channel_id=1, source_target_pairs={{0,1},{1,0},{2,3},{3,2},{4,5},{5,4},{6,7},{7,6},{8,9},{9,8},{10,11... | collective-permute-start | bytes 688136 | tf_op jit(solution)/shard_map/ppermute | solution.py:205
  40.3 1.6 %collective-permute-start.12 = (bf16[16,7168]{1,0:T(8,128)(2,1)S(1)}, bf16[16,7168]{1,0:T(8,128)(2,1)S(1)}, u32[]{:S(2)}, u32[]{:S(2)}) collective-permute-start(bf16[16,7168]{1,0:T(8,128)(2,1)S(1)} %get-tuple-element.73), channel_id=1, source_target_pairs={{0,2},{1,3},{2,0},{3,1},{4,6},{5,7},{6,4},{7,5},{8,10},{9,11},{10,... | collective-permute-start | bytes 688136 | tf_op jit(solution)/shard_map/ppermute | solution.py:205
  41.9 2.2 %collective-permute-done.10 = bf16[16,7168]{1,0:T(8,128)(2,1)S(1)} collective-permute-done((bf16[16,7168]{1,0:T(8,128)(2,1)S(1)}, bf16[16,7168]{1,0:T(8,128)(2,1)S(1)}, u32[]{:S(2)}, u32[]{:S(2)}) %collective-permute-start.10) | collective-permute-done | bytes 229408 | tf_op jit(solution)/shard_map/ppermute | solution.py:205
  44.1 1.5 %collective-permute-start.11 = (bf16[16,7168]{1,0:T(8,128)(2,1)S(1)}, bf16[16,7168]{1,0:T(8,128)(2,1)S(1)}, u32[]{:S(2)}, u32[]{:S(2)}) collective-permute-start(bf16[16,7168]{1,0:T(8,128)(2,1)S(1)} %get-tuple-element.72), channel_id=1, source_target_pairs={{0,1},{1,0},{2,3},{3,2},{4,5},{5,4},{6,7},{7,6},{8,9},{9,8},{10,11... | collective-permute-start | bytes 688136 | tf_op jit(solution)/shard_map/ppermute | solution.py:205
  45.7 1.6 %collective-permute-start.14 = (bf16[16,7168]{1,0:T(8,128)(2,1)S(1)}, bf16[16,7168]{1,0:T(8,128)(2,1)S(1)}, u32[]{:S(2)}, u32[]{:S(2)}) collective-permute-start(bf16[16,7168]{1,0:T(8,128)(2,1)S(1)} %add_convert_fusion.2), channel_id=1, source_target_pairs={{0,2},{1,3},{2,0},{3,1},{4,6},{5,7},{6,4},{7,5},{8,10},{9,11},{10,... | collective-permute-start | bytes 688136 | tf_op jit(solution)/shard_map/ppermute | solution.py:205
  47.3 2.8 %collective-permute-done.11 = bf16[16,7168]{1,0:T(8,128)(2,1)S(1)} collective-permute-done((bf16[16,7168]{1,0:T(8,128)(2,1)S(1)}, bf16[16,7168]{1,0:T(8,128)(2,1)S(1)}, u32[]{:S(2)}, u32[]{:S(2)}) %collective-permute-start.11) | collective-permute-done | bytes 229408 | tf_op jit(solution)/shard_map/ppermute | solution.py:205
  50.2 1.6 %collective-permute-done.14 = bf16[16,7168]{1,0:T(8,128)(2,1)S(1)} collective-permute-done((bf16[16,7168]{1,0:T(8,128)(2,1)S(1)}, bf16[16,7168]{1,0:T(8,128)(2,1)S(1)}, u32[]{:S(2)}, u32[]{:S(2)}) %collective-permute-start.14) | collective-permute-done | bytes 229408 | tf_op jit(solution)/shard_map/ppermute | solution.py:205
  51.9 2.7 %collective-permute-start.16 = (bf16[16,7168]{1,0:T(8,128)(2,1)S(1)}, bf16[16,7168]{1,0:T(8,128)(2,1)S(1)}, u32[]{:S(2)}, u32[]{:S(2)}) collective-permute-start(bf16[16,7168]{1,0:T(8,128)(2,1)S(1)} %add_convert_fusion.1), channel_id=1, source_target_pairs={{0,4},{1,5},{2,6},{3,7},{4,0},{5,1},{6,2},{7,3},{8,12},{9,13},{10,... | collective-permute-start | bytes 688136 | tf_op jit(solution)/shard_map/ppermute | solution.py:205
  55.6 1.2 %fusion.2 = bf16[1,128,512]{2,1,0:T(8,128)(2,1)} fusion(bf16[1,1024,576]{1,2,0:T(8,128)(2,1)S(1)} %copy-done.5, f32[128,1024]{1,0:T(8,128)S(1)} %get-tuple-element.85, f32[128]{0:T(128)S(1)} %fusion.5, f32[128]{0:T(128)S(1)} %get-tuple-element.84), kind=kOutput, calls=%fused_computation.4 | convolution fusion | flops 134676480 | bytes 1704960 | tf_op jit(solution)/shard_map/rhl,rlk->rhk/dot_general | solution.py:186
  56.7 5.8 %collective-permute-done.16 = bf16[16,7168]{1,0:T(8,128)(2,1)S(1)} collective-permute-done((bf16[16,7168]{1,0:T(8,128)(2,1)S(1)}, bf16[16,7168]{1,0:T(8,128)(2,1)S(1)}, u32[]{:S(2)}, u32[]{:S(2)}) %collective-permute-start.16) | collective-permute-done | bytes 229408 | tf_op jit(solution)/shard_map/ppermute | solution.py:205
  (38 shorter events, 6.7 us)
Async XLA Ops:
  0.6 38.9 %copy-start = (bf16[1,128,576]{1,2,0:T(8,128)(2,1)S(1)}, bf16[1,128,576]{1,2,0:T(8,128)(2,1)}, u32[]{:S(2)}) copy-start(bf16[1,128,576]{1,2,0:T(8,128)(2,1)} %param.15) | copy-start | bytes 442372
  1.8 17.0 %copy-start.4 = (bf16[1,256,7168]{2,1,0:T(8,128)(2,1)S(1)}, bf16[1,256,7168]{2,1,0:T(8,128)(2,1)}, u32[]{:S(2)}) copy-start(bf16[1,256,7168]{2,1,0:T(8,128)(2,1)} %refs_2_.1) | copy-start | bytes 11010052
  1.8 17.0 %collective-permute-start.3 = (bf16[1,7168,256]{2,1,0:T(8,128)(2,1)}, bf16[1,7168,256]{2,1,0:T(8,128)(2,1)S(1)}, u32[]{:S(2)}, u32[]{:S(2)}) collective-permute-start(bf16[1,7168,256]{2,1,0:T(8,128)(2,1)} %refs_0_), channel_id=1, source_target_pairs={{0,8},{8,0},{1,9},{9,1},{2,10},{10,2},{3,11},{11,3},{4,12},{12,4},... | collective-permute-start | bytes 11010056 | tf_op jit(solution)/shard_map/ppermute | solution.py:208
  2.3 16.4 %collective-permute-start.4 = (bf16[1,7168,256]{2,1,0:T(8,128)(2,1)}, bf16[1,7168,256]{2,1,0:T(8,128)(2,1)S(1)}, u32[]{:S(2)}, u32[]{:S(2)}) collective-permute-start(bf16[1,7168,256]{2,1,0:T(8,128)(2,1)} %refs_1_), channel_id=1, source_target_pairs={{0,8},{8,0},{1,9},{9,1},{2,10},{10,2},{3,11},{11,3},{4,12},{12,4},... | collective-permute-start | bytes 11010056 | tf_op jit(solution)/shard_map/ppermute | solution.py:208
  2.4 13.8 %collective-permute-start = (bf16[16,7296]{1,0:T(8,128)(2,1)S(1)}, bf16[16,7296]{1,0:T(8,128)(2,1)S(1)}, u32[]{:S(2)}, u32[]{:S(2)}) collective-permute-start(bf16[16,7296]{1,0:T(8,128)(2,1)S(1)} %pack.1.refs_0_), channel_id=1, source_target_pairs={{0,2},{1,3},{2,0},{3,1},{4,6},{5,7},{6,4},{7,5},{8,10},{9,11},{10,... | collective-permute-start | bytes 700424 | tf_op jit(solution)/shard_map/ppermute | solution.py:205
  5.4 13.3 %collective-permute-start.1 = (bf16[16,7296]{1,0:T(8,128)(2,1)S(1)}, bf16[16,7296]{1,0:T(8,128)(2,1)S(1)}, u32[]{:S(2)}, u32[]{:S(2)}) collective-permute-start(bf16[16,7296]{1,0:T(8,128)(2,1)S(1)} %pack.1.refs_0_), channel_id=1, source_target_pairs={{0,4},{1,5},{2,6},{3,7},{4,0},{5,1},{6,2},{7,3},{8,12},{9,13},{10,... | collective-permute-start | bytes 700424 | tf_op jit(solution)/shard_map/ppermute | solution.py:205
  8.0 10.8 %collective-permute-start.2 = (bf16[16,7296]{1,0:T(8,128)(2,1)S(1)}, bf16[16,7296]{1,0:T(8,128)(2,1)S(1)}, u32[]{:S(2)}, u32[]{:S(2)}) collective-permute-start(bf16[16,7296]{1,0:T(8,128)(2,1)S(1)} %pack.1.refs_0_), channel_id=1, source_target_pairs={{0,1},{1,0},{2,3},{3,2},{4,5},{5,4},{6,7},{7,6},{8,9},{9,8},{10,11... | collective-permute-start | bytes 700424 | tf_op jit(solution)/shard_map/ppermute | solution.py:205
  18.8 2.2 %copy-start.1 = (bf16[1,7168,256]{2,1,0:T(8,128)(2,1)}, bf16[1,7168,256]{2,1,0:T(8,128)(2,1)S(1)}, u32[]{:S(2)}) copy-start(bf16[1,7168,256]{2,1,0:T(8,128)(2,1)S(1)} %collective-permute-done.3.refs_0_) | copy-start | bytes 11010052
  18.8 2.9 %copy-start.2 = (bf16[1,7168,256]{2,1,0:T(8,128)(2,1)}, bf16[1,7168,256]{2,1,0:T(8,128)(2,1)S(1)}, u32[]{:S(2)}) copy-start(bf16[1,7168,256]{2,1,0:T(8,128)(2,1)S(1)} %collective-permute-done.4.refs_1_) | copy-start | bytes 11010052
  18.8 10.8 %collective-permute-start.9 = (bf16[1,256,7168]{2,1,0:T(8,128)(2,1)S(1)}, bf16[1,256,7168]{2,1,0:T(8,128)(2,1)S(1)}, u32[]{:S(2)}, u32[]{:S(2)}) collective-permute-start(bf16[1,256,7168]{2,1,0:T(8,128)(2,1)S(1)} %copy-done.4), channel_id=1, source_target_pairs={{0,8},{8,0},{1,9},{9,1},{2,10},{10,2},{3,11},{11,3},{4,12},{12,4},... | collective-permute-start | bytes 11010056 | tf_op jit(solution)/shard_map/ppermute | solution.py:208
  18.9 8.1 %collective-permute-start.5 = (bf16[16,7296]{1,0:T(8,128)(2,1)S(1)}, bf16[16,7296]{1,0:T(8,128)(2,1)S(1)}, u32[]{:S(2)}, u32[]{:S(2)}) collective-permute-start(bf16[16,7296]{1,0:T(8,128)(2,1)S(1)} %collective-permute-done.1.refs_4_), channel_id=1, source_target_pairs={{0,2},{1,3},{2,0},{3,1},{4,6},{5,7},{6,4},{7,5},{8,10},{9,11},{10,... | collective-permute-start | bytes 700424 | tf_op jit(solution)/shard_map/ppermute | solution.py:205
  19.4 14.1 %collective-permute-start.7 = (bf16[16,7296]{1,0:T(8,128)(2,1)S(1)}, bf16[16,7296]{1,0:T(8,128)(2,1)S(1)}, u32[]{:S(2)}, u32[]{:S(2)}) collective-permute-start(bf16[16,7296]{1,0:T(8,128)(2,1)S(1)} %collective-permute-done.1.refs_4_), channel_id=1, source_target_pairs={{0,1},{1,0},{2,3},{3,2},{4,5},{5,4},{6,7},{7,6},{8,9},{9,8},{10,11... | collective-permute-start | bytes 700424 | tf_op jit(solution)/shard_map/ppermute | solution.py:205
  27.0 7.3 %collective-permute-start.6 = (bf16[16,7296]{1,0:T(8,128)(2,1)S(1)}, bf16[16,7296]{1,0:T(8,128)(2,1)S(1)}, u32[]{:S(2)}, u32[]{:S(2)}) collective-permute-start(bf16[16,7296]{1,0:T(8,128)(2,1)S(1)} %collective-permute-done.2.refs_1_), channel_id=1, source_target_pairs={{0,2},{1,3},{2,0},{3,1},{4,6},{5,7},{6,4},{7,5},{8,10},{9,11},{10,... | collective-permute-start | bytes 700424 | tf_op jit(solution)/shard_map/ppermute | solution.py:205
  27.4 7.0 %collective-permute-start.8 = (bf16[16,7296]{1,0:T(8,128)(2,1)S(1)}, bf16[16,7296]{1,0:T(8,128)(2,1)S(1)}, u32[]{:S(2)}, u32[]{:S(2)}) collective-permute-start(bf16[16,7296]{1,0:T(8,128)(2,1)S(1)} %collective-permute-done.5.refs_6_), channel_id=1, source_target_pairs={{0,1},{1,0},{2,3},{3,2},{4,5},{5,4},{6,7},{7,6},{8,9},{9,8},{10,11... | collective-permute-start | bytes 700424 | tf_op jit(solution)/shard_map/ppermute | solution.py:205
  29.6 1.8 %copy-start.3 = (bf16[1,256,7168]{2,1,0:T(8,128)(2,1)}, bf16[1,256,7168]{2,1,0:T(8,128)(2,1)S(1)}, u32[]{:S(2)}) copy-start(bf16[1,256,7168]{2,1,0:T(8,128)(2,1)S(1)} %collective-permute-done.9.refs_0_) | copy-start | bytes 11010052
  33.5 6.1 %copy-start.5 = (bf16[1,1024,576]{1,2,0:T(8,128)(2,1)S(1)}, bf16[1,1024,576]{1,2,0:T(8,128)(2,1)}, u32[]{:S(2)}) copy-start(bf16[1,1024,576]{1,2,0:T(8,128)(2,1)} %param.16) | copy-start | bytes 3538948
  38.0 6.2 %collective-permute-start.10 = (bf16[16,7168]{1,0:T(8,128)(2,1)S(1)}, bf16[16,7168]{1,0:T(8,128)(2,1)S(1)}, u32[]{:S(2)}, u32[]{:S(2)}) collective-permute-start(bf16[16,7168]{1,0:T(8,128)(2,1)S(1)} %get-tuple-element.71), channel_id=1, source_target_pairs={{0,1},{1,0},{2,3},{3,2},{4,5},{5,4},{6,7},{7,6},{8,9},{9,8},{10,11... | collective-permute-start | bytes 688136 | tf_op jit(solution)/shard_map/ppermute | solution.py:205
  40.3 7.0 %collective-permute-start.12 = (bf16[16,7168]{1,0:T(8,128)(2,1)S(1)}, bf16[16,7168]{1,0:T(8,128)(2,1)S(1)}, u32[]{:S(2)}, u32[]{:S(2)}) collective-permute-start(bf16[16,7168]{1,0:T(8,128)(2,1)S(1)} %get-tuple-element.73), channel_id=1, source_target_pairs={{0,2},{1,3},{2,0},{3,1},{4,6},{5,7},{6,4},{7,5},{8,10},{9,11},{10,... | collective-permute-start | bytes 688136 | tf_op jit(solution)/shard_map/ppermute | solution.py:205
  44.1 6.0 %collective-permute-start.11 = (bf16[16,7168]{1,0:T(8,128)(2,1)S(1)}, bf16[16,7168]{1,0:T(8,128)(2,1)S(1)}, u32[]{:S(2)}, u32[]{:S(2)}) collective-permute-start(bf16[16,7168]{1,0:T(8,128)(2,1)S(1)} %get-tuple-element.72), channel_id=1, source_target_pairs={{0,1},{1,0},{2,3},{3,2},{4,5},{5,4},{6,7},{7,6},{8,9},{9,8},{10,11... | collective-permute-start | bytes 688136 | tf_op jit(solution)/shard_map/ppermute | solution.py:205
  45.7 6.1 %collective-permute-start.14 = (bf16[16,7168]{1,0:T(8,128)(2,1)S(1)}, bf16[16,7168]{1,0:T(8,128)(2,1)S(1)}, u32[]{:S(2)}, u32[]{:S(2)}) collective-permute-start(bf16[16,7168]{1,0:T(8,128)(2,1)S(1)} %add_convert_fusion.2), channel_id=1, source_target_pairs={{0,2},{1,3},{2,0},{3,1},{4,6},{5,7},{6,4},{7,5},{8,10},{9,11},{10,... | collective-permute-start | bytes 688136 | tf_op jit(solution)/shard_map/ppermute | solution.py:205
  51.9 10.7 %collective-permute-start.16 = (bf16[16,7168]{1,0:T(8,128)(2,1)S(1)}, bf16[16,7168]{1,0:T(8,128)(2,1)S(1)}, u32[]{:S(2)}, u32[]{:S(2)}) collective-permute-start(bf16[16,7168]{1,0:T(8,128)(2,1)S(1)} %add_convert_fusion.1), channel_id=1, source_target_pairs={{0,4},{1,5},{2,6},{3,7},{4,0},{5,1},{6,2},{7,3},{8,12},{9,13},{10,... | collective-permute-start | bytes 688136 | tf_op jit(solution)/shard_map/ppermute | solution.py:205
  54.6 8.0 %collective-permute-start.13 = (bf16[16,7168]{1,0:T(8,128)(2,1)S(1)}, bf16[16,7168]{1,0:T(8,128)(2,1)S(1)}, u32[]{:S(2)}, u32[]{:S(2)}) collective-permute-start(bf16[16,7168]{1,0:T(8,128)(2,1)S(1)} %add_convert_fusion.3), channel_id=1, source_target_pairs={{0,1},{1,0},{2,3},{3,2},{4,5},{5,4},{6,7},{7,6},{8,9},{9,8},{10,11... | collective-permute-start | bytes 688136 | tf_op jit(solution)/shard_map/ppermute | solution.py:205
  55.1 8.0 %collective-permute-start.15 = (bf16[16,7168]{1,0:T(8,128)(2,1)S(1)}, bf16[16,7168]{1,0:T(8,128)(2,1)S(1)}, u32[]{:S(2)}, u32[]{:S(2)}) collective-permute-start(bf16[16,7168]{1,0:T(8,128)(2,1)S(1)} %get-tuple-element.80), channel_id=1, source_target_pairs={{0,2},{1,3},{2,0},{3,1},{4,6},{5,7},{6,4},{7,5},{8,10},{9,11},{10,... | collective-permute-start | bytes 688136 | tf_op jit(solution)/shard_map/ppermute | solution.py:205

commit v4 on v3

--- a/solution.py
+++ b/solution.py
@@ -170,7 +170,7 @@
     )(*operands)
 
 
-def attend(queries, latent_cache, lengths):
+def probabilities(queries, latent_cache, lengths):
     score_scale = HEAD_QK ** (-0.5)
     scores = (
         jnp.einsum("rhk,rlk->rhl", queries, latent_cache, preferred_element_type=jnp.float32)
@@ -182,9 +182,12 @@
     row_max = jnp.max(scores, axis=-1, keepdims=True)
     expo = jnp.exp(scores - row_max)
     row_sum = jnp.sum(expo, axis=-1, keepdims=True)
-    weights_bf = (expo / row_sum).astype(jnp.bfloat16)
+    return (expo / row_sum).astype(jnp.bfloat16)
+
+
+def attend(probs, latent_cache):
     context = jnp.einsum(
-        "rhl,rlk->rhk", weights_bf, latent_cache[:, :, :LAT], preferred_element_type=jnp.float32
+        "rhl,rlk->rhk", probs, latent_cache[:, :, :LAT], preferred_element_type=jnp.float32
     )
     return context.astype(jnp.bfloat16)
 
@@ -222,11 +225,11 @@
     bits = [1 << i for i in reversed(range(lines.bit_length() - 1))]
     gathered, across = {0: packed}, {}
     for bit in bits:
-        gathered[bit] = hop(packed, bit * PAIR)
+        gathered[bit] = hop(packed, (2 * bit - 1) * PAIR)
     across[0] = hop(packed, 1)
     weights_here = stage(w_gate, w_up, w_down)
-    gathered, across, weights_here, gate_there, up_there = barrier(
-        (gathered, across, weights_here, gate_there, up_there)
+    gathered, across, weights_here, gate_there = barrier(
+        (gathered, across, weights_here, gate_there)
     )
     w_down, gate_there = barrier((w_down, gate_there))
     down_there = swap(w_down)
@@ -234,7 +237,7 @@
     for bit in bits[1:]:
         for m in sorted(gathered):
             if m & -m > bit:
-                gathered[m ^ bit] = hop(gathered[m], bit * PAIR)
+                gathered[m ^ bit] = hop(gathered[m], (2 * bit - 1) * PAIR)
     other, far, into_there = barrier((across[0], gathered[lines - 1], into_there))
     gathered[lines - 1] = far
     across[1] = hop(other, PAIR)
@@ -250,7 +253,7 @@
         blocks = [(gathered, across)[s][m] for m, s in cut]
         for key, value in zip(cut, run_experts(blocks, masks, weights), strict=True):
             terms[key] = [value]
-    context = attend(queries, latent_cache, lengths)
+    probs = probabilities(queries, latent_cache, lengths)
 
     aside = hop(add_all(*terms.pop((1, 1))), PAIR)
     before = None
@@ -272,9 +275,11 @@
             out = add_all(*terms.pop((m, 0)))
             if before is not None:
                 out, terms[before, 0][-1] = barrier((out, terms[before, 0][-1]))
-            terms[m ^ bit, 0].append(hop(out, bit * PAIR))
+            terms[m ^ bit, 0].append(hop(out, (2 * bit - 1) * PAIR))
             before = m ^ bit
-    return add_all(*terms[0, 0]), context
+        if bit == 1:
+            probs, terms[0, 0][-1] = barrier((probs, terms[0, 0][-1]))
+    return add_all(*terms[0, 0]), attend(probs, latent_cache)
 
 
 def solution(mesh):

time: 64 us -> 63.4 us (level)
  local copies, waits for them, and re-layouts: 2.6 us -> 3.66 us
  starting transfers between devices: 21.8 us -> 20.9 us
  waiting for transfers between devices: 21 us -> 20.1 us
    unnamed x12, local copies, waits for them, and re-layouts: 2.6 us -> 3.66 us
    ppermute x14, waiting for transfers between devices: 21 us -> 20.1 us  [hop(): return lax.ppermute(value, 'dev', [(d, d ^ offset) for d in range(devs)])]
    ppermute x14, starting transfers between devices: 21.1 us -> 20.3 us  [hop(): return lax.ppermute(value, 'dev', [(d, d ^ offset) for d in range(devs)])]
  transfers between devices with their start and end apart: 17 -> 17, of which waited for: 10 -> 8; matrix products, arithmetic and copies ran while one was open for 3% -> 4% of each run, Pallas kernels for 15% -> 15%
where the time goes in v4:
time: 63.4 us; the launch traced here: 63.3 us
  starting transfers between devices  20.9 us (33%)
  waiting for transfers between devices  20.1 us (32%)
  Pallas kernels  14 us (22%)
  local copies, waits for them, and re-layouts  3.66 us (6%)
  matrix products  1.62 us (3%)
  other arithmetic  1.58 us (2%)
  between operations  1.45 us (2%)
    ppermute x14, starting transfers between devices, hop(): return lax.ppermute(value, 'dev', [(d, d ^ offset) for d in range(devs)])  20.3 us
    ppermute x14, waiting for transfers between devices, hop(): return lax.ppermute(value, 'dev', [(d, d ^ offset) for d in range(devs)])  20.1 us
    pallas_call x3, Pallas kernels, stage(): pl.pallas_call(functools.partial(stage_kernel, count), out_shape=[pltpu.V...  9.45 us
    unnamed x12, local copies, waits for them, and re-layouts  3.66 us
    pallas_call x1, Pallas kernels, run_experts(): pl.pallas_call(functools.partial(expert_kernel, count, steps), out_shape=...  3.54 us
  transfers between devices with their start and end apart: 17, of which 8 were waited for; matrix products, arithmetic and copies ran while one was open for 4% of the time, Pallas kernels for 15%

profile of v4, /device:TPU:0, one launch (start us, length us, event | category | flops | bytes accessed | tf_op | source)
XLA Modules:
  0.0 63.3 jit_solution(5191740951544122374)
XLA Ops:
  2.3 2.7 %collective-permute-start = (bf16[16,7296]{1,0:T(8,128)(2,1)S(1)}, bf16[16,7296]{1,0:T(8,128)(2,1)S(1)}, u32[]{:S(2)}, u32[]{:S(2)}) collective-permute-start(bf16[16,7296]{1,0:T(8,128)(2,1)S(1)} %pack.1.refs_0_), channel_id=1, source_target_pairs={{0,2},{1,3},{2,0},{3,1},{4,6},{5,7},{6,4},{7,5},{8,10},{9,11},{10,... | collective-permute-start | bytes 700424 | tf_op jit(solution)/shard_map/ppermute | solution.py:208
  5.0 2.5 %collective-permute-start.1 = (bf16[16,7296]{1,0:T(8,128)(2,1)S(1)}, bf16[16,7296]{1,0:T(8,128)(2,1)S(1)}, u32[]{:S(2)}, u32[]{:S(2)}) collective-permute-start(bf16[16,7296]{1,0:T(8,128)(2,1)S(1)} %pack.1.refs_0_), channel_id=1, source_target_pairs={{0,6},{1,7},{2,4},{3,5},{4,2},{5,3},{6,0},{7,1},{8,14},{9,15},{10,... | collective-permute-start | bytes 700424 | tf_op jit(solution)/shard_map/ppermute | solution.py:208
  7.5 1.5 %collective-permute-start.2 = (bf16[16,7296]{1,0:T(8,128)(2,1)S(1)}, bf16[16,7296]{1,0:T(8,128)(2,1)S(1)}, u32[]{:S(2)}, u32[]{:S(2)}) collective-permute-start(bf16[16,7296]{1,0:T(8,128)(2,1)S(1)} %pack.1.refs_0_), channel_id=1, source_target_pairs={{0,1},{1,0},{2,3},{3,2},{4,5},{5,4},{6,7},{7,6},{8,9},{9,8},{10,11... | collective-permute-start | bytes 700424 | tf_op jit(solution)/shard_map/ppermute | solution.py:208
  9.0 4.2 %stage.3 = (bf16[1,7168,256]{2,1,0:T(8,128)(2,1)S(1)}, bf16[1,7168,256]{2,1,0:T(8,128)(2,1)S(1)}, bf16[1,256,7168]{2,1,0:T(8,128)(2,1)S(1)}) custom-call(bf16[1,7168,256]{2,1,0:T(8,128)(2,1)} %refs_0_, bf16[1,7168,256]{2,1,0:T(8,128)(2,1)} %refs_1_, bf16[1,256,7168]{2,1,0:T(8,128)(2,1)} %refs_2_.1), custom_call_target="tpu_custom_call" | custom-call | bytes 11010048 | tf_op jit(solution)/shard_map/stage/pallas_call | solution.py:138
  13.2 5.4 %collective-permute-done.1.refs_4_ = bf16[16,7296]{1,0:T(8,128)(2,1)S(1)} collective-permute-done((bf16[16,7296]{1,0:T(8,128)(2,1)S(1)}, bf16[16,7296]{1,0:T(8,128)(2,1)S(1)}, u32[]{:S(2)}, u32[]{:S(2)}) %collective-permute-start.1) | collective-permute-done | bytes 233504 | tf_op jit(solution)/shard_map/ppermute | solution.py:208
  19.3 1.5 %collective-permute-start.7 = (bf16[16,7296]{1,0:T(8,128)(2,1)S(1)}, bf16[16,7296]{1,0:T(8,128)(2,1)S(1)}, u32[]{:S(2)}, u32[]{:S(2)}) collective-permute-start(bf16[16,7296]{1,0:T(8,128)(2,1)S(1)} %collective-permute-done.1.refs_4_), channel_id=1, source_target_pairs={{0,1},{1,0},{2,3},{3,2},{4,5},{5,4},{6,7},{7,6},{8,9},{9,8},{10,11... | collective-permute-start | bytes 700424 | tf_op jit(solution)/shard_map/ppermute | solution.py:208
  20.8 1.9 %copy-done.2 = bf16[1,7168,256]{2,1,0:T(8,128)(2,1)} copy-done((bf16[1,7168,256]{2,1,0:T(8,128)(2,1)}, bf16[1,7168,256]{2,1,0:T(8,128)(2,1)S(1)}, u32[]{:S(2)}) %copy-start.2) | copy-done | bytes 3670040
  22.7 3.2 %stage.4 = (bf16[1,7168,256]{2,1,0:T(8,128)(2,1)S(1)}, bf16[1,7168,256]{2,1,0:T(8,128)(2,1)S(1)}) custom-call(bf16[1,7168,256]{2,1,0:T(8,128)(2,1)} %copy-done.1, bf16[1,7168,256]{2,1,0:T(8,128)(2,1)} %copy-done.2), custom_call_target="tpu_custom_call" | custom-call | bytes 7340032 | tf_op jit(solution)/shard_map/stage/pallas_call | solution.py:138
  27.4 1.5 %collective-permute-start.8 = (bf16[16,7296]{1,0:T(8,128)(2,1)S(1)}, bf16[16,7296]{1,0:T(8,128)(2,1)S(1)}, u32[]{:S(2)}, u32[]{:S(2)}) collective-permute-start(bf16[16,7296]{1,0:T(8,128)(2,1)S(1)} %collective-permute-done.4.refs_6_), channel_id=1, source_target_pairs={{0,1},{1,0},{2,3},{3,2},{4,5},{5,4},{6,7},{7,6},{8,9},{9,8},{10,11... | collective-permute-start | bytes 700424 | tf_op jit(solution)/shard_map/ppermute | solution.py:208
  28.9 1.8 %copy-done.3 = bf16[1,256,7168]{2,1,0:T(8,128)(2,1)} copy-done((bf16[1,256,7168]{2,1,0:T(8,128)(2,1)}, bf16[1,256,7168]{2,1,0:T(8,128)(2,1)S(1)}, u32[]{:S(2)}) %copy-start.3) | copy-done | bytes 3670040
  30.7 2.0 %stage.5.refs_14_ = bf16[1,256,7168]{2,1,0:T(8,128)(2,1)S(1)} custom-call(bf16[1,256,7168]{2,1,0:T(8,128)(2,1)} %copy-done.3), custom_call_target="tpu_custom_call" | custom-call | bytes 3670016 | tf_op jit(solution)/shard_map/stage/pallas_call | solution.py:138
  32.7 1.3 %collective-permute-done.6.refs_3_ = bf16[16,7296]{1,0:T(8,128)(2,1)S(1)} collective-permute-done((bf16[16,7296]{1,0:T(8,128)(2,1)S(1)}, bf16[16,7296]{1,0:T(8,128)(2,1)S(1)}, u32[]{:S(2)}, u32[]{:S(2)}) %collective-permute-start.6) | collective-permute-done | bytes 233504 | tf_op jit(solution)/shard_map/ppermute | solution.py:208
  34.6 3.5 %experts.1 = (bf16[16,7168]{1,0:T(8,128)(2,1)S(1)}, bf16[16,7168]{1,0:T(8,128)(2,1)S(1)}, bf16[16,7168]{1,0:T(8,128)(2,1)S(1)}, bf16[16,7168]{1,0:T(8,128)(2,1)S...) custom-call(bf16[16,7296]{1,0:T(8,128)(2,1)S(1)} %pack.1.refs_0_, ...), custom_call_target="tpu_custom_call" | custom-call | flops 2818572288 | bytes 22020096 | tf_op jit(solution)/shard_map/experts/pallas_call | solution.py:158
  38.2 1.3 %collective-permute-start.10 = (bf16[16,7168]{1,0:T(8,128)(2,1)S(1)}, bf16[16,7168]{1,0:T(8,128)(2,1)S(1)}, u32[]{:S(2)}, u32[]{:S(2)}) collective-permute-start(bf16[16,7168]{1,0:T(8,128)(2,1)S(1)} %get-tuple-element.71), channel_id=1, source_target_pairs={{0,1},{1,0},{2,3},{3,2},{4,5},{5,4},{6,7},{7,6},{8,9},{9,8},{10,11... | collective-permute-start | bytes 688136 | tf_op jit(solution)/shard_map/ppermute | solution.py:208
  40.1 1.5 %collective-permute-start.12 = (bf16[16,7168]{1,0:T(8,128)(2,1)S(1)}, bf16[16,7168]{1,0:T(8,128)(2,1)S(1)}, u32[]{:S(2)}, u32[]{:S(2)}) collective-permute-start(bf16[16,7168]{1,0:T(8,128)(2,1)S(1)} %get-tuple-element.73), channel_id=1, source_target_pairs={{0,2},{1,3},{2,0},{3,1},{4,6},{5,7},{6,4},{7,5},{8,10},{9,11},{10,... | collective-permute-start | bytes 688136 | tf_op jit(solution)/shard_map/ppermute | solution.py:208
  41.6 2.8 %collective-permute-done.10 = bf16[16,7168]{1,0:T(8,128)(2,1)S(1)} collective-permute-done((bf16[16,7168]{1,0:T(8,128)(2,1)S(1)}, bf16[16,7168]{1,0:T(8,128)(2,1)S(1)}, u32[]{:S(2)}, u32[]{:S(2)}) %collective-permute-start.10) | collective-permute-done | bytes 229408 | tf_op jit(solution)/shard_map/ppermute | solution.py:208
  45.5 1.5 %collective-permute-start.11 = (bf16[16,7168]{1,0:T(8,128)(2,1)S(1)}, bf16[16,7168]{1,0:T(8,128)(2,1)S(1)}, u32[]{:S(2)}, u32[]{:S(2)}) collective-permute-start(bf16[16,7168]{1,0:T(8,128)(2,1)S(1)} %get-tuple-element.72), channel_id=1, source_target_pairs={{0,1},{1,0},{2,3},{3,2},{4,5},{5,4},{6,7},{7,6},{8,9},{9,8},{10,11... | collective-permute-start | bytes 688136 | tf_op jit(solution)/shard_map/ppermute | solution.py:208
  47.8 3.3 %collective-permute-done.14 = bf16[16,7168]{1,0:T(8,128)(2,1)S(1)} collective-permute-done((bf16[16,7168]{1,0:T(8,128)(2,1)S(1)}, bf16[16,7168]{1,0:T(8,128)(2,1)S(1)}, u32[]{:S(2)}, u32[]{:S(2)}) %collective-permute-start.14) | collective-permute-done | bytes 229408 | tf_op jit(solution)/shard_map/ppermute | solution.py:208
  51.1 1.5 %collective-permute-start.15 = (bf16[16,7168]{1,0:T(8,128)(2,1)S(1)}, bf16[16,7168]{1,0:T(8,128)(2,1)S(1)}, u32[]{:S(2)}, u32[]{:S(2)}) collective-permute-start(bf16[16,7168]{1,0:T(8,128)(2,1)S(1)} %get-tuple-element.80), channel_id=1, source_target_pairs={{0,2},{1,3},{2,0},{3,1},{4,6},{5,7},{6,4},{7,5},{8,10},{9,11},{10,... | collective-permute-start | bytes 688136 | tf_op jit(solution)/shard_map/ppermute | solution.py:208
  52.7 1.5 %collective-permute-start.16 = (bf16[16,7168]{1,0:T(8,128)(2,1)S(1)}, bf16[16,7168]{1,0:T(8,128)(2,1)S(1)}, u32[]{:S(2)}, u32[]{:S(2)}) collective-permute-start(bf16[16,7168]{1,0:T(8,128)(2,1)S(1)} %add_convert_fusion.1), channel_id=1, source_target_pairs={{0,6},{1,7},{2,4},{3,5},{4,2},{5,3},{6,0},{7,1},{8,14},{9,15},{10,... | collective-permute-start | bytes 688136 | tf_op jit(solution)/shard_map/ppermute | solution.py:208
  54.3 1.1 %collective-permute-start.13 = (bf16[16,7168]{1,0:T(8,128)(2,1)S(1)}, bf16[16,7168]{1,0:T(8,128)(2,1)S(1)}, u32[]{:S(2)}, u32[]{:S(2)}) collective-permute-start(bf16[16,7168]{1,0:T(8,128)(2,1)S(1)} %add_convert_fusion.3), channel_id=1, source_target_pairs={{0,1},{1,0},{2,3},{3,2},{4,5},{5,4},{6,7},{7,6},{8,9},{9,8},{10,11... | collective-permute-start | bytes 688136 | tf_op jit(solution)/shard_map/ppermute | solution.py:208
  55.5 4.1 %collective-permute-done.15 = bf16[16,7168]{1,0:T(8,128)(2,1)S(1)} collective-permute-done((bf16[16,7168]{1,0:T(8,128)(2,1)S(1)}, bf16[16,7168]{1,0:T(8,128)(2,1)S(1)}, u32[]{:S(2)}, u32[]{:S(2)}) %collective-permute-start.15) | collective-permute-done | bytes 229408 | tf_op jit(solution)/shard_map/ppermute | solution.py:208
  59.6 1.1 %fusion.2 = bf16[1,128,512]{2,1,0:T(8,128)(2,1)} fusion(bf16[1,1024,576]{1,2,0:T(8,128)(2,1)S(1)} %copy-done.5, bf16[1,128,1024]{2,1,0:T(8,128)(2,1)S(1)} %fusion.7), kind=kOutput, calls=%fused_computation.4 | convolution fusion | flops 134283264 | bytes 1441792 | tf_op jit(solution)/shard_map/rhl,rlk->rhk/dot_general | solution.py:189
  60.7 1.7 %collective-permute-done.16 = bf16[16,7168]{1,0:T(8,128)(2,1)S(1)} collective-permute-done((bf16[16,7168]{1,0:T(8,128)(2,1)S(1)}, bf16[16,7168]{1,0:T(8,128)(2,1)S(1)}, u32[]{:S(2)}, u32[]{:S(2)}) %collective-permute-start.16) | collective-permute-done | bytes 229408 | tf_op jit(solution)/shard_map/ppermute | solution.py:208
  (39 shorter events, 7.4 us)
Async XLA Ops:
  0.6 46.4 %copy-start = (bf16[1,128,576]{1,2,0:T(8,128)(2,1)S(1)}, bf16[1,128,576]{1,2,0:T(8,128)(2,1)}, u32[]{:S(2)}) copy-start(bf16[1,128,576]{1,2,0:T(8,128)(2,1)} %param.15) | copy-start | bytes 442372
  1.8 16.8 %copy-start.4 = (bf16[1,256,7168]{2,1,0:T(8,128)(2,1)S(1)}, bf16[1,256,7168]{2,1,0:T(8,128)(2,1)}, u32[]{:S(2)}) copy-start(bf16[1,256,7168]{2,1,0:T(8,128)(2,1)} %refs_2_.1) | copy-start | bytes 11010052
  1.8 16.8 %collective-permute-start.3 = (bf16[1,7168,256]{2,1,0:T(8,128)(2,1)}, bf16[1,7168,256]{2,1,0:T(8,128)(2,1)S(1)}, u32[]{:S(2)}, u32[]{:S(2)}) collective-permute-start(bf16[1,7168,256]{2,1,0:T(8,128)(2,1)} %refs_0_), channel_id=1, source_target_pairs={{0,8},{8,0},{1,9},{9,1},{2,10},{10,2},{3,11},{11,3},{4,12},{12,4},... | collective-permute-start | bytes 11010056 | tf_op jit(solution)/shard_map/ppermute | solution.py:211
  2.3 10.9 %collective-permute-start = (bf16[16,7296]{1,0:T(8,128)(2,1)S(1)}, bf16[16,7296]{1,0:T(8,128)(2,1)S(1)}, u32[]{:S(2)}, u32[]{:S(2)}) collective-permute-start(bf16[16,7296]{1,0:T(8,128)(2,1)S(1)} %pack.1.refs_0_), channel_id=1, source_target_pairs={{0,2},{1,3},{2,0},{3,1},{4,6},{5,7},{6,4},{7,5},{8,10},{9,11},{10,... | collective-permute-start | bytes 700424 | tf_op jit(solution)/shard_map/ppermute | solution.py:208
  5.0 13.6 %collective-permute-start.1 = (bf16[16,7296]{1,0:T(8,128)(2,1)S(1)}, bf16[16,7296]{1,0:T(8,128)(2,1)S(1)}, u32[]{:S(2)}, u32[]{:S(2)}) collective-permute-start(bf16[16,7296]{1,0:T(8,128)(2,1)S(1)} %pack.1.refs_0_), channel_id=1, source_target_pairs={{0,6},{1,7},{2,4},{3,5},{4,2},{5,3},{6,0},{7,1},{8,14},{9,15},{10,... | collective-permute-start | bytes 700424 | tf_op jit(solution)/shard_map/ppermute | solution.py:208
  7.5 11.1 %collective-permute-start.2 = (bf16[16,7296]{1,0:T(8,128)(2,1)S(1)}, bf16[16,7296]{1,0:T(8,128)(2,1)S(1)}, u32[]{:S(2)}, u32[]{:S(2)}) collective-permute-start(bf16[16,7296]{1,0:T(8,128)(2,1)S(1)} %pack.1.refs_0_), channel_id=1, source_target_pairs={{0,1},{1,0},{2,3},{3,2},{4,5},{5,4},{6,7},{7,6},{8,9},{9,8},{10,11... | collective-permute-start | bytes 700424 | tf_op jit(solution)/shard_map/ppermute | solution.py:208
  9.0 11.9 %collective-permute-start.5 = (bf16[1,7168,256]{2,1,0:T(8,128)(2,1)}, bf16[1,7168,256]{2,1,0:T(8,128)(2,1)S(1)}, u32[]{:S(2)}, u32[]{:S(2)}) collective-permute-start(bf16[1,7168,256]{2,1,0:T(8,128)(2,1)} %refs_1_), channel_id=1, source_target_pairs={{0,8},{8,0},{1,9},{9,1},{2,10},{10,2},{3,11},{11,3},{4,12},{12,4},... | collective-permute-start | bytes 11010056 | tf_op jit(solution)/shard_map/ppermute | solution.py:211
  18.6 2.3 %copy-start.1 = (bf16[1,7168,256]{2,1,0:T(8,128)(2,1)}, bf16[1,7168,256]{2,1,0:T(8,128)(2,1)S(1)}, u32[]{:S(2)}) copy-start(bf16[1,7168,256]{2,1,0:T(8,128)(2,1)S(1)} %collective-permute-done.3.refs_0_) | copy-start | bytes 11010052
  18.6 10.3 %collective-permute-start.9 = (bf16[1,256,7168]{2,1,0:T(8,128)(2,1)S(1)}, bf16[1,256,7168]{2,1,0:T(8,128)(2,1)S(1)}, u32[]{:S(2)}, u32[]{:S(2)}) collective-permute-start(bf16[1,256,7168]{2,1,0:T(8,128)(2,1)S(1)} %copy-done.4), channel_id=1, source_target_pairs={{0,8},{8,0},{1,9},{9,1},{2,10},{10,2},{3,11},{11,3},{4,12},{12,4},... | collective-permute-start | bytes 11010056 | tf_op jit(solution)/shard_map/ppermute | solution.py:211
  18.7 8.1 %collective-permute-start.4 = (bf16[16,7296]{1,0:T(8,128)(2,1)S(1)}, bf16[16,7296]{1,0:T(8,128)(2,1)S(1)}, u32[]{:S(2)}, u32[]{:S(2)}) collective-permute-start(bf16[16,7296]{1,0:T(8,128)(2,1)S(1)} %collective-permute-done.1.refs_4_), channel_id=1, source_target_pairs={{0,2},{1,3},{2,0},{3,1},{4,6},{5,7},{6,4},{7,5},{8,10},{9,11},{10,... | collective-permute-start | bytes 700424 | tf_op jit(solution)/shard_map/ppermute | solution.py:208
  19.3 13.4 %collective-permute-start.7 = (bf16[16,7296]{1,0:T(8,128)(2,1)S(1)}, bf16[16,7296]{1,0:T(8,128)(2,1)S(1)}, u32[]{:S(2)}, u32[]{:S(2)}) collective-permute-start(bf16[16,7296]{1,0:T(8,128)(2,1)S(1)} %collective-permute-done.1.refs_4_), channel_id=1, source_target_pairs={{0,1},{1,0},{2,3},{3,2},{4,5},{5,4},{6,7},{7,6},{8,9},{9,8},{10,11... | collective-permute-start | bytes 700424 | tf_op jit(solution)/shard_map/ppermute | solution.py:208
  20.8 1.9 %copy-start.2 = (bf16[1,7168,256]{2,1,0:T(8,128)(2,1)}, bf16[1,7168,256]{2,1,0:T(8,128)(2,1)S(1)}, u32[]{:S(2)}) copy-start(bf16[1,7168,256]{2,1,0:T(8,128)(2,1)S(1)} %collective-permute-done.5.refs_1_) | copy-start | bytes 11010052
  26.8 7.3 %collective-permute-start.6 = (bf16[16,7296]{1,0:T(8,128)(2,1)S(1)}, bf16[16,7296]{1,0:T(8,128)(2,1)S(1)}, u32[]{:S(2)}, u32[]{:S(2)}) collective-permute-start(bf16[16,7296]{1,0:T(8,128)(2,1)S(1)} %collective-permute-done.2.refs_1_), channel_id=1, source_target_pairs={{0,2},{1,3},{2,0},{3,1},{4,6},{5,7},{6,4},{7,5},{8,10},{9,11},{10,... | collective-permute-start | bytes 700424 | tf_op jit(solution)/shard_map/ppermute | solution.py:208
  27.4 7.2 %collective-permute-start.8 = (bf16[16,7296]{1,0:T(8,128)(2,1)S(1)}, bf16[16,7296]{1,0:T(8,128)(2,1)S(1)}, u32[]{:S(2)}, u32[]{:S(2)}) collective-permute-start(bf16[16,7296]{1,0:T(8,128)(2,1)S(1)} %collective-permute-done.4.refs_6_), channel_id=1, source_target_pairs={{0,1},{1,0},{2,3},{3,2},{4,5},{5,4},{6,7},{7,6},{8,9},{9,8},{10,11... | collective-permute-start | bytes 700424 | tf_op jit(solution)/shard_map/ppermute | solution.py:208
  28.9 1.8 %copy-start.3 = (bf16[1,256,7168]{2,1,0:T(8,128)(2,1)}, bf16[1,256,7168]{2,1,0:T(8,128)(2,1)S(1)}, u32[]{:S(2)}) copy-start(bf16[1,256,7168]{2,1,0:T(8,128)(2,1)S(1)} %collective-permute-done.9.refs_0_) | copy-start | bytes 11010052
  32.7 14.3 %copy-start.5 = (bf16[1,1024,576]{1,2,0:T(8,128)(2,1)S(1)}, bf16[1,1024,576]{1,2,0:T(8,128)(2,1)}, u32[]{:S(2)}) copy-start(bf16[1,1024,576]{1,2,0:T(8,128)(2,1)} %param.16) | copy-start | bytes 3538948
  38.2 6.3 %collective-permute-start.10 = (bf16[16,7168]{1,0:T(8,128)(2,1)S(1)}, bf16[16,7168]{1,0:T(8,128)(2,1)S(1)}, u32[]{:S(2)}, u32[]{:S(2)}) collective-permute-start(bf16[16,7168]{1,0:T(8,128)(2,1)S(1)} %get-tuple-element.71), channel_id=1, source_target_pairs={{0,1},{1,0},{2,3},{3,2},{4,5},{5,4},{6,7},{7,6},{8,9},{9,8},{10,11... | collective-permute-start | bytes 688136 | tf_op jit(solution)/shard_map/ppermute | solution.py:208
  40.1 12.5 %collective-permute-start.12 = (bf16[16,7168]{1,0:T(8,128)(2,1)S(1)}, bf16[16,7168]{1,0:T(8,128)(2,1)S(1)}, u32[]{:S(2)}, u32[]{:S(2)}) collective-permute-start(bf16[16,7168]{1,0:T(8,128)(2,1)S(1)} %get-tuple-element.73), channel_id=1, source_target_pairs={{0,2},{1,3},{2,0},{3,1},{4,6},{5,7},{6,4},{7,5},{8,10},{9,11},{10,... | collective-permute-start | bytes 688136 | tf_op jit(solution)/shard_map/ppermute | solution.py:208
  44.5 6.6 %collective-permute-start.14 = (bf16[16,7168]{1,0:T(8,128)(2,1)S(1)}, bf16[16,7168]{1,0:T(8,128)(2,1)S(1)}, u32[]{:S(2)}, u32[]{:S(2)}) collective-permute-start(bf16[16,7168]{1,0:T(8,128)(2,1)S(1)} %add_convert_fusion.2), channel_id=1, source_target_pairs={{0,2},{1,3},{2,0},{3,1},{4,6},{5,7},{6,4},{7,5},{8,10},{9,11},{10,... | collective-permute-start | bytes 688136 | tf_op jit(solution)/shard_map/ppermute | solution.py:208
  45.5 7.0 %collective-permute-start.11 = (bf16[16,7168]{1,0:T(8,128)(2,1)S(1)}, bf16[16,7168]{1,0:T(8,128)(2,1)S(1)}, u32[]{:S(2)}, u32[]{:S(2)}) collective-permute-start(bf16[16,7168]{1,0:T(8,128)(2,1)S(1)} %get-tuple-element.72), channel_id=1, source_target_pairs={{0,1},{1,0},{2,3},{3,2},{4,5},{5,4},{6,7},{7,6},{8,9},{9,8},{10,11... | collective-permute-start | bytes 688136 | tf_op jit(solution)/shard_map/ppermute | solution.py:208
  51.1 8.5 %collective-permute-start.15 = (bf16[16,7168]{1,0:T(8,128)(2,1)S(1)}, bf16[16,7168]{1,0:T(8,128)(2,1)S(1)}, u32[]{:S(2)}, u32[]{:S(2)}) collective-permute-start(bf16[16,7168]{1,0:T(8,128)(2,1)S(1)} %get-tuple-element.80), channel_id=1, source_target_pairs={{0,2},{1,3},{2,0},{3,1},{4,6},{5,7},{6,4},{7,5},{8,10},{9,11},{10,... | collective-permute-start | bytes 688136 | tf_op jit(solution)/shard_map/ppermute | solution.py:208
  52.7 9.7 %collective-permute-start.16 = (bf16[16,7168]{1,0:T(8,128)(2,1)S(1)}, bf16[16,7168]{1,0:T(8,128)(2,1)S(1)}, u32[]{:S(2)}, u32[]{:S(2)}) collective-permute-start(bf16[16,7168]{1,0:T(8,128)(2,1)S(1)} %add_convert_fusion.1), channel_id=1, source_target_pairs={{0,6},{1,7},{2,4},{3,5},{4,2},{5,3},{6,0},{7,1},{8,14},{9,15},{10,... | collective-permute-start | bytes 688136 | tf_op jit(solution)/shard_map/ppermute | solution.py:208
  54.3 8.2 %collective-permute-start.13 = (bf16[16,7168]{1,0:T(8,128)(2,1)S(1)}, bf16[16,7168]{1,0:T(8,128)(2,1)S(1)}, u32[]{:S(2)}, u32[]{:S(2)}) collective-permute-start(bf16[16,7168]{1,0:T(8,128)(2,1)S(1)} %add_convert_fusion.3), channel_id=1, source_target_pairs={{0,1},{1,0},{2,3},{3,2},{4,5},{5,4},{6,7},{7,6},{8,9},{9,8},{10,11... | collective-permute-start | bytes 688136 | tf_op jit(solution)/shard_map/ppermute | solution.py:208

commit v5 on v4

--- a/solution.py
+++ b/solution.py
@@ -153,7 +153,7 @@
     count = len(blocks)
     rows, packed = blocks[0].shape
     width, hidden = weights[0].shape[1:]
-    steps = width // chunk_of(width, 1024)
+    steps = width // chunk_of(width, 1792)
     operands = [pltpu.with_memory_space_constraint(a, pltpu.VMEM) for a in (*blocks, masks, *weights)]
     return pl.pallas_call(
         functools.partial(expert_kernel, count, steps),
@@ -217,10 +217,10 @@
     column = jnp.arange(extra, dtype=jnp.int32)
     named = jnp.where(column < 3 * experts_all, column % experts_all, -1)
     masks = (named[None, :] == experts_here[:, None]).astype(jnp.float32)
-    tokens, masks = barrier((tokens, masks))
     packed = pack(tokens, routes, route_weight, experts_all)
 
     w_gate, w_up, packed = barrier((w_gate, w_up, packed))
+    w_down, masks = barrier((w_down, masks))
     gate_there, up_there = swap(w_gate), swap(w_up)
     bits = [1 << i for i in reversed(range(lines.bit_length() - 1))]
     gathered, across = {0: packed}, {}

time: 63.4 us -> 63.6 us (level)
  local copies, waits for them, and re-layouts: 3.66 us -> 1.8 us
  waiting for transfers between devices: 20.1 us -> 21.4 us
  starting transfers between devices: 20.9 us -> 21.6 us
    unnamed x12 -> x8, local copies, waits for them, and re-layouts: 3.66 us -> 1.8 us
    ppermute x14, waiting for transfers between devices: 20.1 us -> 21.4 us  [hop(): return lax.ppermute(value, 'dev', [(d, d ^ offset) for d in range(devs)])]
    ppermute x14, starting transfers between devices: 20.3 us -> 21 us  [hop(): return lax.ppermute(value, 'dev', [(d, d ^ offset) for d in range(devs)])]
where the time goes in v5:
time: 63.6 us; the launch traced here: 63.5 us
  starting transfers between devices  21.6 us (34%)
  waiting for transfers between devices  21.4 us (34%)
  Pallas kernels  14 us (22%)
  local copies, waits for them, and re-layouts  1.8 us (3%)
  matrix products  1.62 us (3%)
  other arithmetic  1.57 us (2%)
  between operations  1.42 us (2%)
    ppermute x14, waiting for transfers between devices, hop(): return lax.ppermute(value, 'dev', [(d, d ^ offset) for d in range(devs)])  21.4 us
    ppermute x14, starting transfers between devices, hop(): return lax.ppermute(value, 'dev', [(d, d ^ offset) for d in range(devs)])  21 us
    pallas_call x3, Pallas kernels, stage(): pl.pallas_call(functools.partial(stage_kernel, count), out_shape=[pltpu.V...  9.58 us
    pallas_call x1, Pallas kernels, run_experts(): pl.pallas_call(functools.partial(expert_kernel, count, steps), out_shape=...  3.46 us
    unnamed x8, local copies, waits for them, and re-layouts  1.8 us
  transfers between devices with their start and end apart: 17, of which 8 were waited for; matrix products, arithmetic and copies ran while one was open for 4% of the time, Pallas kernels for 15%

profile of v5, /device:TPU:0, one launch (start us, length us, event | category | flops | bytes accessed | tf_op | source)
XLA Modules:
  0.0 63.5 jit_solution(15453561896019252641)
XLA Ops:
  2.2 2.7 %collective-permute-start = (bf16[16,7296]{1,0:T(8,128)(2,1)S(1)}, bf16[16,7296]{1,0:T(8,128)(2,1)S(1)}, u32[]{:S(2)}, u32[]{:S(2)}) collective-permute-start(bf16[16,7296]{1,0:T(8,128)(2,1)S(1)} %pack.1.refs_0_), channel_id=1, source_target_pairs={{0,2},{1,3},{2,0},{3,1},{4,6},{5,7},{6,4},{7,5},{8,10},{9,11},{10,... | collective-permute-start | bytes 700424 | tf_op jit(solution)/shard_map/ppermute | solution.py:208
  4.8 2.5 %collective-permute-start.1 = (bf16[16,7296]{1,0:T(8,128)(2,1)S(1)}, bf16[16,7296]{1,0:T(8,128)(2,1)S(1)}, u32[]{:S(2)}, u32[]{:S(2)}) collective-permute-start(bf16[16,7296]{1,0:T(8,128)(2,1)S(1)} %pack.1.refs_0_), channel_id=1, source_target_pairs={{0,6},{1,7},{2,4},{3,5},{4,2},{5,3},{6,0},{7,1},{8,14},{9,15},{10,... | collective-permute-start | bytes 700424 | tf_op jit(solution)/shard_map/ppermute | solution.py:208
  7.3 1.5 %collective-permute-start.2 = (bf16[16,7296]{1,0:T(8,128)(2,1)S(1)}, bf16[16,7296]{1,0:T(8,128)(2,1)S(1)}, u32[]{:S(2)}, u32[]{:S(2)}) collective-permute-start(bf16[16,7296]{1,0:T(8,128)(2,1)S(1)} %pack.1.refs_0_), channel_id=1, source_target_pairs={{0,1},{1,0},{2,3},{3,2},{4,5},{5,4},{6,7},{7,6},{8,9},{9,8},{10,11... | collective-permute-start | bytes 700424 | tf_op jit(solution)/shard_map/ppermute | solution.py:208
  9.0 4.4 %stage.3 = (bf16[1,7168,256]{2,1,0:T(8,128)(2,1)S(1)}, bf16[1,7168,256]{2,1,0:T(8,128)(2,1)S(1)}, bf16[1,256,7168]{2,1,0:T(8,128)(2,1)S(1)}) custom-call(bf16[1,7168,256]{2,1,0:T(8,128)(2,1)} %refs_0_, bf16[1,7168,256]{2,1,0:T(8,128)(2,1)} %refs_1_, bf16[1,256,7168]{2,1,0:T(8,128)(2,1)} %refs_2_), custom_call_target="tpu_custom_call" | custom-call | bytes 11010048 | tf_op jit(solution)/shard_map/stage/pallas_call | solution.py:138
  13.4 5.1 %collective-permute-done.1.refs_4_ = bf16[16,7296]{1,0:T(8,128)(2,1)S(1)} collective-permute-done((bf16[16,7296]{1,0:T(8,128)(2,1)S(1)}, bf16[16,7296]{1,0:T(8,128)(2,1)S(1)}, u32[]{:S(2)}, u32[]{:S(2)}) %collective-permute-start.1) | collective-permute-done | bytes 233504 | tf_op jit(solution)/shard_map/ppermute | solution.py:208
  19.2 1.5 %collective-permute-start.7 = (bf16[16,7296]{1,0:T(8,128)(2,1)S(1)}, bf16[16,7296]{1,0:T(8,128)(2,1)S(1)}, u32[]{:S(2)}, u32[]{:S(2)}) collective-permute-start(bf16[16,7296]{1,0:T(8,128)(2,1)S(1)} %collective-permute-done.1.refs_4_), channel_id=1, source_target_pairs={{0,1},{1,0},{2,3},{3,2},{4,5},{5,4},{6,7},{7,6},{8,9},{9,8},{10,11... | collective-permute-start | bytes 700424 | tf_op jit(solution)/shard_map/ppermute | solution.py:208
  20.7 3.2 %stage.4 = (bf16[1,7168,256]{2,1,0:T(8,128)(2,1)S(1)}, bf16[1,7168,256]{2,1,0:T(8,128)(2,1)S(1)}) custom-call(bf16[1,7168,256]{2,1,0:T(8,128)(2,1)} %collective-permute-done.3.refs_0_, bf16[1,7168,256]{2,1,0:T(8,128)(2,1)} %collective-permute-done.5.refs_1_), custom_call_target="tpu_custom_call" | custom-call | bytes 7340032 | tf_op jit(solution)/shard_map/stage/pallas_call | solution.py:138
  23.9 2.8 %collective-permute-done.4.refs_6_ = bf16[16,7296]{1,0:T(8,128)(2,1)S(1)} collective-permute-done((bf16[16,7296]{1,0:T(8,128)(2,1)S(1)}, bf16[16,7296]{1,0:T(8,128)(2,1)S(1)}, u32[]{:S(2)}, u32[]{:S(2)}) %collective-permute-start.4) | collective-permute-done | bytes 233504 | tf_op jit(solution)/shard_map/ppermute | solution.py:208
  27.2 1.5 %collective-permute-start.8 = (bf16[16,7296]{1,0:T(8,128)(2,1)S(1)}, bf16[16,7296]{1,0:T(8,128)(2,1)S(1)}, u32[]{:S(2)}, u32[]{:S(2)}) collective-permute-start(bf16[16,7296]{1,0:T(8,128)(2,1)S(1)} %collective-permute-done.4.refs_6_), channel_id=1, source_target_pairs={{0,1},{1,0},{2,3},{3,2},{4,5},{5,4},{6,7},{7,6},{8,9},{9,8},{10,11... | collective-permute-start | bytes 700424 | tf_op jit(solution)/shard_map/ppermute | solution.py:208
  28.7 1.8 %copy-done.1 = bf16[1,256,7168]{2,1,0:T(8,128)(2,1)} copy-done((bf16[1,256,7168]{2,1,0:T(8,128)(2,1)}, bf16[1,256,7168]{2,1,0:T(8,128)(2,1)S(1)}, u32[]{:S(2)}) %copy-start.1) | copy-done | bytes 3670040
  30.5 2.0 %stage.5.refs_14_ = bf16[1,256,7168]{2,1,0:T(8,128)(2,1)S(1)} custom-call(bf16[1,256,7168]{2,1,0:T(8,128)(2,1)} %copy-done.1), custom_call_target="tpu_custom_call" | custom-call | bytes 3670016 | tf_op jit(solution)/shard_map/stage/pallas_call | solution.py:138
  32.6 1.3 %collective-permute-done.6.refs_3_ = bf16[16,7296]{1,0:T(8,128)(2,1)S(1)} collective-permute-done((bf16[16,7296]{1,0:T(8,128)(2,1)S(1)}, bf16[16,7296]{1,0:T(8,128)(2,1)S(1)}, u32[]{:S(2)}, u32[]{:S(2)}) %collective-permute-start.6) | collective-permute-done | bytes 233504 | tf_op jit(solution)/shard_map/ppermute | solution.py:208
  34.2 3.5 %experts.1 = (bf16[16,7168]{1,0:T(8,128)(2,1)S(1)}, bf16[16,7168]{1,0:T(8,128)(2,1)S(1)}, bf16[16,7168]{1,0:T(8,128)(2,1)S(1)}, bf16[16,7168]{1,0:T(8,128)(2,1)S...) custom-call(bf16[16,7296]{1,0:T(8,128)(2,1)S(1)} %pack.1.refs_0_, ...), custom_call_target="tpu_custom_call" | custom-call | flops 2818572288 | bytes 22020096 | tf_op jit(solution)/shard_map/experts/pallas_call | solution.py:158
  37.6 1.6 %collective-permute-start.10 = (bf16[16,7168]{1,0:T(8,128)(2,1)S(1)}, bf16[16,7168]{1,0:T(8,128)(2,1)S(1)}, u32[]{:S(2)}, u32[]{:S(2)}) collective-permute-start(bf16[16,7168]{1,0:T(8,128)(2,1)S(1)} %get-tuple-element.71), channel_id=1, source_target_pairs={{0,1},{1,0},{2,3},{3,2},{4,5},{5,4},{6,7},{7,6},{8,9},{9,8},{10,11... | collective-permute-start | bytes 688136 | tf_op jit(solution)/shard_map/ppermute | solution.py:208
  39.9 1.5 %collective-permute-start.12 = (bf16[16,7168]{1,0:T(8,128)(2,1)S(1)}, bf16[16,7168]{1,0:T(8,128)(2,1)S(1)}, u32[]{:S(2)}, u32[]{:S(2)}) collective-permute-start(bf16[16,7168]{1,0:T(8,128)(2,1)S(1)} %get-tuple-element.73), channel_id=1, source_target_pairs={{0,2},{1,3},{2,0},{3,1},{4,6},{5,7},{6,4},{7,5},{8,10},{9,11},{10,... | collective-permute-start | bytes 688136 | tf_op jit(solution)/shard_map/ppermute | solution.py:208
  41.4 2.3 %collective-permute-done.10 = bf16[16,7168]{1,0:T(8,128)(2,1)S(1)} collective-permute-done((bf16[16,7168]{1,0:T(8,128)(2,1)S(1)}, bf16[16,7168]{1,0:T(8,128)(2,1)S(1)}, u32[]{:S(2)}, u32[]{:S(2)}) %collective-permute-start.10) | collective-permute-done | bytes 229408 | tf_op jit(solution)/shard_map/ppermute | solution.py:208
  43.8 1.5 %collective-permute-start.14 = (bf16[16,7168]{1,0:T(8,128)(2,1)S(1)}, bf16[16,7168]{1,0:T(8,128)(2,1)S(1)}, u32[]{:S(2)}, u32[]{:S(2)}) collective-permute-start(bf16[16,7168]{1,0:T(8,128)(2,1)S(1)} %add_convert_fusion.2), channel_id=1, source_target_pairs={{0,2},{1,3},{2,0},{3,1},{4,6},{5,7},{6,4},{7,5},{8,10},{9,11},{10,... | collective-permute-start | bytes 688136 | tf_op jit(solution)/shard_map/ppermute | solution.py:208
  45.3 1.5 %collective-permute-start.11 = (bf16[16,7168]{1,0:T(8,128)(2,1)S(1)}, bf16[16,7168]{1,0:T(8,128)(2,1)S(1)}, u32[]{:S(2)}, u32[]{:S(2)}) collective-permute-start(bf16[16,7168]{1,0:T(8,128)(2,1)S(1)} %get-tuple-element.72), channel_id=1, source_target_pairs={{0,1},{1,0},{2,3},{3,2},{4,5},{5,4},{6,7},{7,6},{8,9},{9,8},{10,11... | collective-permute-start | bytes 688136 | tf_op jit(solution)/shard_map/ppermute | solution.py:208
  47.5 3.3 %collective-permute-done.14 = bf16[16,7168]{1,0:T(8,128)(2,1)S(1)} collective-permute-done((bf16[16,7168]{1,0:T(8,128)(2,1)S(1)}, bf16[16,7168]{1,0:T(8,128)(2,1)S(1)}, u32[]{:S(2)}, u32[]{:S(2)}) %collective-permute-start.14) | collective-permute-done | bytes 229408 | tf_op jit(solution)/shard_map/ppermute | solution.py:208
  50.9 1.5 %collective-permute-start.15 = (bf16[16,7168]{1,0:T(8,128)(2,1)S(1)}, bf16[16,7168]{1,0:T(8,128)(2,1)S(1)}, u32[]{:S(2)}, u32[]{:S(2)}) collective-permute-start(bf16[16,7168]{1,0:T(8,128)(2,1)S(1)} %get-tuple-element.80), channel_id=1, source_target_pairs={{0,2},{1,3},{2,0},{3,1},{4,6},{5,7},{6,4},{7,5},{8,10},{9,11},{10,... | collective-permute-start | bytes 688136 | tf_op jit(solution)/shard_map/ppermute | solution.py:208
  52.5 1.5 %collective-permute-start.16 = (bf16[16,7168]{1,0:T(8,128)(2,1)S(1)}, bf16[16,7168]{1,0:T(8,128)(2,1)S(1)}, u32[]{:S(2)}, u32[]{:S(2)}) collective-permute-start(bf16[16,7168]{1,0:T(8,128)(2,1)S(1)} %add_convert_fusion.1), channel_id=1, source_target_pairs={{0,6},{1,7},{2,4},{3,5},{4,2},{5,3},{6,0},{7,1},{8,14},{9,15},{10,... | collective-permute-start | bytes 688136 | tf_op jit(solution)/shard_map/ppermute | solution.py:208
  55.2 3.6 %collective-permute-done.15 = bf16[16,7168]{1,0:T(8,128)(2,1)S(1)} collective-permute-done((bf16[16,7168]{1,0:T(8,128)(2,1)S(1)}, bf16[16,7168]{1,0:T(8,128)(2,1)S(1)}, u32[]{:S(2)}, u32[]{:S(2)}) %collective-permute-start.15) | collective-permute-done | bytes 229408 | tf_op jit(solution)/shard_map/ppermute | solution.py:208
  58.8 1.1 %fusion.2 = bf16[1,128,512]{2,1,0:T(8,128)(2,1)} fusion(bf16[1,1024,576]{1,2,0:T(8,128)(2,1)S(1)} %copy-done.3, bf16[1,128,1024]{2,1,0:T(8,128)(2,1)S(1)} %fusion.7), kind=kOutput, calls=%fused_computation.4 | convolution fusion | flops 134283264 | bytes 1441792 | tf_op jit(solution)/shard_map/rhl,rlk->rhk/dot_general | solution.py:189
  60.0 2.7 %collective-permute-done.16 = bf16[16,7168]{1,0:T(8,128)(2,1)S(1)} collective-permute-done((bf16[16,7168]{1,0:T(8,128)(2,1)S(1)}, bf16[16,7168]{1,0:T(8,128)(2,1)S(1)}, u32[]{:S(2)}, u32[]{:S(2)}) %collective-permute-start.16) | collective-permute-done | bytes 229408 | tf_op jit(solution)/shard_map/ppermute | solution.py:208
  (35 shorter events, 6.2 us)
Async XLA Ops:
  0.6 46.2 %copy-start = (bf16[1,128,576]{1,2,0:T(8,128)(2,1)S(1)}, bf16[1,128,576]{1,2,0:T(8,128)(2,1)}, u32[]{:S(2)}) copy-start(bf16[1,128,576]{1,2,0:T(8,128)(2,1)} %param.15) | copy-start | bytes 442372
  1.7 16.8 %collective-permute-start.3 = (bf16[1,7168,256]{2,1,0:T(8,128)(2,1)}, bf16[1,7168,256]{2,1,0:T(8,128)(2,1)}, u32[]{:S(2)}, u32[]{:S(2)}) collective-permute-start(bf16[1,7168,256]{2,1,0:T(8,128)(2,1)} %refs_0_), channel_id=1, source_target_pairs={{0,8},{8,0},{1,9},{9,1},{2,10},{10,2},{3,11},{11,3},{4,12},{12,4},... | collective-permute-start | bytes 11010056 | tf_op jit(solution)/shard_map/ppermute | solution.py:211
  2.2 11.2 %collective-permute-start = (bf16[16,7296]{1,0:T(8,128)(2,1)S(1)}, bf16[16,7296]{1,0:T(8,128)(2,1)S(1)}, u32[]{:S(2)}, u32[]{:S(2)}) collective-permute-start(bf16[16,7296]{1,0:T(8,128)(2,1)S(1)} %pack.1.refs_0_), channel_id=1, source_target_pairs={{0,2},{1,3},{2,0},{3,1},{4,6},{5,7},{6,4},{7,5},{8,10},{9,11},{10,... | collective-permute-start | bytes 700424 | tf_op jit(solution)/shard_map/ppermute | solution.py:208
  4.8 13.6 %collective-permute-start.1 = (bf16[16,7296]{1,0:T(8,128)(2,1)S(1)}, bf16[16,7296]{1,0:T(8,128)(2,1)S(1)}, u32[]{:S(2)}, u32[]{:S(2)}) collective-permute-start(bf16[16,7296]{1,0:T(8,128)(2,1)S(1)} %pack.1.refs_0_), channel_id=1, source_target_pairs={{0,6},{1,7},{2,4},{3,5},{4,2},{5,3},{6,0},{7,1},{8,14},{9,15},{10,... | collective-permute-start | bytes 700424 | tf_op jit(solution)/shard_map/ppermute | solution.py:208
  7.3 11.1 %collective-permute-start.2 = (bf16[16,7296]{1,0:T(8,128)(2,1)S(1)}, bf16[16,7296]{1,0:T(8,128)(2,1)S(1)}, u32[]{:S(2)}, u32[]{:S(2)}) collective-permute-start(bf16[16,7296]{1,0:T(8,128)(2,1)S(1)} %pack.1.refs_0_), channel_id=1, source_target_pairs={{0,1},{1,0},{2,3},{3,2},{4,5},{5,4},{6,7},{7,6},{8,9},{9,8},{10,11... | collective-permute-start | bytes 700424 | tf_op jit(solution)/shard_map/ppermute | solution.py:208
  8.8 11.9 %collective-permute-start.5 = (bf16[1,7168,256]{2,1,0:T(8,128)(2,1)}, bf16[1,7168,256]{2,1,0:T(8,128)(2,1)}, u32[]{:S(2)}, u32[]{:S(2)}) collective-permute-start(bf16[1,7168,256]{2,1,0:T(8,128)(2,1)} %refs_1_), channel_id=1, source_target_pairs={{0,8},{8,0},{1,9},{9,1},{2,10},{10,2},{3,11},{11,3},{4,12},{12,4},... | collective-permute-start | bytes 11010056 | tf_op jit(solution)/shard_map/ppermute | solution.py:211
  9.0 9.4 %copy-start.2 = (bf16[1,256,7168]{2,1,0:T(8,128)(2,1)S(1)}, bf16[1,256,7168]{2,1,0:T(8,128)(2,1)}, u32[]{:S(2)}) copy-start(bf16[1,256,7168]{2,1,0:T(8,128)(2,1)} %refs_2_) | copy-start | bytes 11010052
  18.4 10.3 %collective-permute-start.9 = (bf16[1,256,7168]{2,1,0:T(8,128)(2,1)S(1)}, bf16[1,256,7168]{2,1,0:T(8,128)(2,1)S(1)}, u32[]{:S(2)}, u32[]{:S(2)}) collective-permute-start(bf16[1,256,7168]{2,1,0:T(8,128)(2,1)S(1)} %copy-done.2), channel_id=1, source_target_pairs={{0,8},{8,0},{1,9},{9,1},{2,10},{10,2},{3,11},{11,3},{4,12},{12,4},... | collective-permute-start | bytes 11010056 | tf_op jit(solution)/shard_map/ppermute | solution.py:211
  18.5 8.1 %collective-permute-start.4 = (bf16[16,7296]{1,0:T(8,128)(2,1)S(1)}, bf16[16,7296]{1,0:T(8,128)(2,1)S(1)}, u32[]{:S(2)}, u32[]{:S(2)}) collective-permute-start(bf16[16,7296]{1,0:T(8,128)(2,1)S(1)} %collective-permute-done.1.refs_4_), channel_id=1, source_target_pairs={{0,2},{1,3},{2,0},{3,1},{4,6},{5,7},{6,4},{7,5},{8,10},{9,11},{10,... | collective-permute-start | bytes 700424 | tf_op jit(solution)/shard_map/ppermute | solution.py:208
  19.2 13.4 %collective-permute-start.7 = (bf16[16,7296]{1,0:T(8,128)(2,1)S(1)}, bf16[16,7296]{1,0:T(8,128)(2,1)S(1)}, u32[]{:S(2)}, u32[]{:S(2)}) collective-permute-start(bf16[16,7296]{1,0:T(8,128)(2,1)S(1)} %collective-permute-done.1.refs_4_), channel_id=1, source_target_pairs={{0,1},{1,0},{2,3},{3,2},{4,5},{5,4},{6,7},{7,6},{8,9},{9,8},{10,11... | collective-permute-start | bytes 700424 | tf_op jit(solution)/shard_map/ppermute | solution.py:208
  26.6 7.3 %collective-permute-start.6 = (bf16[16,7296]{1,0:T(8,128)(2,1)S(1)}, bf16[16,7296]{1,0:T(8,128)(2,1)S(1)}, u32[]{:S(2)}, u32[]{:S(2)}) collective-permute-start(bf16[16,7296]{1,0:T(8,128)(2,1)S(1)} %collective-permute-done.2.refs_1_), channel_id=1, source_target_pairs={{0,2},{1,3},{2,0},{3,1},{4,6},{5,7},{6,4},{7,5},{8,10},{9,11},{10,... | collective-permute-start | bytes 700424 | tf_op jit(solution)/shard_map/ppermute | solution.py:208
  27.2 7.0 %collective-permute-start.8 = (bf16[16,7296]{1,0:T(8,128)(2,1)S(1)}, bf16[16,7296]{1,0:T(8,128)(2,1)S(1)}, u32[]{:S(2)}, u32[]{:S(2)}) collective-permute-start(bf16[16,7296]{1,0:T(8,128)(2,1)S(1)} %collective-permute-done.4.refs_6_), channel_id=1, source_target_pairs={{0,1},{1,0},{2,3},{3,2},{4,5},{5,4},{6,7},{7,6},{8,9},{9,8},{10,11... | collective-permute-start | bytes 700424 | tf_op jit(solution)/shard_map/ppermute | solution.py:208
  28.7 1.8 %copy-start.1 = (bf16[1,256,7168]{2,1,0:T(8,128)(2,1)}, bf16[1,256,7168]{2,1,0:T(8,128)(2,1)S(1)}, u32[]{:S(2)}) copy-start(bf16[1,256,7168]{2,1,0:T(8,128)(2,1)S(1)} %collective-permute-done.9.refs_0_) | copy-start | bytes 11010052
  32.6 14.3 %copy-start.3 = (bf16[1,1024,576]{1,2,0:T(8,128)(2,1)S(1)}, bf16[1,1024,576]{1,2,0:T(8,128)(2,1)}, u32[]{:S(2)}) copy-start(bf16[1,1024,576]{1,2,0:T(8,128)(2,1)} %param.16) | copy-start | bytes 3538948
  37.6 6.1 %collective-permute-start.10 = (bf16[16,7168]{1,0:T(8,128)(2,1)S(1)}, bf16[16,7168]{1,0:T(8,128)(2,1)S(1)}, u32[]{:S(2)}, u32[]{:S(2)}) collective-permute-start(bf16[16,7168]{1,0:T(8,128)(2,1)S(1)} %get-tuple-element.71), channel_id=1, source_target_pairs={{0,1},{1,0},{2,3},{3,2},{4,5},{5,4},{6,7},{7,6},{8,9},{9,8},{10,11... | collective-permute-start | bytes 688136 | tf_op jit(solution)/shard_map/ppermute | solution.py:208
  39.9 12.5 %collective-permute-start.12 = (bf16[16,7168]{1,0:T(8,128)(2,1)S(1)}, bf16[16,7168]{1,0:T(8,128)(2,1)S(1)}, u32[]{:S(2)}, u32[]{:S(2)}) collective-permute-start(bf16[16,7168]{1,0:T(8,128)(2,1)S(1)} %get-tuple-element.73), channel_id=1, source_target_pairs={{0,2},{1,3},{2,0},{3,1},{4,6},{5,7},{6,4},{7,5},{8,10},{9,11},{10,... | collective-permute-start | bytes 688136 | tf_op jit(solution)/shard_map/ppermute | solution.py:208
  43.8 7.1 %collective-permute-start.14 = (bf16[16,7168]{1,0:T(8,128)(2,1)S(1)}, bf16[16,7168]{1,0:T(8,128)(2,1)S(1)}, u32[]{:S(2)}, u32[]{:S(2)}) collective-permute-start(bf16[16,7168]{1,0:T(8,128)(2,1)S(1)} %add_convert_fusion.2), channel_id=1, source_target_pairs={{0,2},{1,3},{2,0},{3,1},{4,6},{5,7},{6,4},{7,5},{8,10},{9,11},{10,... | collective-permute-start | bytes 688136 | tf_op jit(solution)/shard_map/ppermute | solution.py:208
  45.3 7.0 %collective-permute-start.11 = (bf16[16,7168]{1,0:T(8,128)(2,1)S(1)}, bf16[16,7168]{1,0:T(8,128)(2,1)S(1)}, u32[]{:S(2)}, u32[]{:S(2)}) collective-permute-start(bf16[16,7168]{1,0:T(8,128)(2,1)S(1)} %get-tuple-element.72), channel_id=1, source_target_pairs={{0,1},{1,0},{2,3},{3,2},{4,5},{5,4},{6,7},{7,6},{8,9},{9,8},{10,11... | collective-permute-start | bytes 688136 | tf_op jit(solution)/shard_map/ppermute | solution.py:208
  50.9 7.9 %collective-permute-start.15 = (bf16[16,7168]{1,0:T(8,128)(2,1)S(1)}, bf16[16,7168]{1,0:T(8,128)(2,1)S(1)}, u32[]{:S(2)}, u32[]{:S(2)}) collective-permute-start(bf16[16,7168]{1,0:T(8,128)(2,1)S(1)} %get-tuple-element.80), channel_id=1, source_target_pairs={{0,2},{1,3},{2,0},{3,1},{4,6},{5,7},{6,4},{7,5},{8,10},{9,11},{10,... | collective-permute-start | bytes 688136 | tf_op jit(solution)/shard_map/ppermute | solution.py:208
  52.5 10.1 %collective-permute-start.16 = (bf16[16,7168]{1,0:T(8,128)(2,1)S(1)}, bf16[16,7168]{1,0:T(8,128)(2,1)S(1)}, u32[]{:S(2)}, u32[]{:S(2)}) collective-permute-start(bf16[16,7168]{1,0:T(8,128)(2,1)S(1)} %add_convert_fusion.1), channel_id=1, source_target_pairs={{0,6},{1,7},{2,4},{3,5},{4,2},{5,3},{6,0},{7,1},{8,14},{9,15},{10,... | collective-permute-start | bytes 688136 | tf_op jit(solution)/shard_map/ppermute | solution.py:208
  54.1 8.6 %collective-permute-start.13 = (bf16[16,7168]{1,0:T(8,128)(2,1)S(1)}, bf16[16,7168]{1,0:T(8,128)(2,1)S(1)}, u32[]{:S(2)}, u32[]{:S(2)}) collective-permute-start(bf16[16,7168]{1,0:T(8,128)(2,1)S(1)} %add_convert_fusion.3), channel_id=1, source_target_pairs={{0,1},{1,0},{2,3},{3,2},{4,5},{5,4},{6,7},{7,6},{8,9},{9,8},{10,11... | collective-permute-start | bytes 688136 | tf_op jit(solution)/shard_map/ppermute | solution.py:208

commit v6 on v4

--- a/solution.py
+++ b/solution.py
@@ -228,10 +228,7 @@
         gathered[bit] = hop(packed, (2 * bit - 1) * PAIR)
     across[0] = hop(packed, 1)
     weights_here = stage(w_gate, w_up, w_down)
-    gathered, across, weights_here, gate_there = barrier(
-        (gathered, across, weights_here, gate_there)
-    )
-    w_down, gate_there = barrier((w_down, gate_there))
+    gathered, weights_here, gate_there = barrier((gathered, weights_here, gate_there))
     down_there = swap(w_down)
     into_there = stage(gate_there, up_there)
     for bit in bits[1:]:

time: 63.4 us -> 62.6 us (0.987)
  waiting for transfers between devices: 20.1 us -> 19.1 us
    ppermute x14, waiting for transfers between devices: 20.1 us -> 19.1 us  [hop(): return lax.ppermute(value, 'dev', [(d, d ^ offset) for d in range(devs)])]
    unnamed x12 -> x10, local copies, waits for them, and re-layouts: 3.66 us -> 3.63 us
where the time goes in v6:
time: 62.6 us; the launch traced here: 62.4 us
  starting transfers between devices  21 us (34%)
  waiting for transfers between devices  19.1 us (31%)
  Pallas kernels  13.9 us (22%)
  local copies, waits for them, and re-layouts  3.63 us (6%)
  matrix products  1.63 us (3%)
  other arithmetic  1.58 us (3%)
  between operations  1.43 us (2%)
    ppermute x14, starting transfers between devices, hop(): return lax.ppermute(value, 'dev', [(d, d ^ offset) for d in range(devs)])  20 us
    ppermute x14, waiting for transfers between devices, hop(): return lax.ppermute(value, 'dev', [(d, d ^ offset) for d in range(devs)])  19.1 us
    pallas_call x3, Pallas kernels, stage(): pl.pallas_call(functools.partial(stage_kernel, count), out_shape=[pltpu.V...  9.45 us
    unnamed x10, local copies, waits for them, and re-layouts  3.63 us
    pallas_call x1, Pallas kernels, run_experts(): pl.pallas_call(functools.partial(expert_kernel, count, steps), out_shape=...  3.52 us
  transfers between devices with their start and end apart: 17, of which 8 were waited for; matrix products, arithmetic and copies ran while one was open for 4% of the time, Pallas kernels for 15%

profile of v6, /device:TPU:0, one launch (start us, length us, event | category | flops | bytes accessed | tf_op | source)
XLA Modules:
  0.0 62.4 jit_solution(14853270130562460530)
XLA Ops:
  0.8 1.0 %pack.1.refs_0_ = bf16[16,7296]{1,0:T(8,128)(2,1)S(1)} custom-call(s32[2,16]{1,0:T(2,128)} %bitcast.26, f32[2,16]{1,0:T(2,128)} %bitcast.27, bf16[16,7168]{1,0:T(8,128)(2,1)} %tokens_hbm), custom_call_target="tpu_custom_call" | custom-call | tf_op jit(solution)/shard_map/pack/pallas_call | solution.py:72
  2.8 2.7 %collective-permute-start = (bf16[16,7296]{1,0:T(8,128)(2,1)S(1)}, bf16[16,7296]{1,0:T(8,128)(2,1)S(1)}, u32[]{:S(2)}, u32[]{:S(2)}) collective-permute-start(bf16[16,7296]{1,0:T(8,128)(2,1)S(1)} %pack.1.refs_0_), channel_id=1, source_target_pairs={{0,2},{1,3},{2,0},{3,1},{4,6},{5,7},{6,4},{7,5},{8,10},{9,11},{10,... | collective-permute-start | bytes 700424 | tf_op jit(solution)/shard_map/ppermute | solution.py:208
  5.5 2.5 %collective-permute-start.1 = (bf16[16,7296]{1,0:T(8,128)(2,1)S(1)}, bf16[16,7296]{1,0:T(8,128)(2,1)S(1)}, u32[]{:S(2)}, u32[]{:S(2)}) collective-permute-start(bf16[16,7296]{1,0:T(8,128)(2,1)S(1)} %pack.1.refs_0_), channel_id=1, source_target_pairs={{0,6},{1,7},{2,4},{3,5},{4,2},{5,3},{6,0},{7,1},{8,14},{9,15},{10,... | collective-permute-start | bytes 700424 | tf_op jit(solution)/shard_map/ppermute | solution.py:208
  8.0 4.2 %stage.3 = (bf16[1,7168,256]{2,1,0:T(8,128)(2,1)S(1)}, bf16[1,7168,256]{2,1,0:T(8,128)(2,1)S(1)}, bf16[1,256,7168]{2,1,0:T(8,128)(2,1)S(1)}) custom-call(bf16[1,7168,256]{2,1,0:T(8,128)(2,1)} %refs_0_, bf16[1,7168,256]{2,1,0:T(8,128)(2,1)} %refs_1_, bf16[1,256,7168]{2,1,0:T(8,128)(2,1)} %refs_2_.1), custom_call_target="tpu_custom_call" | custom-call | bytes 11010048 | tf_op jit(solution)/shard_map/stage/pallas_call | solution.py:138
  12.2 1.6 %collective-permute-start.3 = (bf16[16,7296]{1,0:T(8,128)(2,1)S(1)}, bf16[16,7296]{1,0:T(8,128)(2,1)S(1)}, u32[]{:S(2)}, u32[]{:S(2)}) collective-permute-start(bf16[16,7296]{1,0:T(8,128)(2,1)S(1)} %pack.1.refs_0_), channel_id=1, source_target_pairs={{0,1},{1,0},{2,3},{3,2},{4,5},{5,4},{6,7},{7,6},{8,9},{9,8},{10,11... | collective-permute-start | bytes 700424 | tf_op jit(solution)/shard_map/ppermute | solution.py:208
  13.8 5.3 %collective-permute-done.1.refs_4_ = bf16[16,7296]{1,0:T(8,128)(2,1)S(1)} collective-permute-done((bf16[16,7296]{1,0:T(8,128)(2,1)S(1)}, bf16[16,7296]{1,0:T(8,128)(2,1)S(1)}, u32[]{:S(2)}, u32[]{:S(2)}) %collective-permute-start.1) | collective-permute-done | bytes 233504 | tf_op jit(solution)/shard_map/ppermute | solution.py:208
  19.7 1.5 %collective-permute-start.7 = (bf16[16,7296]{1,0:T(8,128)(2,1)S(1)}, bf16[16,7296]{1,0:T(8,128)(2,1)S(1)}, u32[]{:S(2)}, u32[]{:S(2)}) collective-permute-start(bf16[16,7296]{1,0:T(8,128)(2,1)S(1)} %collective-permute-done.1.refs_4_), channel_id=1, source_target_pairs={{0,1},{1,0},{2,3},{3,2},{4,5},{5,4},{6,7},{7,6},{8,9},{9,8},{10,11... | collective-permute-start | bytes 700424 | tf_op jit(solution)/shard_map/ppermute | solution.py:208
  21.2 1.8 %copy-done.3 = bf16[1,7168,256]{2,1,0:T(8,128)(2,1)} copy-done((bf16[1,7168,256]{2,1,0:T(8,128)(2,1)}, bf16[1,7168,256]{2,1,0:T(8,128)(2,1)S(1)}, u32[]{:S(2)}) %copy-start.3) | copy-done | bytes 3670040
  23.0 3.2 %stage.4 = (bf16[1,7168,256]{2,1,0:T(8,128)(2,1)S(1)}, bf16[1,7168,256]{2,1,0:T(8,128)(2,1)S(1)}) custom-call(bf16[1,7168,256]{2,1,0:T(8,128)(2,1)} %copy-done.2, bf16[1,7168,256]{2,1,0:T(8,128)(2,1)} %copy-done.3), custom_call_target="tpu_custom_call" | custom-call | bytes 7340032 | tf_op jit(solution)/shard_map/stage/pallas_call | solution.py:138
  26.3 1.5 %collective-permute-start.6 = (bf16[16,7296]{1,0:T(8,128)(2,1)S(1)}, bf16[16,7296]{1,0:T(8,128)(2,1)S(1)}, u32[]{:S(2)}, u32[]{:S(2)}) collective-permute-start(bf16[16,7296]{1,0:T(8,128)(2,1)S(1)} %collective-permute-done.3.refs_1_), channel_id=1, source_target_pairs={{0,2},{1,3},{2,0},{3,1},{4,6},{5,7},{6,4},{7,5},{8,10},{9,11},{10,... | collective-permute-start | bytes 700424 | tf_op jit(solution)/shard_map/ppermute | solution.py:208
  28.3 1.8 %copy-done.1 = bf16[1,256,7168]{2,1,0:T(8,128)(2,1)} copy-done((bf16[1,256,7168]{2,1,0:T(8,128)(2,1)}, bf16[1,256,7168]{2,1,0:T(8,128)(2,1)S(1)}, u32[]{:S(2)}) %copy-start.1) | copy-done | bytes 3670040
  30.0 2.0 %stage.5.refs_14_ = bf16[1,256,7168]{2,1,0:T(8,128)(2,1)S(1)} custom-call(bf16[1,256,7168]{2,1,0:T(8,128)(2,1)} %copy-done.1), custom_call_target="tpu_custom_call" | custom-call | bytes 3670016 | tf_op jit(solution)/shard_map/stage/pallas_call | solution.py:138
  32.1 1.1 %collective-permute-done.6.refs_3_ = bf16[16,7296]{1,0:T(8,128)(2,1)S(1)} collective-permute-done((bf16[16,7296]{1,0:T(8,128)(2,1)S(1)}, bf16[16,7296]{1,0:T(8,128)(2,1)S(1)}, u32[]{:S(2)}, u32[]{:S(2)}) %collective-permute-start.6) | collective-permute-done | bytes 233504 | tf_op jit(solution)/shard_map/ppermute | solution.py:208
  33.2 0.9 %collective-permute-done.8.refs_7_ = bf16[16,7296]{1,0:T(8,128)(2,1)S(1)} collective-permute-done((bf16[16,7296]{1,0:T(8,128)(2,1)S(1)}, bf16[16,7296]{1,0:T(8,128)(2,1)S(1)}, u32[]{:S(2)}, u32[]{:S(2)}) %collective-permute-start.8) | collective-permute-done | bytes 233504 | tf_op jit(solution)/shard_map/ppermute | solution.py:208
  34.1 3.5 %experts.1 = (bf16[16,7168]{1,0:T(8,128)(2,1)S(1)}, bf16[16,7168]{1,0:T(8,128)(2,1)S(1)}, bf16[16,7168]{1,0:T(8,128)(2,1)S(1)}, bf16[16,7168]{1,0:T(8,128)(2,1)S...) custom-call(bf16[16,7296]{1,0:T(8,128)(2,1)S(1)} %pack.1.refs_0_, ...), custom_call_target="tpu_custom_call" | custom-call | flops 2818572288 | bytes 22020096 | tf_op jit(solution)/shard_map/experts/pallas_call | solution.py:158
  39.0 1.7 %collective-permute-start.12 = (bf16[16,7168]{1,0:T(8,128)(2,1)S(1)}, bf16[16,7168]{1,0:T(8,128)(2,1)S(1)}, u32[]{:S(2)}, u32[]{:S(2)}) collective-permute-start(bf16[16,7168]{1,0:T(8,128)(2,1)S(1)} %get-tuple-element.67), channel_id=1, source_target_pairs={{0,2},{1,3},{2,0},{3,1},{4,6},{5,7},{6,4},{7,5},{8,10},{9,11},{10,... | collective-permute-start | bytes 688136 | tf_op jit(solution)/shard_map/ppermute | solution.py:208
  40.7 3.0 %collective-permute-done.10 = bf16[16,7168]{1,0:T(8,128)(2,1)S(1)} collective-permute-done((bf16[16,7168]{1,0:T(8,128)(2,1)S(1)}, bf16[16,7168]{1,0:T(8,128)(2,1)S(1)}, u32[]{:S(2)}, u32[]{:S(2)}) %collective-permute-start.10) | collective-permute-done | bytes 229408 | tf_op jit(solution)/shard_map/ppermute | solution.py:208
  44.6 1.5 %collective-permute-start.11 = (bf16[16,7168]{1,0:T(8,128)(2,1)S(1)}, bf16[16,7168]{1,0:T(8,128)(2,1)S(1)}, u32[]{:S(2)}, u32[]{:S(2)}) collective-permute-start(bf16[16,7168]{1,0:T(8,128)(2,1)S(1)} %get-tuple-element.66), channel_id=1, source_target_pairs={{0,1},{1,0},{2,3},{3,2},{4,5},{5,4},{6,7},{7,6},{8,9},{9,8},{10,11... | collective-permute-start | bytes 688136 | tf_op jit(solution)/shard_map/ppermute | solution.py:208
  46.9 3.1 %collective-permute-done.14 = bf16[16,7168]{1,0:T(8,128)(2,1)S(1)} collective-permute-done((bf16[16,7168]{1,0:T(8,128)(2,1)S(1)}, bf16[16,7168]{1,0:T(8,128)(2,1)S(1)}, u32[]{:S(2)}, u32[]{:S(2)}) %collective-permute-start.14) | collective-permute-done | bytes 229408 | tf_op jit(solution)/shard_map/ppermute | solution.py:208
  50.0 1.5 %collective-permute-start.15 = (bf16[16,7168]{1,0:T(8,128)(2,1)S(1)}, bf16[16,7168]{1,0:T(8,128)(2,1)S(1)}, u32[]{:S(2)}, u32[]{:S(2)}) collective-permute-start(bf16[16,7168]{1,0:T(8,128)(2,1)S(1)} %get-tuple-element.74), channel_id=1, source_target_pairs={{0,2},{1,3},{2,0},{3,1},{4,6},{5,7},{6,4},{7,5},{8,10},{9,11},{10,... | collective-permute-start | bytes 688136 | tf_op jit(solution)/shard_map/ppermute | solution.py:208
  51.7 2.0 %collective-permute-start.16 = (bf16[16,7168]{1,0:T(8,128)(2,1)S(1)}, bf16[16,7168]{1,0:T(8,128)(2,1)S(1)}, u32[]{:S(2)}, u32[]{:S(2)}) collective-permute-start(bf16[16,7168]{1,0:T(8,128)(2,1)S(1)} %add_convert_fusion.1), channel_id=1, source_target_pairs={{0,6},{1,7},{2,4},{3,5},{4,2},{5,3},{6,0},{7,1},{8,14},{9,15},{10,... | collective-permute-start | bytes 688136 | tf_op jit(solution)/shard_map/ppermute | solution.py:208
  54.7 3.7 %collective-permute-done.15 = bf16[16,7168]{1,0:T(8,128)(2,1)S(1)} collective-permute-done((bf16[16,7168]{1,0:T(8,128)(2,1)S(1)}, bf16[16,7168]{1,0:T(8,128)(2,1)S(1)}, u32[]{:S(2)}, u32[]{:S(2)}) %collective-permute-start.15) | collective-permute-done | bytes 229408 | tf_op jit(solution)/shard_map/ppermute | solution.py:208
  58.5 1.1 %fusion.2 = bf16[1,128,512]{2,1,0:T(8,128)(2,1)} fusion(bf16[1,1024,576]{1,2,0:T(8,128)(2,1)S(1)} %copy-done.4, bf16[1,128,1024]{2,1,0:T(8,128)(2,1)S(1)} %fusion.7), kind=kOutput, calls=%fused_computation.4 | convolution fusion | flops 134283264 | bytes 1441792 | tf_op jit(solution)/shard_map/rhl,rlk->rhk/dot_general | solution.py:189
  59.6 1.9 %collective-permute-done.16 = bf16[16,7168]{1,0:T(8,128)(2,1)S(1)} collective-permute-done((bf16[16,7168]{1,0:T(8,128)(2,1)S(1)}, bf16[16,7168]{1,0:T(8,128)(2,1)S(1)}, u32[]{:S(2)}, u32[]{:S(2)}) %collective-permute-start.16) | collective-permute-done | bytes 229408 | tf_op jit(solution)/shard_map/ppermute | solution.py:208
  (37 shorter events, 6.8 us)
Async XLA Ops:
  0.6 45.5 %copy-start = (bf16[1,128,576]{1,2,0:T(8,128)(2,1)S(1)}, bf16[1,128,576]{1,2,0:T(8,128)(2,1)}, u32[]{:S(2)}) copy-start(bf16[1,128,576]{1,2,0:T(8,128)(2,1)} %param.15) | copy-start | bytes 442372
  1.8 17.3 %collective-permute-start.2 = (bf16[1,7168,256]{2,1,0:T(8,128)(2,1)}, bf16[1,7168,256]{2,1,0:T(8,128)(2,1)S(1)}, u32[]{:S(2)}, u32[]{:S(2)}) collective-permute-start(bf16[1,7168,256]{2,1,0:T(8,128)(2,1)} %refs_0_), channel_id=1, source_target_pairs={{0,8},{8,0},{1,9},{9,1},{2,10},{10,2},{3,11},{11,3},{4,12},{12,4},... | collective-permute-start | bytes 11010056 | tf_op jit(solution)/shard_map/ppermute | solution.py:211
  2.3 18.9 %collective-permute-start.5 = (bf16[1,7168,256]{2,1,0:T(8,128)(2,1)}, bf16[1,7168,256]{2,1,0:T(8,128)(2,1)S(1)}, u32[]{:S(2)}, u32[]{:S(2)}) collective-permute-start(bf16[1,7168,256]{2,1,0:T(8,128)(2,1)} %refs_1_), channel_id=1, source_target_pairs={{0,8},{8,0},{1,9},{9,1},{2,10},{10,2},{3,11},{11,3},{4,12},{12,4},... | collective-permute-start | bytes 11010056 | tf_op jit(solution)/shard_map/ppermute | solution.py:211
  2.4 25.9 %collective-permute-start.9 = (bf16[1,256,7168]{2,1,0:T(8,128)(2,1)}, bf16[1,256,7168]{2,1,0:T(8,128)(2,1)S(1)}, u32[]{:S(2)}, u32[]{:S(2)}) collective-permute-start(bf16[1,256,7168]{2,1,0:T(8,128)(2,1)} %refs_2_.1), channel_id=1, source_target_pairs={{0,8},{8,0},{1,9},{9,1},{2,10},{10,2},{3,11},{11,3},{4,12},{12,4},... | collective-permute-start | bytes 11010056 | tf_op jit(solution)/shard_map/ppermute | solution.py:211
  2.8 9.4 %collective-permute-start = (bf16[16,7296]{1,0:T(8,128)(2,1)S(1)}, bf16[16,7296]{1,0:T(8,128)(2,1)S(1)}, u32[]{:S(2)}, u32[]{:S(2)}) collective-permute-start(bf16[16,7296]{1,0:T(8,128)(2,1)S(1)} %pack.1.refs_0_), channel_id=1, source_target_pairs={{0,2},{1,3},{2,0},{3,1},{4,6},{5,7},{6,4},{7,5},{8,10},{9,11},{10,... | collective-permute-start | bytes 700424 | tf_op jit(solution)/shard_map/ppermute | solution.py:208
  5.5 13.6 %collective-permute-start.1 = (bf16[16,7296]{1,0:T(8,128)(2,1)S(1)}, bf16[16,7296]{1,0:T(8,128)(2,1)S(1)}, u32[]{:S(2)}, u32[]{:S(2)}) collective-permute-start(bf16[16,7296]{1,0:T(8,128)(2,1)S(1)} %pack.1.refs_0_), channel_id=1, source_target_pairs={{0,6},{1,7},{2,4},{3,5},{4,2},{5,3},{6,0},{7,1},{8,14},{9,15},{10,... | collective-permute-start | bytes 700424 | tf_op jit(solution)/shard_map/ppermute | solution.py:208
  12.2 14.0 %collective-permute-start.3 = (bf16[16,7296]{1,0:T(8,128)(2,1)S(1)}, bf16[16,7296]{1,0:T(8,128)(2,1)S(1)}, u32[]{:S(2)}, u32[]{:S(2)}) collective-permute-start(bf16[16,7296]{1,0:T(8,128)(2,1)S(1)} %pack.1.refs_0_), channel_id=1, source_target_pairs={{0,1},{1,0},{2,3},{3,2},{4,5},{5,4},{6,7},{7,6},{8,9},{9,8},{10,11... | collective-permute-start | bytes 700424 | tf_op jit(solution)/shard_map/ppermute | solution.py:208
  19.1 2.1 %copy-start.2 = (bf16[1,7168,256]{2,1,0:T(8,128)(2,1)}, bf16[1,7168,256]{2,1,0:T(8,128)(2,1)S(1)}, u32[]{:S(2)}) copy-start(bf16[1,7168,256]{2,1,0:T(8,128)(2,1)S(1)} %collective-permute-done.2.refs_0_) | copy-start | bytes 11010052
  19.1 7.2 %collective-permute-start.4 = (bf16[16,7296]{1,0:T(8,128)(2,1)S(1)}, bf16[16,7296]{1,0:T(8,128)(2,1)S(1)}, u32[]{:S(2)}, u32[]{:S(2)}) collective-permute-start(bf16[16,7296]{1,0:T(8,128)(2,1)S(1)} %collective-permute-done.1.refs_4_), channel_id=1, source_target_pairs={{0,2},{1,3},{2,0},{3,1},{4,6},{5,7},{6,4},{7,5},{8,10},{9,11},{10,... | collective-permute-start | bytes 700424 | tf_op jit(solution)/shard_map/ppermute | solution.py:208
  19.7 12.4 %collective-permute-start.7 = (bf16[16,7296]{1,0:T(8,128)(2,1)S(1)}, bf16[16,7296]{1,0:T(8,128)(2,1)S(1)}, u32[]{:S(2)}, u32[]{:S(2)}) collective-permute-start(bf16[16,7296]{1,0:T(8,128)(2,1)S(1)} %collective-permute-done.1.refs_4_), channel_id=1, source_target_pairs={{0,1},{1,0},{2,3},{3,2},{4,5},{5,4},{6,7},{7,6},{8,9},{9,8},{10,11... | collective-permute-start | bytes 700424 | tf_op jit(solution)/shard_map/ppermute | solution.py:208
  21.2 1.8 %copy-start.3 = (bf16[1,7168,256]{2,1,0:T(8,128)(2,1)}, bf16[1,7168,256]{2,1,0:T(8,128)(2,1)S(1)}, u32[]{:S(2)}) copy-start(bf16[1,7168,256]{2,1,0:T(8,128)(2,1)S(1)} %collective-permute-done.5.refs_1_) | copy-start | bytes 11010052
  26.3 6.9 %collective-permute-start.6 = (bf16[16,7296]{1,0:T(8,128)(2,1)S(1)}, bf16[16,7296]{1,0:T(8,128)(2,1)S(1)}, u32[]{:S(2)}, u32[]{:S(2)}) collective-permute-start(bf16[16,7296]{1,0:T(8,128)(2,1)S(1)} %collective-permute-done.3.refs_1_), channel_id=1, source_target_pairs={{0,2},{1,3},{2,0},{3,1},{4,6},{5,7},{6,4},{7,5},{8,10},{9,11},{10,... | collective-permute-start | bytes 700424 | tf_op jit(solution)/shard_map/ppermute | solution.py:208
  27.7 6.4 %collective-permute-start.8 = (bf16[16,7296]{1,0:T(8,128)(2,1)S(1)}, bf16[16,7296]{1,0:T(8,128)(2,1)S(1)}, u32[]{:S(2)}, u32[]{:S(2)}) collective-permute-start(bf16[16,7296]{1,0:T(8,128)(2,1)S(1)} %collective-permute-done.4.refs_6_), channel_id=1, source_target_pairs={{0,1},{1,0},{2,3},{3,2},{4,5},{5,4},{6,7},{7,6},{8,9},{9,8},{10,11... | collective-permute-start | bytes 700424 | tf_op jit(solution)/shard_map/ppermute | solution.py:208
  28.3 1.8 %copy-start.1 = (bf16[1,256,7168]{2,1,0:T(8,128)(2,1)}, bf16[1,256,7168]{2,1,0:T(8,128)(2,1)S(1)}, u32[]{:S(2)}) copy-start(bf16[1,256,7168]{2,1,0:T(8,128)(2,1)S(1)} %collective-permute-done.9.refs_0_) | copy-start | bytes 11010052
  32.1 14.1 %copy-start.4 = (bf16[1,1024,576]{1,2,0:T(8,128)(2,1)S(1)}, bf16[1,1024,576]{1,2,0:T(8,128)(2,1)}, u32[]{:S(2)}) copy-start(bf16[1,1024,576]{1,2,0:T(8,128)(2,1)} %param.16) | copy-start | bytes 3538948
  37.6 6.1 %collective-permute-start.10 = (bf16[16,7168]{1,0:T(8,128)(2,1)S(1)}, bf16[16,7168]{1,0:T(8,128)(2,1)S(1)}, u32[]{:S(2)}, u32[]{:S(2)}) collective-permute-start(bf16[16,7168]{1,0:T(8,128)(2,1)S(1)} %get-tuple-element.65), channel_id=1, source_target_pairs={{0,1},{1,0},{2,3},{3,2},{4,5},{5,4},{6,7},{7,6},{8,9},{9,8},{10,11... | collective-permute-start | bytes 688136 | tf_op jit(solution)/shard_map/ppermute | solution.py:208
  39.0 12.5 %collective-permute-start.12 = (bf16[16,7168]{1,0:T(8,128)(2,1)S(1)}, bf16[16,7168]{1,0:T(8,128)(2,1)S(1)}, u32[]{:S(2)}, u32[]{:S(2)}) collective-permute-start(bf16[16,7168]{1,0:T(8,128)(2,1)S(1)} %get-tuple-element.67), channel_id=1, source_target_pairs={{0,2},{1,3},{2,0},{3,1},{4,6},{5,7},{6,4},{7,5},{8,10},{9,11},{10,... | collective-permute-start | bytes 688136 | tf_op jit(solution)/shard_map/ppermute | solution.py:208
  43.8 6.2 %collective-permute-start.14 = (bf16[16,7168]{1,0:T(8,128)(2,1)S(1)}, bf16[16,7168]{1,0:T(8,128)(2,1)S(1)}, u32[]{:S(2)}, u32[]{:S(2)}) collective-permute-start(bf16[16,7168]{1,0:T(8,128)(2,1)S(1)} %add_convert_fusion.2), channel_id=1, source_target_pairs={{0,2},{1,3},{2,0},{3,1},{4,6},{5,7},{6,4},{7,5},{8,10},{9,11},{10,... | collective-permute-start | bytes 688136 | tf_op jit(solution)/shard_map/ppermute | solution.py:208
  44.6 6.9 %collective-permute-start.11 = (bf16[16,7168]{1,0:T(8,128)(2,1)S(1)}, bf16[16,7168]{1,0:T(8,128)(2,1)S(1)}, u32[]{:S(2)}, u32[]{:S(2)}) collective-permute-start(bf16[16,7168]{1,0:T(8,128)(2,1)S(1)} %get-tuple-element.66), channel_id=1, source_target_pairs={{0,1},{1,0},{2,3},{3,2},{4,5},{5,4},{6,7},{7,6},{8,9},{9,8},{10,11... | collective-permute-start | bytes 688136 | tf_op jit(solution)/shard_map/ppermute | solution.py:208
  50.0 8.5 %collective-permute-start.15 = (bf16[16,7168]{1,0:T(8,128)(2,1)S(1)}, bf16[16,7168]{1,0:T(8,128)(2,1)S(1)}, u32[]{:S(2)}, u32[]{:S(2)}) collective-permute-start(bf16[16,7168]{1,0:T(8,128)(2,1)S(1)} %get-tuple-element.74), channel_id=1, source_target_pairs={{0,2},{1,3},{2,0},{3,1},{4,6},{5,7},{6,4},{7,5},{8,10},{9,11},{10,... | collective-permute-start | bytes 688136 | tf_op jit(solution)/shard_map/ppermute | solution.py:208
  51.7 9.9 %collective-permute-start.16 = (bf16[16,7168]{1,0:T(8,128)(2,1)S(1)}, bf16[16,7168]{1,0:T(8,128)(2,1)S(1)}, u32[]{:S(2)}, u32[]{:S(2)}) collective-permute-start(bf16[16,7168]{1,0:T(8,128)(2,1)S(1)} %add_convert_fusion.1), channel_id=1, source_target_pairs={{0,6},{1,7},{2,4},{3,5},{4,2},{5,3},{6,0},{7,1},{8,14},{9,15},{10,... | collective-permute-start | bytes 688136 | tf_op jit(solution)/shard_map/ppermute | solution.py:208
  53.7 7.9 %collective-permute-start.13 = (bf16[16,7168]{1,0:T(8,128)(2,1)S(1)}, bf16[16,7168]{1,0:T(8,128)(2,1)S(1)}, u32[]{:S(2)}, u32[]{:S(2)}) collective-permute-start(bf16[16,7168]{1,0:T(8,128)(2,1)S(1)} %add_convert_fusion.3), channel_id=1, source_target_pairs={{0,1},{1,0},{2,3},{3,2},{4,5},{5,4},{6,7},{7,6},{8,9},{9,8},{10,11... | collective-permute-start | bytes 688136 | tf_op jit(solution)/shard_map/ppermute | solution.py:208

commit v7 on v6

--- a/solution.py
+++ b/solution.py
@@ -217,10 +217,10 @@
     column = jnp.arange(extra, dtype=jnp.int32)
     named = jnp.where(column < 3 * experts_all, column % experts_all, -1)
     masks = (named[None, :] == experts_here[:, None]).astype(jnp.float32)
-    tokens, masks = barrier((tokens, masks))
     packed = pack(tokens, routes, route_weight, experts_all)
 
     w_gate, w_up, packed = barrier((w_gate, w_up, packed))
+    w_down, masks = barrier((w_down, masks))
     gate_there, up_there = swap(w_gate), swap(w_up)
     bits = [1 << i for i in reversed(range(lines.bit_length() - 1))]
     gathered, across = {0: packed}, {}

time: 62.6 us -> 64.7 us (1.034)
  starting transfers between devices: 21 us -> 23.2 us
  waiting for transfers between devices: 19.1 us -> 21.1 us
  local copies, waits for them, and re-layouts: 3.63 us -> 1.8 us
    ppermute x14, starting transfers between devices: 20 us -> 22.1 us  [hop(): return lax.ppermute(value, 'dev', [(d, d ^ offset) for d in range(devs)])]
    ppermute x14, waiting for transfers between devices: 19.1 us -> 21.1 us  [hop(): return lax.ppermute(value, 'dev', [(d, d ^ offset) for d in range(devs)])]
    unnamed x10 -> x6, local copies, waits for them, and re-layouts: 3.63 us -> 1.8 us
  transfers between devices with their start and end apart: 17 -> 17, of which waited for: 8 -> 8; matrix products, arithmetic and copies ran while one was open for 4% -> 3% of each run, Pallas kernels for 15% -> 15%
where the time goes in v7:
time: 64.7 us; the launch traced here: 64.6 us
  starting transfers between devices  23.2 us (36%)
  waiting for transfers between devices  21.1 us (33%)
  Pallas kernels  13.9 us (21%)
  local copies, waits for them, and re-layouts  1.8 us (3%)
  matrix products  1.62 us (3%)
  other arithmetic  1.6 us (2%)
  between operations  1.41 us (2%)
    ppermute x14, starting transfers between devices, hop(): return lax.ppermute(value, 'dev', [(d, d ^ offset) for d in range(devs)])  22.1 us
    ppermute x14, waiting for transfers between devices, hop(): return lax.ppermute(value, 'dev', [(d, d ^ offset) for d in range(devs)])  21.1 us
    pallas_call x3, Pallas kernels, stage(): pl.pallas_call(functools.partial(stage_kernel, count), out_shape=[pltpu.V...  9.45 us
    pallas_call x1, Pallas kernels, run_experts(): pl.pallas_call(functools.partial(expert_kernel, count, steps), out_shape=...  3.44 us
    unnamed x6, local copies, waits for them, and re-layouts  1.8 us
  transfers between devices with their start and end apart: 17, of which 8 were waited for; matrix products, arithmetic and copies ran while one was open for 3% of the time, Pallas kernels for 15%

profile of v7, /device:TPU:0, one launch (start us, length us, event | category | flops | bytes accessed | tf_op | source)
XLA Modules:
  0.0 64.6 jit_solution(12626609323833388235)
XLA Ops:
  0.6 1.0 %pack.1.refs_0_ = bf16[16,7296]{1,0:T(8,128)(2,1)S(1)} custom-call(s32[2,16]{1,0:T(2,128)} %bitcast.26, f32[2,16]{1,0:T(2,128)} %bitcast.27, bf16[16,7168]{1,0:T(8,128)(2,1)} %tokens_hbm.1), custom_call_target="tpu_custom_call" | custom-call | tf_op jit(solution)/shard_map/pack/pallas_call | solution.py:72
  2.8 2.7 %collective-permute-start = (bf16[16,7296]{1,0:T(8,128)(2,1)S(1)}, bf16[16,7296]{1,0:T(8,128)(2,1)S(1)}, u32[]{:S(2)}, u32[]{:S(2)}) collective-permute-start(bf16[16,7296]{1,0:T(8,128)(2,1)S(1)} %pack.1.refs_0_), channel_id=1, source_target_pairs={{0,2},{1,3},{2,0},{3,1},{4,6},{5,7},{6,4},{7,5},{8,10},{9,11},{10,... | collective-permute-start | bytes 700424 | tf_op jit(solution)/shard_map/ppermute | solution.py:208
  5.5 2.5 %collective-permute-start.1 = (bf16[16,7296]{1,0:T(8,128)(2,1)S(1)}, bf16[16,7296]{1,0:T(8,128)(2,1)S(1)}, u32[]{:S(2)}, u32[]{:S(2)}) collective-permute-start(bf16[16,7296]{1,0:T(8,128)(2,1)S(1)} %pack.1.refs_0_), channel_id=1, source_target_pairs={{0,6},{1,7},{2,4},{3,5},{4,2},{5,3},{6,0},{7,1},{8,14},{9,15},{10,... | collective-permute-start | bytes 700424 | tf_op jit(solution)/shard_map/ppermute | solution.py:208
  8.0 4.2 %stage.3 = (bf16[1,7168,256]{2,1,0:T(8,128)(2,1)S(1)}, bf16[1,7168,256]{2,1,0:T(8,128)(2,1)S(1)}, bf16[1,256,7168]{2,1,0:T(8,128)(2,1)S(1)}) custom-call(bf16[1,7168,256]{2,1,0:T(8,128)(2,1)} %refs_0_, bf16[1,7168,256]{2,1,0:T(8,128)(2,1)} %refs_1_, bf16[1,256,7168]{2,1,0:T(8,128)(2,1)} %refs_2_), custom_call_target="tpu_custom_call" | custom-call | bytes 11010048 | tf_op jit(solution)/shard_map/stage/pallas_call | solution.py:138
  12.2 1.6 %collective-permute-start.3 = (bf16[16,7296]{1,0:T(8,128)(2,1)S(1)}, bf16[16,7296]{1,0:T(8,128)(2,1)S(1)}, u32[]{:S(2)}, u32[]{:S(2)}) collective-permute-start(bf16[16,7296]{1,0:T(8,128)(2,1)S(1)} %pack.1.refs_0_), channel_id=1, source_target_pairs={{0,1},{1,0},{2,3},{3,2},{4,5},{5,4},{6,7},{7,6},{8,9},{9,8},{10,11... | collective-permute-start | bytes 700424 | tf_op jit(solution)/shard_map/ppermute | solution.py:208
  13.8 5.3 %collective-permute-done.1.refs_4_ = bf16[16,7296]{1,0:T(8,128)(2,1)S(1)} collective-permute-done((bf16[16,7296]{1,0:T(8,128)(2,1)S(1)}, bf16[16,7296]{1,0:T(8,128)(2,1)S(1)}, u32[]{:S(2)}, u32[]{:S(2)}) %collective-permute-start.1) | collective-permute-done | bytes 233504 | tf_op jit(solution)/shard_map/ppermute | solution.py:208
  19.7 1.5 %collective-permute-start.7 = (bf16[16,7296]{1,0:T(8,128)(2,1)S(1)}, bf16[16,7296]{1,0:T(8,128)(2,1)S(1)}, u32[]{:S(2)}, u32[]{:S(2)}) collective-permute-start(bf16[16,7296]{1,0:T(8,128)(2,1)S(1)} %collective-permute-done.1.refs_4_), channel_id=1, source_target_pairs={{0,1},{1,0},{2,3},{3,2},{4,5},{5,4},{6,7},{7,6},{8,9},{9,8},{10,11... | collective-permute-start | bytes 700424 | tf_op jit(solution)/shard_map/ppermute | solution.py:208
  21.2 3.2 %stage.4 = (bf16[1,7168,256]{2,1,0:T(8,128)(2,1)S(1)}, bf16[1,7168,256]{2,1,0:T(8,128)(2,1)S(1)}) custom-call(bf16[1,7168,256]{2,1,0:T(8,128)(2,1)} %collective-permute-done.2.refs_0_, bf16[1,7168,256]{2,1,0:T(8,128)(2,1)} %collective-permute-done.5.refs_1_), custom_call_target="tpu_custom_call" | custom-call | bytes 7340032 | tf_op jit(solution)/shard_map/stage/pallas_call | solution.py:138
  24.4 1.9 %collective-permute-done.4.refs_6_ = bf16[16,7296]{1,0:T(8,128)(2,1)S(1)} collective-permute-done((bf16[16,7296]{1,0:T(8,128)(2,1)S(1)}, bf16[16,7296]{1,0:T(8,128)(2,1)S(1)}, u32[]{:S(2)}, u32[]{:S(2)}) %collective-permute-start.4) | collective-permute-done | bytes 233504 | tf_op jit(solution)/shard_map/ppermute | solution.py:208
  26.6 1.5 %collective-permute-start.8 = (bf16[16,7296]{1,0:T(8,128)(2,1)S(1)}, bf16[16,7296]{1,0:T(8,128)(2,1)S(1)}, u32[]{:S(2)}, u32[]{:S(2)}) collective-permute-start(bf16[16,7296]{1,0:T(8,128)(2,1)S(1)} %collective-permute-done.4.refs_6_), channel_id=1, source_target_pairs={{0,1},{1,0},{2,3},{3,2},{4,5},{5,4},{6,7},{7,6},{8,9},{9,8},{10,11... | collective-permute-start | bytes 700424 | tf_op jit(solution)/shard_map/ppermute | solution.py:208
  28.1 1.8 %copy-done.1 = bf16[1,256,7168]{2,1,0:T(8,128)(2,1)} copy-done((bf16[1,256,7168]{2,1,0:T(8,128)(2,1)}, bf16[1,256,7168]{2,1,0:T(8,128)(2,1)S(1)}, u32[]{:S(2)}) %copy-start.1) | copy-done | bytes 3670040
  29.9 2.0 %stage.5.refs_14_ = bf16[1,256,7168]{2,1,0:T(8,128)(2,1)S(1)} custom-call(bf16[1,256,7168]{2,1,0:T(8,128)(2,1)} %copy-done.1), custom_call_target="tpu_custom_call" | custom-call | bytes 3670016 | tf_op jit(solution)/shard_map/stage/pallas_call | solution.py:138
  32.7 3.4 %experts.1 = (bf16[16,7168]{1,0:T(8,128)(2,1)S(1)}, bf16[16,7168]{1,0:T(8,128)(2,1)S(1)}, bf16[16,7168]{1,0:T(8,128)(2,1)S(1)}, bf16[16,7168]{1,0:T(8,128)(2,1)S...) custom-call(bf16[16,7296]{1,0:T(8,128)(2,1)S(1)} %pack.1.refs_0_, ...), custom_call_target="tpu_custom_call" | custom-call | flops 2818572288 | bytes 22020096 | tf_op jit(solution)/shard_map/experts/pallas_call | solution.py:158
  36.2 1.6 %collective-permute-start.10 = (bf16[16,7168]{1,0:T(8,128)(2,1)S(1)}, bf16[16,7168]{1,0:T(8,128)(2,1)S(1)}, u32[]{:S(2)}, u32[]{:S(2)}) collective-permute-start(bf16[16,7168]{1,0:T(8,128)(2,1)S(1)} %get-tuple-element.65), channel_id=1, source_target_pairs={{0,1},{1,0},{2,3},{3,2},{4,5},{5,4},{6,7},{7,6},{8,9},{9,8},{10,11... | collective-permute-start | bytes 688136 | tf_op jit(solution)/shard_map/ppermute | solution.py:208
  38.4 1.7 %collective-permute-start.12 = (bf16[16,7168]{1,0:T(8,128)(2,1)S(1)}, bf16[16,7168]{1,0:T(8,128)(2,1)S(1)}, u32[]{:S(2)}, u32[]{:S(2)}) collective-permute-start(bf16[16,7168]{1,0:T(8,128)(2,1)S(1)} %get-tuple-element.67), channel_id=1, source_target_pairs={{0,2},{1,3},{2,0},{3,1},{4,6},{5,7},{6,4},{7,5},{8,10},{9,11},{10,... | collective-permute-start | bytes 688136 | tf_op jit(solution)/shard_map/ppermute | solution.py:208
  40.1 2.1 %collective-permute-done.10 = bf16[16,7168]{1,0:T(8,128)(2,1)S(1)} collective-permute-done((bf16[16,7168]{1,0:T(8,128)(2,1)S(1)}, bf16[16,7168]{1,0:T(8,128)(2,1)S(1)}, u32[]{:S(2)}, u32[]{:S(2)}) %collective-permute-start.10) | collective-permute-done | bytes 229408 | tf_op jit(solution)/shard_map/ppermute | solution.py:208
  42.3 2.4 %collective-permute-start.14 = (bf16[16,7168]{1,0:T(8,128)(2,1)S(1)}, bf16[16,7168]{1,0:T(8,128)(2,1)S(1)}, u32[]{:S(2)}, u32[]{:S(2)}) collective-permute-start(bf16[16,7168]{1,0:T(8,128)(2,1)S(1)} %add_convert_fusion.2), channel_id=1, source_target_pairs={{0,2},{1,3},{2,0},{3,1},{4,6},{5,7},{6,4},{7,5},{8,10},{9,11},{10,... | collective-permute-start | bytes 688136 | tf_op jit(solution)/shard_map/ppermute | solution.py:208
  44.7 1.5 %collective-permute-start.11 = (bf16[16,7168]{1,0:T(8,128)(2,1)S(1)}, bf16[16,7168]{1,0:T(8,128)(2,1)S(1)}, u32[]{:S(2)}, u32[]{:S(2)}) collective-permute-start(bf16[16,7168]{1,0:T(8,128)(2,1)S(1)} %get-tuple-element.66), channel_id=1, source_target_pairs={{0,1},{1,0},{2,3},{3,2},{4,5},{5,4},{6,7},{7,6},{8,9},{9,8},{10,11... | collective-permute-start | bytes 688136 | tf_op jit(solution)/shard_map/ppermute | solution.py:208
  46.9 1.9 %collective-permute-done.14 = bf16[16,7168]{1,0:T(8,128)(2,1)S(1)} collective-permute-done((bf16[16,7168]{1,0:T(8,128)(2,1)S(1)}, bf16[16,7168]{1,0:T(8,128)(2,1)S(1)}, u32[]{:S(2)}, u32[]{:S(2)}) %collective-permute-start.14) | collective-permute-done | bytes 229408 | tf_op jit(solution)/shard_map/ppermute | solution.py:208
  48.8 1.9 %collective-permute-done.11 = bf16[16,7168]{1,0:T(8,128)(2,1)S(1)} collective-permute-done((bf16[16,7168]{1,0:T(8,128)(2,1)S(1)}, bf16[16,7168]{1,0:T(8,128)(2,1)S(1)}, u32[]{:S(2)}, u32[]{:S(2)}) %collective-permute-start.11) | collective-permute-done | bytes 229408 | tf_op jit(solution)/shard_map/ppermute | solution.py:208
  50.9 2.5 %collective-permute-start.16 = (bf16[16,7168]{1,0:T(8,128)(2,1)S(1)}, bf16[16,7168]{1,0:T(8,128)(2,1)S(1)}, u32[]{:S(2)}, u32[]{:S(2)}) collective-permute-start(bf16[16,7168]{1,0:T(8,128)(2,1)S(1)} %add_convert_fusion.1), channel_id=1, source_target_pairs={{0,6},{1,7},{2,4},{3,5},{4,2},{5,3},{6,0},{7,1},{8,14},{9,15},{10,... | collective-permute-start | bytes 688136 | tf_op jit(solution)/shard_map/ppermute | solution.py:208
  53.7 1.5 %collective-permute-start.13 = (bf16[16,7168]{1,0:T(8,128)(2,1)S(1)}, bf16[16,7168]{1,0:T(8,128)(2,1)S(1)}, u32[]{:S(2)}, u32[]{:S(2)}) collective-permute-start(bf16[16,7168]{1,0:T(8,128)(2,1)S(1)} %add_convert_fusion.3), channel_id=1, source_target_pairs={{0,1},{1,0},{2,3},{3,2},{4,5},{5,4},{6,7},{7,6},{8,9},{9,8},{10,11... | collective-permute-start | bytes 688136 | tf_op jit(solution)/shard_map/ppermute | solution.py:208
  55.4 7.2 %collective-permute-done.15 = bf16[16,7168]{1,0:T(8,128)(2,1)S(1)} collective-permute-done((bf16[16,7168]{1,0:T(8,128)(2,1)S(1)}, bf16[16,7168]{1,0:T(8,128)(2,1)S(1)}, u32[]{:S(2)}, u32[]{:S(2)}) %collective-permute-start.15) | collective-permute-done | bytes 229408 | tf_op jit(solution)/shard_map/ppermute | solution.py:208
  62.6 1.1 %fusion.2 = bf16[1,128,512]{2,1,0:T(8,128)(2,1)} fusion(bf16[1,1024,576]{1,2,0:T(8,128)(2,1)S(1)} %copy-done.2, bf16[1,128,1024]{2,1,0:T(8,128)(2,1)S(1)} %fusion.7), kind=kOutput, calls=%fused_computation.4 | convolution fusion | flops 134283264 | bytes 1441792 | tf_op jit(solution)/shard_map/rhl,rlk->rhk/dot_general | solution.py:189
  (33 shorter events, 5.1 us)
Async XLA Ops:
  0.6 45.6 %copy-start = (bf16[1,128,576]{1,2,0:T(8,128)(2,1)S(1)}, bf16[1,128,576]{1,2,0:T(8,128)(2,1)}, u32[]{:S(2)}) copy-start(bf16[1,128,576]{1,2,0:T(8,128)(2,1)} %param.15) | copy-start | bytes 442372
  1.7 17.4 %collective-permute-start.2 = (bf16[1,7168,256]{2,1,0:T(8,128)(2,1)}, bf16[1,7168,256]{2,1,0:T(8,128)(2,1)}, u32[]{:S(2)}, u32[]{:S(2)}) collective-permute-start(bf16[1,7168,256]{2,1,0:T(8,128)(2,1)} %refs_0_), channel_id=1, source_target_pairs={{0,8},{8,0},{1,9},{9,1},{2,10},{10,2},{3,11},{11,3},{4,12},{12,4},... | collective-permute-start | bytes 11010056 | tf_op jit(solution)/shard_map/ppermute | solution.py:211
  2.2 19.0 %collective-permute-start.5 = (bf16[1,7168,256]{2,1,0:T(8,128)(2,1)}, bf16[1,7168,256]{2,1,0:T(8,128)(2,1)}, u32[]{:S(2)}, u32[]{:S(2)}) collective-permute-start(bf16[1,7168,256]{2,1,0:T(8,128)(2,1)} %refs_1_), channel_id=1, source_target_pairs={{0,8},{8,0},{1,9},{9,1},{2,10},{10,2},{3,11},{11,3},{4,12},{12,4},... | collective-permute-start | bytes 11010056 | tf_op jit(solution)/shard_map/ppermute | solution.py:211
  2.4 25.7 %collective-permute-start.9 = (bf16[1,256,7168]{2,1,0:T(8,128)(2,1)}, bf16[1,256,7168]{2,1,0:T(8,128)(2,1)S(1)}, u32[]{:S(2)}, u32[]{:S(2)}) collective-permute-start(bf16[1,256,7168]{2,1,0:T(8,128)(2,1)} %refs_2_), channel_id=1, source_target_pairs={{0,8},{8,0},{1,9},{9,1},{2,10},{10,2},{3,11},{11,3},{4,12},{12,4},... | collective-permute-start | bytes 11010056 | tf_op jit(solution)/shard_map/ppermute | solution.py:211
  2.8 9.4 %collective-permute-start = (bf16[16,7296]{1,0:T(8,128)(2,1)S(1)}, bf16[16,7296]{1,0:T(8,128)(2,1)S(1)}, u32[]{:S(2)}, u32[]{:S(2)}) collective-permute-start(bf16[16,7296]{1,0:T(8,128)(2,1)S(1)} %pack.1.refs_0_), channel_id=1, source_target_pairs={{0,2},{1,3},{2,0},{3,1},{4,6},{5,7},{6,4},{7,5},{8,10},{9,11},{10,... | collective-permute-start | bytes 700424 | tf_op jit(solution)/shard_map/ppermute | solution.py:208
  5.5 13.6 %collective-permute-start.1 = (bf16[16,7296]{1,0:T(8,128)(2,1)S(1)}, bf16[16,7296]{1,0:T(8,128)(2,1)S(1)}, u32[]{:S(2)}, u32[]{:S(2)}) collective-permute-start(bf16[16,7296]{1,0:T(8,128)(2,1)S(1)} %pack.1.refs_0_), channel_id=1, source_target_pairs={{0,6},{1,7},{2,4},{3,5},{4,2},{5,3},{6,0},{7,1},{8,14},{9,15},{10,... | collective-permute-start | bytes 700424 | tf_op jit(solution)/shard_map/ppermute | solution.py:208
  12.2 12.2 %collective-permute-start.3 = (bf16[16,7296]{1,0:T(8,128)(2,1)S(1)}, bf16[16,7296]{1,0:T(8,128)(2,1)S(1)}, u32[]{:S(2)}, u32[]{:S(2)}) collective-permute-start(bf16[16,7296]{1,0:T(8,128)(2,1)S(1)} %pack.1.refs_0_), channel_id=1, source_target_pairs={{0,1},{1,0},{2,3},{3,2},{4,5},{5,4},{6,7},{7,6},{8,9},{9,8},{10,11... | collective-permute-start | bytes 700424 | tf_op jit(solution)/shard_map/ppermute | solution.py:208
  19.1 7.2 %collective-permute-start.4 = (bf16[16,7296]{1,0:T(8,128)(2,1)S(1)}, bf16[16,7296]{1,0:T(8,128)(2,1)S(1)}, u32[]{:S(2)}, u32[]{:S(2)}) collective-permute-start(bf16[16,7296]{1,0:T(8,128)(2,1)S(1)} %collective-permute-done.1.refs_4_), channel_id=1, source_target_pairs={{0,2},{1,3},{2,0},{3,1},{4,6},{5,7},{6,4},{7,5},{8,10},{9,11},{10,... | collective-permute-start | bytes 700424 | tf_op jit(solution)/shard_map/ppermute | solution.py:208
  19.7 12.3 %collective-permute-start.7 = (bf16[16,7296]{1,0:T(8,128)(2,1)S(1)}, bf16[16,7296]{1,0:T(8,128)(2,1)S(1)}, u32[]{:S(2)}, u32[]{:S(2)}) collective-permute-start(bf16[16,7296]{1,0:T(8,128)(2,1)S(1)} %collective-permute-done.1.refs_4_), channel_id=1, source_target_pairs={{0,1},{1,0},{2,3},{3,2},{4,5},{5,4},{6,7},{7,6},{8,9},{9,8},{10,11... | collective-permute-start | bytes 700424 | tf_op jit(solution)/shard_map/ppermute | solution.py:208
  26.3 6.3 %collective-permute-start.6 = (bf16[16,7296]{1,0:T(8,128)(2,1)S(1)}, bf16[16,7296]{1,0:T(8,128)(2,1)S(1)}, u32[]{:S(2)}, u32[]{:S(2)}) collective-permute-start(bf16[16,7296]{1,0:T(8,128)(2,1)S(1)} %collective-permute-done.3.refs_1_), channel_id=1, source_target_pairs={{0,2},{1,3},{2,0},{3,1},{4,6},{5,7},{6,4},{7,5},{8,10},{9,11},{10,... | collective-permute-start | bytes 700424 | tf_op jit(solution)/shard_map/ppermute | solution.py:208
  26.6 6.1 %collective-permute-start.8 = (bf16[16,7296]{1,0:T(8,128)(2,1)S(1)}, bf16[16,7296]{1,0:T(8,128)(2,1)S(1)}, u32[]{:S(2)}, u32[]{:S(2)}) collective-permute-start(bf16[16,7296]{1,0:T(8,128)(2,1)S(1)} %collective-permute-done.4.refs_6_), channel_id=1, source_target_pairs={{0,1},{1,0},{2,3},{3,2},{4,5},{5,4},{6,7},{7,6},{8,9},{9,8},{10,11... | collective-permute-start | bytes 700424 | tf_op jit(solution)/shard_map/ppermute | solution.py:208
  28.1 1.8 %copy-start.1 = (bf16[1,256,7168]{2,1,0:T(8,128)(2,1)}, bf16[1,256,7168]{2,1,0:T(8,128)(2,1)S(1)}, u32[]{:S(2)}) copy-start(bf16[1,256,7168]{2,1,0:T(8,128)(2,1)S(1)} %collective-permute-done.9.refs_0_) | copy-start | bytes 11010052
  31.9 14.3 %copy-start.2 = (bf16[1,1024,576]{1,2,0:T(8,128)(2,1)S(1)}, bf16[1,1024,576]{1,2,0:T(8,128)(2,1)}, u32[]{:S(2)}) copy-start(bf16[1,1024,576]{1,2,0:T(8,128)(2,1)} %param.16) | copy-start | bytes 3538948
  36.2 6.1 %collective-permute-start.10 = (bf16[16,7168]{1,0:T(8,128)(2,1)S(1)}, bf16[16,7168]{1,0:T(8,128)(2,1)S(1)}, u32[]{:S(2)}, u32[]{:S(2)}) collective-permute-start(bf16[16,7168]{1,0:T(8,128)(2,1)S(1)} %get-tuple-element.65), channel_id=1, source_target_pairs={{0,1},{1,0},{2,3},{3,2},{4,5},{5,4},{6,7},{7,6},{8,9},{9,8},{10,11... | collective-permute-start | bytes 688136 | tf_op jit(solution)/shard_map/ppermute | solution.py:208
  38.4 10.4 %collective-permute-start.12 = (bf16[16,7168]{1,0:T(8,128)(2,1)S(1)}, bf16[16,7168]{1,0:T(8,128)(2,1)S(1)}, u32[]{:S(2)}, u32[]{:S(2)}) collective-permute-start(bf16[16,7168]{1,0:T(8,128)(2,1)S(1)} %get-tuple-element.67), channel_id=1, source_target_pairs={{0,2},{1,3},{2,0},{3,1},{4,6},{5,7},{6,4},{7,5},{8,10},{9,11},{10,... | collective-permute-start | bytes 688136 | tf_op jit(solution)/shard_map/ppermute | solution.py:208
  42.3 6.5 %collective-permute-start.14 = (bf16[16,7168]{1,0:T(8,128)(2,1)S(1)}, bf16[16,7168]{1,0:T(8,128)(2,1)S(1)}, u32[]{:S(2)}, u32[]{:S(2)}) collective-permute-start(bf16[16,7168]{1,0:T(8,128)(2,1)S(1)} %add_convert_fusion.2), channel_id=1, source_target_pairs={{0,2},{1,3},{2,0},{3,1},{4,6},{5,7},{6,4},{7,5},{8,10},{9,11},{10,... | collective-permute-start | bytes 688136 | tf_op jit(solution)/shard_map/ppermute | solution.py:208
  44.7 6.0 %collective-permute-start.11 = (bf16[16,7168]{1,0:T(8,128)(2,1)S(1)}, bf16[16,7168]{1,0:T(8,128)(2,1)S(1)}, u32[]{:S(2)}, u32[]{:S(2)}) collective-permute-start(bf16[16,7168]{1,0:T(8,128)(2,1)S(1)} %get-tuple-element.66), channel_id=1, source_target_pairs={{0,1},{1,0},{2,3},{3,2},{4,5},{5,4},{6,7},{7,6},{8,9},{9,8},{10,11... | collective-permute-start | bytes 688136 | tf_op jit(solution)/shard_map/ppermute | solution.py:208
  50.9 12.9 %collective-permute-start.16 = (bf16[16,7168]{1,0:T(8,128)(2,1)S(1)}, bf16[16,7168]{1,0:T(8,128)(2,1)S(1)}, u32[]{:S(2)}, u32[]{:S(2)}) collective-permute-start(bf16[16,7168]{1,0:T(8,128)(2,1)S(1)} %add_convert_fusion.1), channel_id=1, source_target_pairs={{0,6},{1,7},{2,4},{3,5},{4,2},{5,3},{6,0},{7,1},{8,14},{9,15},{10,... | collective-permute-start | bytes 688136 | tf_op jit(solution)/shard_map/ppermute | solution.py:208
  53.4 9.2 %collective-permute-start.15 = (bf16[16,7168]{1,0:T(8,128)(2,1)S(1)}, bf16[16,7168]{1,0:T(8,128)(2,1)S(1)}, u32[]{:S(2)}, u32[]{:S(2)}) collective-permute-start(bf16[16,7168]{1,0:T(8,128)(2,1)S(1)} %get-tuple-element.74), channel_id=1, source_target_pairs={{0,2},{1,3},{2,0},{3,1},{4,6},{5,7},{6,4},{7,5},{8,10},{9,11},{10,... | collective-permute-start | bytes 688136 | tf_op jit(solution)/shard_map/ppermute | solution.py:208
  53.7 10.1 %collective-permute-start.13 = (bf16[16,7168]{1,0:T(8,128)(2,1)S(1)}, bf16[16,7168]{1,0:T(8,128)(2,1)S(1)}, u32[]{:S(2)}, u32[]{:S(2)}) collective-permute-start(bf16[16,7168]{1,0:T(8,128)(2,1)S(1)} %add_convert_fusion.3), channel_id=1, source_target_pairs={{0,1},{1,0},{2,3},{3,2},{4,5},{5,4},{6,7},{7,6},{8,9},{9,8},{10,11... | collective-permute-start | bytes 688136 | tf_op jit(solution)/shard_map/ppermute | solution.py:208
